TPU v7x, 32 devices: a whole 2x2x4 slice. The times are simulated.
32 devices in a mesh: frag: 8 (over z, y), tile: 4 (over x, core).
Axes of the slice: x: 2, y: 2, z: 4, core: 2. Of those that a mesh axis runs over, the one named last changes fastest.
Arguments:
- core_fock: float32 [64, 256, 256], P('frag', 'tile'), as said below
- intersection: float32 [64, 256, 256], P('frag', 'tile'), as said below
- gamma_tile: float32 [64, 256, 256], P('frag', 'tile'), may hold values from -0.375 to 0.375
- charge_old: float32 [64, 256], P('frag'), may hold values from -6 to 6
- embed_old: float32 [64, 256], P('frag'), may hold values from -4 to 4
- core_pop: float32 [64, 256], P('frag'), may hold values from 0 to 1
- centres: float32 [64, 3, 256], P('frag'), may hold values from -10 to 10
- frag_sizes: int32 [64], P('frag'), may hold values from 20 to 256, as said below
- near_list: int32 [64, 8], P('frag'), may hold values from 0 to 63, as said below
- far_list: int32 [64, 8], P('frag'), may hold values from 0 to 63
Outputs:
- density: float32 [64, 256, 256], P('frag', 'tile')
- esp_matrix: float32 [64, 256, 256], P('frag', 'tile')
Inputs may be any that keep to these rules, and one draw needn't show every extreme that they name: `frag_sizes`: each fragment uses at least 20 basis functions; some fragment uses exactly 256. near_list[f, k] is a fragment whose index differs from f by 1 to 8; the distance 8 occurs. `core_fock`: symmetric in its last two dimensions. `intersection`: symmetric in its last two dimensions.
All inputs are finite; a program needn't handle non-finite values.
Results may differ from a plain program's by a relative error of at most 0.0003.
Values sent between devices are 32-bit elements; how exact they have to be, the bound alone decides.
No kernel may reach another device: no remote copies, remote signals or barrier semaphores. Data moves between devices by JAX's collectives and lax.ppermute only.
A program may use at most 64 MiB of HBM per device.

v0:
```python
import jax
import jax.numpy as jnp
from jax import lax
from jax.sharding import PartitionSpec as P

PC = 8
ITERS = 12


precise = lax.Precision.HIGHEST
screening = 0.25


def extended(x, sides, width):
    for axis, dim in sides:
        peers, length = (lax.axis_size(axis), x.shape[dim])
        up = [(i, (i + 1) % peers) for i in range(peers - 1)]
        down = [(j, i) for i, j in up]
        last = lax.slice_in_dim(x, length - width, length, axis=dim)
        leading = lax.slice_in_dim(x, 0, width, axis=dim)
        before = lax.ppermute(last, axis, up)
        after = lax.ppermute(leading, axis, down)
        x = jnp.concatenate([before, x, after], axis=dim)
    return x


def coulomb(centre_set, source):
    dist_sq = (centre_set[0][:, None] - source[1][None, :]) ** 2
    dist_sq = dist_sq + (centre_set[1][:, None] - source[2][None, :]) ** 2
    dist_sq = dist_sq + (centre_set[2][:, None] - source[3][None, :]) ** 2
    return jnp.sum(source[0][None, :] * lax.rsqrt(dist_sq + 1.0), axis=1)


def point_blocks(charges, centres):
    frag_count = charges.shape[0]
    group = charges.shape[1] // PC
    block_charge = jnp.sum(charges.reshape(frag_count, PC, group), axis=2)
    block_place = jnp.mean(centres.reshape(frag_count, 3, PC, group), axis=3)
    return jnp.concatenate([block_charge[:, None, :], block_place], axis=1)


def potentials(centres, near_rows, far_rows, table, blocks):
    basis_count = centres.shape[2]

    def potential_of(inputs):
        centre_set, near_ids, far_ids = inputs

        def add_near(summed, neighbour):
            return (summed + coulomb(centre_set, table[neighbour]), None)

        summed, unused = lax.scan(add_near, jnp.zeros((basis_count,), jnp.float32), near_ids)
        far_source = jnp.transpose(blocks[far_ids], (1, 0, 2)).reshape(4, -1)
        return screening * (summed + coulomb(centre_set, far_source))

    return lax.map(potential_of, (centres, near_rows, far_rows))


def cube_step(sign_est, full_rows):
    squared = jnp.einsum("fij,fjk->fik", sign_est, full_rows, precision=precise)
    return 1.5 * sign_est - 0.5 * jnp.einsum("fij,fjk->fik", squared, full_rows, precision=precise)


def whole_density(fock_matrix, sizes_share, column_index):
    basis_count = fock_matrix.shape[2]
    active = (column_index[None, :] < sizes_share[:, None]).astype(jnp.float32)
    masked = fock_matrix * active[:, :, None] * active[:, None, :]
    frob_norm = jnp.sqrt(jnp.sum(masked * masked, axis=(1, 2)) + 1e-06)
    identity = jnp.eye(basis_count, dtype=jnp.float32)
    start_est = masked / frob_norm[:, None, None] + identity[None] * (1.0 - active)[:, :, None]

    def sweep(sweep_index, sign_est):
        return cube_step(sign_est, sign_est)

    sign_est = lax.fori_loop(0, ITERS, sweep, start_est)
    return 0.5 * (identity[None] - sign_est)


def per_device(
    core_fock,
    intersection,
    gamma_tile,
    charge_old,
    embed_old,
    core_pop,
    centres,
    frag_sizes,
    near_list,
    far_list,
):
    frag_dev = core_fock.shape[0]
    basis_count = core_fock.shape[2]
    tile_count = lax.axis_size("tile")
    tile_at = lax.axis_index("tile")
    frag_at = lax.axis_index("frag")
    column_index = jnp.arange(basis_count, dtype=jnp.int32)
    share_count = frag_dev // tile_count
    share_first = tile_at * share_count

    def select_share(array):
        return lax.dynamic_slice_in_dim(array, share_first, share_count, 0)

    stacked = jnp.stack([core_fock, intersection, gamma_tile], axis=1)
    whole_tiles = lax.all_to_all(stacked, "tile", split_axis=0, concat_axis=2, tiled=True)
    core_whole = whole_tiles[:, 0]
    over_whole = whole_tiles[:, 1]
    gamma_whole = whole_tiles[:, 2]
    field = jnp.einsum(
        "fij,fj->fi", gamma_whole, select_share(charge_old), precision=precise
    ) + select_share(embed_old)
    fock_matrix = core_whole + 0.5 * over_whole * (field[:, :, None] + field[:, None, :])
    density_whole = whole_density(fock_matrix, select_share(frag_sizes), column_index)
    charge_share = jnp.sum(density_whole * over_whole, axis=2) - select_share(core_pop)
    charges = lax.all_gather(charge_share, "tile", axis=0, tiled=True)
    table_own = jnp.concatenate([charges[:, None, :], centres], axis=1)
    blocks_own = point_blocks(charges, centres)
    far_table = lax.all_gather(blocks_own, "frag", axis=0, tiled=True)
    near_table = extended(table_own, (("frag", 0),), frag_dev)
    near_rows = near_list - (frag_at * frag_dev - frag_dev)
    potential = potentials(
        select_share(centres),
        select_share(near_rows),
        select_share(far_list),
        near_table,
        far_table,
    )
    esp_whole = 0.5 * over_whole * (potential[:, :, None] + potential[:, None, :])
    density, esp_matrix = (
        lax.all_to_all(density_whole, "tile", split_axis=1, concat_axis=0, tiled=True),
        lax.all_to_all(esp_whole, "tile", split_axis=1, concat_axis=0, tiled=True),
    )
    return (density, esp_matrix)


def solution(mesh):
    in_specs = (
        P("frag", "tile", None),
        P("frag", "tile", None),
        P("frag", "tile", None),
        P("frag", None),
        P("frag", None),
        P("frag", None),
        P("frag", None, None),
        P("frag"),
        P("frag", None),
        P("frag", None),
    )
    out_specs = (P("frag", "tile", None), P("frag", "tile", None))
    return jax.shard_map(
        per_device, mesh=mesh, in_specs=in_specs, out_specs=out_specs, check_vma=False
    )
```

profile of v0, /device:TPU:0, one launch (start us, length us, event | category | flops | bytes accessed | tf_op | source)
XLA Modules:
  0.0 159.9 jit_solution(15563875190940251396)
XLA Ops:
  0.6 2.7 %pad_maximum_fusion = f32[8,3,64,256]{3,2,1,0:T(8,128)} fusion(f32[8,1,64,256]{3,2,1,0:T(8,128)} %bitcast.134, f32[8,1,64,256]{3,2,1,0:T(8,128)} %bitcast.135, f32[8,1,64,256]{3,2,1,0:T(8,128)} %bitcast.136), kind=kLoop, calls=%fused_computation.26 | loop fusion | flops 786432 | bytes 3145728 | tf_op jit(solution)/shard_map/stack | solution.py:102
  3.3 4.3 %all-to-all-start = ((f32[8,3,64,256]{3,2,1,0:T(8,128)}), f32[8,3,64,256]{3,2,1,0:T(8,128)S(1)}, u32[]{:S(2)}, u32[]{:S(2)}) async-start(f32[8,3,64,256]{3,2,1,0:T(8,128)} %pad_maximum_fusion), calls=%async_computation | async-start | bytes 3145728 | tf_op jit(solution)/shard_map/all_to_all | solution.py:103
  8.0 0.8 copy.70
  9.7 1.3 constant_dynamic-slice_fusion.9
  11.0 0.6 broadcast_multiply_fusion
  11.6 16.2 %all-to-all-done = f32[8,3,64,256]{3,2,1,0:T(8,128)S(1)} async-done(((f32[8,3,64,256]{3,2,1,0:T(8,128)}), f32[8,3,64,256]{3,2,1,0:T(8,128)S(1)}, u32[]{:S(2)}, u32[]{:S(2)}) %all-to-all-start) | async-done | bytes 1572896 | tf_op jit(solution)/shard_map/all_to_all | solution.py:103
  27.8 1.2 copy.68
  29.8 0.7 bitcast_add_fusion
  30.6 1.1 multiply_reduce_fusion.3
  32.2 17.1 %while.31 = (s32[]{:T(128)}, f32[2,256,256]{2,1,0:T(8,128)S(1)}, s32[]{:T(128)}) while((s32[]{:T(128)}, f32[2,256,256]{2,1,0:T(8,128)S(1)}, s32[]{:T(128)}) %tuple.84), condition=%wide.region_2.0_spmd, body=%wide.region_1.0_spmd.sunk | while | flops 805699584 | bytes 3670061 | solution.py:74
  32.3 0.7 fusion.34
  32.9 0.7 fusion.35
  33.7 0.7 fusion.34
  34.4 0.7 fusion.35
  35.1 0.7 fusion.34
  35.8 0.7 fusion.35
  36.5 0.7 fusion.34
  37.2 0.7 fusion.35
  38.0 0.7 fusion.34
  38.6 0.7 fusion.35
  39.4 0.7 fusion.34
  40.1 0.7 fusion.35
  40.8 0.7 fusion.34
  41.5 0.7 fusion.35
  42.3 0.7 fusion.34
  42.9 0.7 fusion.35
  43.7 0.7 fusion.34
  44.4 0.7 fusion.35
  45.1 0.7 fusion.34
  45.8 0.7 fusion.35
  46.6 0.7 fusion.34
  47.2 0.7 fusion.35
  48.0 0.7 fusion.34
  48.6 0.7 fusion.35
  49.4 1.5 multiply_reduce_fusion.2
  51.1 5.2 %all-gather = f32[4,2,256]{2,1,0:T(2,128)S(1)} all-gather(f32[1,2,256]{2,1,0:T(2,128)S(1)} %copy.77), channel_id=1, replica_groups=mesh['frag'=8,'tile'=4] {'tile'}, dimensions={0}, use_global_device_ids=true | all-gather | bytes 10240 | tf_op jit(solution)/shard_map/all_gather | solution.py:113
  56.4 4.2 %collective-permute-start = (f32[8,4,256]{2,1,0:T(4,128)S(1)}, f32[8,4,256]{2,1,0:T(4,128)S(1)}, u32[]{:S(2)}, u32[]{:S(2)}) collective-permute-start(f32[8,4,256]{2,1,0:T(4,128)S(1)} %pad_maximum_fusion.2), channel_id=1, source_target_pairs={{0,4},{4,8},{8,12},{12,16},{16,20},{20,24},{24,28},{1,5},{5,9},{9,... | collective-permute-start | bytes 98312 | tf_op jit(solution)/shard_map/ppermute | solution.py:21
  60.6 1.3 collective-permute-start.1
  62.1 3.5 %all-to-all-start.1 = ((f32[2,256,256]{2,0,1:T(2,128)}), f32[2,256,256]{2,0,1:T(2,128)S(1)}, u32[]{:S(2)}, u32[]{:S(2)}) async-start(f32[2,256,256]{2,0,1:T(2,128)} %get-tuple-element.139), calls=%async_computation.1 | async-start | bytes 1048576 | tf_op jit(solution)/shard_map/all_to_all | solution.py:128
  65.5 33.0 %all_gather.7 = f32[64,4,8]{2,1,0:T(4,128)S(1)} all-gather(f32[8,4,8]{2,1,0:T(4,128)S(1)} %copy.80), channel_id=1, replica_groups=mesh['frag'=8,'tile'=4] {'frag'}, dimensions={0}, use_global_device_ids=true | all-gather | bytes 9216 | tf_op jit(solution)/shard_map/all_gather | solution.py:116
  98.6 46.9 %while.33 = (s32[]{:T(128)}, f32[2,256]{1,0:T(2,128)S(1)}, s32[2,8]{1,0:T(2,128)S(1)}, f32[2,3,256]{2,1,0:T(4,128)S(1)}, f32[24,4,256]{2,1,0:T(4,128)S(1)}, /*in...) while((s32[]{:T(128)}, f32[2,256]{1,0:T(2,128)S(1)}, ...), condition=%wide.region_11.12_spmd, body=%wide.region_6.11_spmd.sunk | while | flops 902693 | bytes 59082 | solution.py:55
  99.8 22.2 %while.34 = (s32[]{:T(128)}, f32[256]{0:T(256)S(1)}, s32[8]{0:T(128)S(1)}, f32[24,4,256]{2,1,0:T(4,128)S(1)}, f32[3,256]{1,0:T(4,128)S(1)}, /*index=5*/s32[]{:T(...) while((s32[]{:T(128)}, f32[256]{0:T(256)S(1)}, s32[8]{0:T(128)S(1)}, ...), condition=%wide.region_9.9_spmd.clone, body=%wide.region_7.8_spmd.clone.sunk | while | flops 721161 | bytes 25817 | solution.py:51
  99.8 0.6 dynamic_slice.72
  102.5 0.6 dynamic_slice.72
  105.3 0.6 dynamic_slice.72
  108.1 0.6 dynamic_slice.72
  110.9 0.6 dynamic_slice.72
  113.6 0.6 dynamic_slice.72
  116.4 0.6 dynamic_slice.72
  119.2 0.6 dynamic_slice.72
  123.2 22.2 %while.34 = (s32[]{:T(128)}, f32[256]{0:T(256)S(1)}, s32[8]{0:T(128)S(1)}, f32[24,4,256]{2,1,0:T(4,128)S(1)}, f32[3,256]{1,0:T(4,128)S(1)}, /*index=5*/s32[]{:T(...) while((s32[]{:T(128)}, f32[256]{0:T(256)S(1)}, s32[8]{0:T(128)S(1)}, ...), condition=%wide.region_9.9_spmd.clone, body=%wide.region_7.8_spmd.clone.sunk | while | flops 721161 | bytes 25817 | solution.py:51
  123.2 0.6 dynamic_slice.72
  126.0 0.6 dynamic_slice.72
  128.8 0.6 dynamic_slice.72
  131.5 0.6 dynamic_slice.72
  134.3 0.6 dynamic_slice.72
  137.1 0.6 dynamic_slice.72
  139.9 0.6 dynamic_slice.72
  142.6 0.6 dynamic_slice.72
  145.6 1.2 add_multiply_fusion.1
  146.8 3.5 %all-to-all-start.2 = ((f32[2,256,256]{2,0,1:T(2,128)}), f32[2,256,256]{2,0,1:T(2,128)S(1)}, u32[]{:S(2)}, u32[]{:S(2)}) async-start(f32[2,256,256]{2,0,1:T(2,128)} %add_multiply_fusion.1), calls=%async_computation.2 | async-start | bytes 1048576 | tf_op jit(solution)/shard_map/all_to_all | solution.py:129
  150.2 0.8 copy.74
  151.1 8.0 %all-to-all-done.2 = f32[2,256,256]{2,0,1:T(2,128)S(1)} async-done(((f32[2,256,256]{2,0,1:T(2,128)}), f32[2,256,256]{2,0,1:T(2,128)S(1)}, u32[]{:S(2)}, u32[]{:S(2)}) %all-to-all-start.2) | async-done | bytes 524320 | tf_op jit(solution)/shard_map/all_to_all | solution.py:129
  159.0 0.8 copy.82
  (166 shorter events, 10.6 us)
Async XLA Ops:
  0.6 8.5 %copy-start = (f32[8,256]{1,0:T(8,128)S(1)}, f32[8,256]{1,0:T(8,128)}, u32[]{:S(2)}) copy-start(f32[8,256]{1,0:T(8,128)} %param.19) | copy-start | bytes 24580
  3.3 4.3 %copy-start.13 = (s32[8]{0:T(128)S(1)}, s32[8]{0:T(128)}, u32[]{:S(2)}) copy-start(s32[8]{0:T(128)} %param.23) | copy-start | bytes 100
  3.3 4.5 %copy-start.4 = (f32[8,3,256]{2,0,1:T(8,128)S(1)}, f32[8,3,256]{2,0,1:T(8,128)}, u32[]{:S(2)}) copy-start(f32[8,3,256]{2,0,1:T(8,128)} %param.22) | copy-start | bytes 73732
  3.3 6.4 %copy-start.10 = (s32[8,8]{1,0:T(8,128)S(1)}, s32[8,8]{1,0:T(8,128)}, u32[]{:S(2)}) copy-start(s32[8,8]{1,0:T(8,128)} %param.24) | copy-start | bytes 772
  3.3 24.4 %all-to-all-start = ((f32[8,3,64,256]{3,2,1,0:T(8,128)}), f32[8,3,64,256]{3,2,1,0:T(8,128)S(1)}, u32[]{:S(2)}, u32[]{:S(2)}) async-start(f32[8,3,64,256]{3,2,1,0:T(8,128)} %pad_maximum_fusion), calls=%async_computation | async-start | bytes 3145728 | tf_op jit(solution)/shard_map/all_to_all | solution.py:103
  7.8 19.9 %copy-start.6 = (f32[2,256]{1,0:T(2,128)}, f32[2,256]{1,0:T(2,128)S(1)}, u32[]{:S(2)}) copy-start(f32[2,256]{1,0:T(2,128)S(1)} %compare_convert_fusion) | copy-start | bytes 6148
  7.9 3.0 %copy-start.2 = (f32[8,3,256]{2,1,0:T(4,128)}, f32[8,3,256]{2,1,0:T(4,128)S(1)}, u32[]{:S(2)}) copy-start(f32[8,3,256]{2,1,0:T(4,128)S(1)} %copy.75) | copy-start | bytes 73732
  27.8 1.4 copy-start.9
  29.0 1.7 %copy-start.1 = (f32[2,256]{0,1:T(8,128)S(1)}, f32[2,256]{0,1:T(8,128)}, u32[]{:S(2)}) copy-start(f32[2,256]{0,1:T(8,128)} %copy.70) | copy-start | bytes 6148
  29.0 1.6 %copy-start.7 = (f32[2,256]{1,0:T(2,128)S(1)}, f32[2,256]{1,0:T(2,128)}, u32[]{:S(2)}) copy-start(f32[2,256]{1,0:T(2,128)} %copy-done.6) | copy-start | bytes 6148
  49.4 7.0 %copy-start.3 = (f32[8,3,256]{2,1,0:T(4,128)S(1)}, f32[8,3,256]{2,1,0:T(4,128)}, u32[]{:S(2)}) copy-start(f32[8,3,256]{2,1,0:T(4,128)} %copy-done.2) | copy-start | bytes 73732
  49.4 12.7 %copy-start.5 = (f32[8,3,8]{2,0,1:T(8,128)S(1)}, f32[8,3,8]{2,0,1:T(8,128)}, u32[]{:S(2)}) copy-start(f32[8,3,8]{2,0,1:T(8,128)} %broadcast_multiply_fusion) | copy-start | bytes 2308
  50.9 47.7 %copy-start.8 = (f32[2,256]{1,0:T(2,128)S(1)}, f32[2,256]{1,0:T(2,128)}, u32[]{:S(2)}) copy-start(f32[2,256]{1,0:T(2,128)} %custom-call.3) | copy-start | bytes 6148
  50.9 47.7 %copy-start.11 = (s32[2,8]{1,0:T(2,128)S(1)}, s32[2,8]{1,0:T(2,128)}, u32[]{:S(2)}) copy-start(s32[2,8]{1,0:T(2,128)} %get-tuple-element.331) | copy-start | bytes 196
  50.9 47.7 %copy-start.12 = (s32[2,8]{1,0:T(2,128)S(1)}, s32[2,8]{1,0:T(2,128)}, u32[]{:S(2)}) copy-start(s32[2,8]{1,0:T(2,128)} %get-tuple-element.328) | copy-start | bytes 196
  56.4 42.1 %collective-permute-start = (f32[8,4,256]{2,1,0:T(4,128)S(1)}, f32[8,4,256]{2,1,0:T(4,128)S(1)}, u32[]{:S(2)}, u32[]{:S(2)}) collective-permute-start(f32[8,4,256]{2,1,0:T(4,128)S(1)} %pad_maximum_fusion.2), channel_id=1, source_target_pairs={{0,4},{4,8},{8,12},{12,16},{16,20},{20,24},{24,28},{1,5},{5,9},{9,... | collective-permute-start | bytes 98312 | tf_op jit(solution)/shard_map/ppermute | solution.py:21
  60.6 37.9 %collective-permute-start.1 = (f32[8,4,256]{2,1,0:T(4,128)S(1)}, f32[8,4,256]{2,1,0:T(4,128)S(1)}, u32[]{:S(2)}, u32[]{:S(2)}) collective-permute-start(f32[8,4,256]{2,1,0:T(4,128)S(1)} %pad_maximum_fusion.2), channel_id=1, source_target_pairs={{4,0},{8,4},{12,8},{16,12},{20,16},{24,20},{28,24},{5,1},{9,5},{13... | collective-permute-start | bytes 98312 | tf_op jit(solution)/shard_map/ppermute | solution.py:22
  62.1 84.7 %all-to-all-start.1 = ((f32[2,256,256]{2,0,1:T(2,128)}), f32[2,256,256]{2,0,1:T(2,128)S(1)}, u32[]{:S(2)}, u32[]{:S(2)}) async-start(f32[2,256,256]{2,0,1:T(2,128)} %get-tuple-element.139), calls=%async_computation.1 | async-start | bytes 1048576 | tf_op jit(solution)/shard_map/all_to_all | solution.py:128
  146.8 12.3 %all-to-all-start.2 = ((f32[2,256,256]{2,0,1:T(2,128)}), f32[2,256,256]{2,0,1:T(2,128)S(1)}, u32[]{:S(2)}, u32[]{:S(2)}) async-start(f32[2,256,256]{2,0,1:T(2,128)} %add_multiply_fusion.1), calls=%async_computation.2 | async-start | bytes 1048576 | tf_op jit(solution)/shard_map/all_to_all | solution.py:129
where the time goes:
time: 161 us; the launch traced here: 160 us
  blocking collectives  38.1 us (24%)
  loops' own time  30.5 us (19%)
  waiting for transfers between devices  24.1 us (15%)
  local copies, waits for them, and re-layouts  19.4 us (12%)
  starting transfers between devices  16.8 us (10%)
  matrix products  16.8 us (10%)
  other arithmetic  13.2 us (8%)
    all_gather x1, blocking collectives, per_device(): far_table = lax.all_gather(blocks_own, 'frag', axis=0, tiled=True)  33 us
    another operation x2, loops' own time, potential_of(): lax.scan(add_near, jnp.zeros((basis_count,), jnp.float32), near_ids)  29.8 us
    all_to_all x1, waiting for transfers between devices, per_device(): lax.all_to_all(stacked, 'tile', split_axis=0, concat_axis=2, tiled=True)  16.2 us
    dynamic_slice x16, local copies, waits for them, and re-layouts, potential_of(): lax.scan(add_near, jnp.zeros((basis_count,), jnp.float32), near_ids)  9.87 us
    dot_general x12, matrix products, cube_step(): jnp.einsum('fij,fjk->fik', squared, full_rows, precision=precise)  8.36 us
    all_to_all x1, waiting for transfers between devices, per_device(): lax.all_to_all(esp_whole, 'tile', split_axis=1, concat_axis=0, tiled=True)  7.97 us
    dot_general x12, matrix products, cube_step(): squared = jnp.einsum('fij,fjk->fik', sign_est, full_rows, precision=precise)  7.9 us
    all_gather x1, blocking collectives, per_device(): charges = lax.all_gather(charge_share, 'tile', axis=0, tiled=True)  5.16 us
  transfers between devices with their start and end apart: 5, of which 2 were waited for; matrix products, arithmetic and copies ran while one was open for 14% of the time, Pallas kernels for 0%

commit v1 on v0

v1 whole, which is shorter than its diff:
```python
import functools

import jax
import jax.numpy as jnp
from jax import lax
from jax.experimental import pallas as pl
from jax.experimental.pallas import tpu as pltpu
from jax.sharding import PartitionSpec as P

PC = 8
ITERS = 12
SCREENING = 0.25
VMEM = pl.BlockSpec(memory_space=pltpu.VMEM)
SMEM = pl.BlockSpec(memory_space=pltpu.SMEM)


def floats(*shape):
    return jax.ShapeDtypeStruct(shape, jnp.float32)


def own_rows(rows, basis, tile_at):
    row = lax.broadcasted_iota(jnp.int32, (rows, basis), 0)
    column = lax.broadcasted_iota(jnp.int32, (rows, basis), 1)
    return column == row + tile_at * rows


def half_fock_kernel(core_ref, over_ref, gamma_ref, charge_ref, embed_ref, *outs):
    tiles = lax.axis_size("tile")
    tile_at = lax.axis_index("tile")
    frag_dev, rows, basis = core_ref.shape
    share = frag_dev // tiles
    pick = own_rows(rows, basis, tile_at)
    for shift in range(tiles):
        target = lax.rem(tile_at + shift, tiles)
        for place in range(share):
            frag = target * share + place
            over = over_ref[frag]
            terms = gamma_ref[frag] * charge_ref[pl.ds(frag, 1), :]
            terms = terms + jnp.where(pick, embed_ref[pl.ds(frag, 1), :], 0.0)
            field = jnp.sum(terms, axis=1, keepdims=True)
            outs[shift][place] = 0.5 * (core_ref[frag] + over * field)
            outs[tiles + shift][place] = over


def split(x):
    high = x.astype(jnp.bfloat16)
    low = (x - high.astype(jnp.float32)).astype(jnp.bfloat16)
    return high, low


def product(left, right):
    lh, ll = left
    rh, rl = right
    dot = functools.partial(jnp.dot, preferred_element_type=jnp.float32)
    return dot(lh, rh) + (dot(lh, rl) + dot(ll, rh))


def density_kernel(tiles, sizes_ref, pop_ref, *refs):
    halves, overs = refs[:tiles], refs[tiles : 2 * tiles]
    chunks, charge_ref = refs[2 * tiles : 3 * tiles], refs[3 * tiles]
    x_ref, s_ref = refs[3 * tiles + 1 :]
    tile_at = lax.axis_index("tile")
    share, rows, basis = halves[0].shape
    for shift in range(tiles):
        source = lax.rem(tile_at + tiles - shift, tiles)
        span = pl.ds(pl.multiple_of(source * rows, rows), rows)
        for place in range(share):
            x_ref[place, span, :] = halves[shift][place]
            s_ref[place, span, :] = overs[shift][place]
    row = lax.broadcasted_iota(jnp.int32, (basis, basis), 0)
    column = lax.broadcasted_iota(jnp.int32, (basis, basis), 1)
    for place in range(share):
        size = sizes_ref[tile_at * share + place]
        half = x_ref[place]
        fock = half + half.T
        masked = jnp.where((row < size) & (column < size), fock, 0.0)
        frob = jnp.sqrt(jnp.sum(masked * masked, keepdims=True) + 1e-06)
        x_ref[place] = masked / frob + jnp.where((row == column) & (row >= size), 1.0, 0.0)

    def sweep(index, carry):
        estimates = [x_ref[place] for place in range(share)]
        parts = [split(x) for x in estimates]
        squares = [split(0.5 * product(p, p)) for p in parts]
        cubes = [product(y, p) for y, p in zip(squares, parts)]
        for place in range(share):
            x_ref[place] = 1.5 * estimates[place] - cubes[place]
        return carry

    lax.fori_loop(0, ITERS, sweep, 0)
    devices = charge_ref.shape[0]
    for place in range(share):
        density = jnp.where(row == column, 0.5, 0.0) - 0.5 * x_ref[place]
        x_ref[place] = density
        charge = jnp.sum(density * s_ref[place], axis=0, keepdims=True)
        charge = charge - pop_ref[pl.ds(tile_at * share + place, 1), :]
        charge_ref[:, place : place + 1, :] = jnp.broadcast_to(charge[None], (devices, 1, basis))
    for shift in range(tiles):
        target = lax.rem(tile_at + shift, tiles)
        span = pl.ds(pl.multiple_of(target * rows, rows), rows)
        for place in range(share):
            chunks[shift][place] = x_ref[place, span, :]


def block_mask(group, basis):
    block = lax.broadcasted_iota(jnp.int32, (PC, basis), 0)
    column = lax.broadcasted_iota(jnp.int32, (PC, basis), 1)
    return (column >= block * group) & (column < (block + 1) * group)


def coulomb_kernel(near_ref, far_ref, place_ref, column_ref, table_ref, near_out, far_out):
    frag_dev, basis, _ = column_ref.shape
    near, far = near_ref.shape[1], far_ref.shape[1]
    group = basis // PC
    mask = block_mask(group, basis)

    def one_fragment(frag, carry):
        spots = column_ref[frag]
        columns = [spots[:, axis : axis + 1] for axis in range(3)]
        rows = [place_ref[frag, axis : axis + 1, :] for axis in range(3)]
        for k in range(near):
            other = near_ref[frag, k]
            total = 1.0
            for axis in range(3):
                gap = columns[axis] - table_ref[other, axis : axis + 1, :]
                total = total + gap * gap
            near_out[frag, k] = lax.rsqrt(total)
        for m in range(far):
            other = far_ref[frag, m]
            total = 1.0
            for axis in range(3):
                inside = jnp.where(mask, table_ref[other, axis : axis + 1, :], 0.0)
                spot = jnp.sum(inside, axis=1, keepdims=True) * (1.0 / group)
                gap = rows[axis] - spot
                total = total + gap * gap
            far_out[frag, m] = lax.rsqrt(total)
        return carry

    lax.fori_loop(0, frag_dev, one_fragment, 0)


def potential_kernel(tiles, near_ref, far_ref, charge_ref, near_part, far_part, over_ref, *refs):
    chunks, density_ref, esp_ref = refs[:tiles], refs[tiles], refs[tiles + 1]
    tile_at = lax.axis_index("tile")
    frag_dev, rows, basis = over_ref.shape
    share = frag_dev // tiles
    near, far = near_ref.shape[1], far_ref.shape[1]
    pick = own_rows(rows, basis, tile_at)
    mask = block_mask(basis // PC, basis)
    for shift in range(tiles):
        source = lax.rem(tile_at + tiles - shift, tiles)
        for place in range(share):
            density_ref[source * share + place] = chunks[shift][place]

    def one_fragment(frag, carry):
        total = jnp.zeros((basis, basis), jnp.float32)
        for k in range(near):
            total = total + near_part[frag, k] * charge_ref[pl.ds(near_ref[frag, k], 1), :]
        folded = total[:, :128]
        for start in range(128, basis, 128):
            folded = folded + total[:, start : start + 128]
        blocks = jnp.zeros((PC, basis), jnp.float32)
        for m in range(far):
            inside = jnp.where(mask, charge_ref[pl.ds(far_ref[frag, m], 1), :], 0.0)
            blocks = blocks + jnp.sum(inside, axis=1, keepdims=True) * far_part[frag, m]
        potential = jnp.sum(folded.T, axis=0, keepdims=True) + jnp.sum(blocks, axis=0, keepdims=True)
        potential = (0.5 * SCREENING) * potential
        mine = jnp.sum(jnp.where(pick, potential, 0.0), axis=1, keepdims=True)
        esp_ref[frag] = over_ref[frag] * (mine + potential)
        return carry

    lax.fori_loop(0, frag_dev, one_fragment, 0)


def call(kernel, outs, inputs, specs, scratch=()):
    return pl.pallas_call(
        kernel,
        out_shape=outs,
        in_specs=specs,
        out_specs=[VMEM] * len(outs),
        scratch_shapes=list(scratch),
        compiler_params=pltpu.CompilerParams(vmem_limit_bytes=48 * 1024 * 1024),
    )(*inputs)


def shifted(chunks, axis):
    peers = lax.axis_size(axis)
    moved = [chunks[0]]
    for shift in range(1, peers):
        pairs = [(i, (i + shift) % peers) for i in range(peers)]
        moved.append(lax.ppermute(chunks[shift], axis, pairs))
    return moved


def per_device(
    core_fock,
    intersection,
    gamma_tile,
    charge_old,
    embed_old,
    core_pop,
    centres,
    frag_sizes,
    near_list,
    far_list,
):
    frag_dev, rows, basis = core_fock.shape
    tiles, peers = lax.axis_size("tile"), lax.axis_size("frag")
    devices, share = tiles * peers, frag_dev // tiles
    chunk = floats(share, rows, basis)
    sent = call(
        half_fock_kernel,
        [chunk] * (2 * tiles),
        (core_fock, intersection, gamma_tile, charge_old, embed_old),
        [VMEM] * 5,
    )
    halves = shifted(sent[:tiles], "tile")
    overs = shifted(sent[tiles:], "tile")
    copies = jnp.broadcast_to(centres[None], (peers,) + centres.shape)
    table = lax.all_to_all(copies, "frag", split_axis=0, concat_axis=0, tiled=True)
    table = table.reshape((peers * frag_dev,) + centres.shape[1:])
    near_part, far_part = call(
        coulomb_kernel,
        [floats(frag_dev, near_list.shape[1], basis, basis), floats(frag_dev, far_list.shape[1], PC, basis)],
        (near_list, far_list, centres, jnp.transpose(centres, (0, 2, 1)), table),
        [SMEM, SMEM, VMEM, VMEM, VMEM],
    )
    *pieces, charges = call(
        functools.partial(density_kernel, tiles),
        [chunk] * tiles + [floats(devices, share, basis)],
        (frag_sizes, core_pop, *halves, *overs),
        [SMEM] + [VMEM] * (1 + 2 * tiles),
        [pltpu.VMEM((share, basis, basis), jnp.float32)] * 2,
    )
    charges = lax.all_to_all(charges, ("frag", "tile"), split_axis=0, concat_axis=0, tiled=True)
    charges = charges.reshape(devices * share, basis)
    pieces = shifted(pieces, "tile")
    density, esp_matrix = call(
        functools.partial(potential_kernel, tiles),
        [floats(frag_dev, rows, basis)] * 2,
        (near_list, far_list, charges, near_part, far_part, intersection, *pieces),
        [SMEM, SMEM] + [VMEM] * (4 + tiles),
    )
    return (density, esp_matrix)


def solution(mesh):
    in_specs = (
        P("frag", "tile", None),
        P("frag", "tile", None),
        P("frag", "tile", None),
        P("frag", None),
        P("frag", None),
        P("frag", None),
        P("frag", None, None),
        P("frag"),
        P("frag", None),
        P("frag", None),
    )
    out_specs = (P("frag", "tile", None), P("frag", "tile", None))
    return jax.shard_map(
        per_device, mesh=mesh, in_specs=in_specs, out_specs=out_specs, check_vma=False
    )
```

time: 161 us -> 84.2 us (0.52)
  Pallas kernels: 0 us -> 31.3 us
  loops' own time: 30.5 us -> 0 us
  blocking collectives: 38.1 us -> 13.5 us
  matrix products: 16.8 us -> 0 us
  other arithmetic: 13.2 us -> 0 us
  waiting for transfers between devices: 24.1 us -> 13.8 us
  local copies, waits for them, and re-layouts: 19.4 us -> 13.1 us
  starting transfers between devices: 16.8 us -> 10.9 us
    all_gather x2 -> x0, blocking collectives: 38.1 us -> none  [the longest x1 33 us: per_device(): far_table = lax.all_gather(blocks_own, 'frag', axis=0, tiled=True)]
    pallas_call x0 -> x4, Pallas kernels: none -> 31.3 us  [call(): pl.pallas_call(kernel, out_shape=outs, in_specs=specs, out_specs=[VMEM] *...]
    another operation x4 -> x0, loops' own time: 30.5 us -> none  [the longest x2 29.8 us: potential_of(): lax.scan(add_near, jnp.zeros((basis_count,), jnp.float32), near_ids)]
    all_to_all x3 -> x1, waiting for transfers between devices: 24.1 us -> 4.57 us  [per_device(): lax.all_to_all(copies, 'frag', split_axis=0, concat_axis=0, tiled=True)]
    dot_general x25 -> x0, matrix products: 16.8 us -> none  [the longest x12 8.36 us: cube_step(): jnp.einsum('fij,fjk->fik', squared, full_rows, precision=precise)]
    all_to_all x0 -> x1, blocking collectives: none -> 13.5 us  [per_device(): lax.all_to_all(charges, ('frag', 'tile'), split_axis=0, concat_axis=0, ti...]
    dynamic_slice x20 -> x0, local copies, waits for them, and re-layouts: 11.8 us -> none  [the longest x16 9.87 us: potential_of(): lax.scan(add_near, jnp.zeros((basis_count,), jnp.float32), near_ids)]
    unnamed x31 -> x26, local copies, waits for them, and re-layouts: 0.29 us -> 11.5 us
  transfers between devices with their start and end apart: 5 -> 10, of which waited for: 2 -> 7; matrix products, arithmetic and copies ran while one was open for 14% -> 2% of each run, Pallas kernels for 0% -> 15%
where the time goes in v1:
time: 84.2 us; the launch traced here: 83.2 us
  Pallas kernels  31.3 us (37%)
  waiting for transfers between devices  13.8 us (16%)
  blocking collectives  13.5 us (16%)
  local copies, waits for them, and re-layouts  13.1 us (16%)
  starting transfers between devices  10.9 us (13%)
    pallas_call x4, Pallas kernels, call(): pl.pallas_call(kernel, out_shape=outs, in_specs=specs, out_specs=[VMEM] *...  31.3 us
    all_to_all x1, blocking collectives, per_device(): lax.all_to_all(charges, ('frag', 'tile'), split_axis=0, concat_axis=0, ti...  13.5 us
    unnamed x26, local copies, waits for them, and re-layouts  11.5 us
    ppermute x9, waiting for transfers between devices, shifted(): moved.append(lax.ppermute(chunks[shift], axis, pairs))  9.18 us
    ppermute x9, starting transfers between devices, shifted(): moved.append(lax.ppermute(chunks[shift], axis, pairs))  7.52 us
    all_to_all x1, waiting for transfers between devices, per_device(): lax.all_to_all(copies, 'frag', split_axis=0, concat_axis=0, tiled=True)  4.57 us
    all_to_all x1, starting transfers between devices, per_device(): lax.all_to_all(copies, 'frag', split_axis=0, concat_axis=0, tiled=True)  3.39 us
  transfers between devices with their start and end apart: 10, of which 7 were waited for; matrix products, arithmetic and copies ran while one was open for 2% of the time, Pallas kernels for 15%

profile of v1, /device:TPU:0, one launch (start us, length us, event | category | flops | bytes accessed | tf_op | source)
XLA Modules:
  0.0 83.2 jit_solution(44290170343354688)
XLA Ops:
  0.6 0.0 copy-start
  0.6 1.0 %copy-done = f32[8,64,256]{2,1,0:T(8,128)S(1)} copy-done((f32[8,64,256]{2,1,0:T(8,128)S(1)}, f32[8,64,256]{2,1,0:T(8,128)}, u32[]{:S(2)}) %copy-start) | copy-done | bytes 524312
  1.7 0.0 copy-start.2
  1.7 1.0 %copy-done.2 = f32[8,64,256]{2,1,0:T(8,128)S(1)} copy-done((f32[8,64,256]{2,1,0:T(8,128)S(1)}, f32[8,64,256]{2,1,0:T(8,128)}, u32[]{:S(2)}) %copy-start.2) | copy-done | bytes 524312
  2.7 0.0 copy-start.3
  2.7 1.0 %copy-done.3 = f32[8,64,256]{2,1,0:T(8,128)S(1)} copy-done((f32[8,64,256]{2,1,0:T(8,128)S(1)}, f32[8,64,256]{2,1,0:T(8,128)}, u32[]{:S(2)}) %copy-start.3) | copy-done | bytes 524312
  3.8 0.0 copy-start.8
  3.8 0.7 copy-done.8
  4.5 0.0 copy-start.9
  4.5 0.7 copy-done.9
  5.2 0.2 shard_map.113
  5.3 0.5 collective-permute-start
  5.8 2.6 %collective-permute-start.1 = (f32[2,64,256]{2,1,0:T(8,128)S(1)}, f32[2,64,256]{2,1,0:T(8,128)S(1)}, u32[]{:S(2)}, u32[]{:S(2)}) collective-permute-start(f32[2,64,256]{2,1,0:T(8,128)S(1)} %get-tuple-element.19), channel_id=1, source_target_pairs={{0,2},{1,3},{2,0},{3,1},{4,6},{5,7},{6,4},{7,5},{8,10},{9,11},{10,... | collective-permute-start | bytes 393224 | tf_op jit(solution)/shard_map/ppermute | solution.py:190
  8.4 1.4 %collective-permute-start.2 = (f32[2,64,256]{2,1,0:T(8,128)S(1)}, f32[2,64,256]{2,1,0:T(8,128)S(1)}, u32[]{:S(2)}, u32[]{:S(2)}) collective-permute-start(f32[2,64,256]{2,1,0:T(8,128)S(1)} %get-tuple-element.20), channel_id=1, source_target_pairs={{0,3},{1,0},{2,1},{3,2},{4,7},{5,4},{6,5},{7,6},{8,11},{9,8},{10,9... | collective-permute-start | bytes 393224 | tf_op jit(solution)/shard_map/ppermute | solution.py:190
  9.8 0.0 collective-permute-start.3
  9.8 0.4 collective-permute-start.4
  10.2 0.7 collective-permute-done.refs_1_
  10.9 0.7 collective-permute-start.5
  11.6 1.0 %collective-permute-done.1.refs_2_ = f32[2,64,256]{2,1,0:T(8,128)S(1)} collective-permute-done((f32[2,64,256]{2,1,0:T(8,128)S(1)}, f32[2,64,256]{2,1,0:T(8,128)S(1)}, u32[]{:S(2)}, u32[]{:S(2)}) %collective-permute-start.1) | collective-permute-done | bytes 131104 | tf_op jit(solution)/shard_map/ppermute | solution.py:190
  12.6 2.5 %collective-permute-done.2.refs_3_ = f32[2,64,256]{2,1,0:T(8,128)S(1)} collective-permute-done((f32[2,64,256]{2,1,0:T(8,128)S(1)}, f32[2,64,256]{2,1,0:T(8,128)S(1)}, u32[]{:S(2)}, u32[]{:S(2)}) %collective-permute-start.2) | collective-permute-done | bytes 131104 | tf_op jit(solution)/shard_map/ppermute | solution.py:190
  15.0 1.6 %collective-permute-done.3.refs_5_ = f32[2,64,256]{2,1,0:T(8,128)S(1)} collective-permute-done((f32[2,64,256]{2,1,0:T(8,128)S(1)}, f32[2,64,256]{2,1,0:T(8,128)S(1)}, u32[]{:S(2)}, u32[]{:S(2)}) %collective-permute-start.3) | collective-permute-done | bytes 131104 | tf_op jit(solution)/shard_map/ppermute | solution.py:190
  16.6 1.6 %collective-permute-done.4.refs_6_ = f32[2,64,256]{2,1,0:T(8,128)S(1)} collective-permute-done((f32[2,64,256]{2,1,0:T(8,128)S(1)}, f32[2,64,256]{2,1,0:T(8,128)S(1)}, u32[]{:S(2)}, u32[]{:S(2)}) %collective-permute-start.4) | collective-permute-done | bytes 131104 | tf_op jit(solution)/shard_map/ppermute | solution.py:190
  18.2 1.9 %collective-permute-done.5.refs_7_ = f32[2,64,256]{2,1,0:T(8,128)S(1)} collective-permute-done((f32[2,64,256]{2,1,0:T(8,128)S(1)}, f32[2,64,256]{2,1,0:T(8,128)S(1)}, u32[]{:S(2)}, u32[]{:S(2)}) %collective-permute-start.5) | collective-permute-done | bytes 131104 | tf_op jit(solution)/shard_map/ppermute | solution.py:190
  20.1 0.0 copy-start.10
  20.1 0.7 copy-done.10
  20.7 0.0 copy-start.11
  20.7 0.7 copy-done.11
  21.4 9.1 %shard_map.114 = (f32[2,64,256]{2,1,0:T(8,128)S(1)}, f32[2,64,256]{2,1,0:T(8,128)S(1)}, f32[2,64,256]{2,1,0:T(8,128)S(1)}, f32[2,64,256]{2,1,0:T(8,128)S(1)}, f32[32,2,256]{2,1,0:T(2,128)S(1)}) custom-call(s32[8]{0:T(128)S(1)} %copy-done.11, f32[8,256]{1,0:T(8,128)S(1)} %copy-done.10, f32[2,64,256]{2,1,0:T(8,128)S(1)} %get-tuple-element.17.refs_0_, ...), custom_call_target="tpu_custom_call" | custom-call | tf_op jit(solution)/shard_map/pallas_call | solution.py:175
  30.6 13.5 %all_to_all.10 = f32[32,2,256]{2,1,0:T(2,128)S(1)} all-to-all(f32[32,2,256]{2,1,0:T(2,128)S(1)} %get-tuple-element.25), channel_id=1, replica_groups=mesh['frag'=8,'tile'=4] {'frag','tile'}, dimensions={0} | all-to-all | bytes 131072 | tf_op jit(solution)/shard_map/all_to_all | solution.py:234
  44.0 1.4 %broadcast_in_dim.2 = f32[8,8,3,256]{3,1,2,0:T(8,128)} broadcast(f32[8,3,256]{2,0,1:T(8,128)} %param.16), dimensions={1,2,3} | broadcast | bytes 221184 | tf_op jit(solution)/shard_map/broadcast_in_dim | solution.py:218
  45.5 3.4 %all-to-all-start.1 = ((f32[8,8,3,256]{3,1,2,0:T(8,128)}), f32[8,8,3,256]{3,1,2,0:T(8,128)S(1)}, u32[]{:S(2)}, u32[]{:S(2)}) async-start(f32[8,8,3,256]{3,1,2,0:T(8,128)} %broadcast_in_dim.2), calls=%async_computation.1 | async-start | bytes 393216 | tf_op jit(solution)/shard_map/all_to_all | solution.py:219
  48.9 0.2 collective-permute-start.6
  49.0 0.4 collective-permute-start.7
  49.5 1.4 %collective-permute-start.8 = (f32[2,64,256]{2,1,0:T(8,128)S(1)}, f32[2,64,256]{2,1,0:T(8,128)S(1)}, u32[]{:S(2)}, u32[]{:S(2)}) collective-permute-start(f32[2,64,256]{2,1,0:T(8,128)S(1)} %get-tuple-element.31), channel_id=1, source_target_pairs={{0,3},{1,0},{2,1},{3,2},{4,7},{5,4},{6,5},{7,6},{8,11},{9,8},{10,9... | collective-permute-start | bytes 393224 | tf_op jit(solution)/shard_map/ppermute | solution.py:190
  50.8 0.8 copy.17.place_ref
  51.6 1.1 %copy.15 = f32[8,3,256]{1,2,0:T(8,128)S(1)} copy(f32[8,3,256]{2,0,1:T(8,128)} %param.16) | data formatting | bytes 49152 | tf_op args[6]
  52.7 4.6 %all-to-all-done.1 = f32[8,8,3,256]{3,1,2,0:T(8,128)S(1)} async-done(((f32[8,8,3,256]{3,1,2,0:T(8,128)}), f32[8,8,3,256]{3,1,2,0:T(8,128)S(1)}, u32[]{:S(2)}, u32[]{:S(2)}) %all-to-all-start.1) | async-done | bytes 196640 | tf_op jit(solution)/shard_map/all_to_all | solution.py:219
  57.3 0.1 copy.16
  57.4 0.0 copy-start.4
  57.4 0.7 copy-done.4
  58.1 0.0 copy-start.6
  58.1 0.7 copy-done.6
  58.8 12.9 %shard_map.115 = (f32[8,8,256,256]{3,2,1,0:T(8,128)}, f32[8,8,8,256]{3,2,1,0:T(8,128)S(1)}) custom-call(s32[8,8]{1,0:T(8,128)S(1)} %copy-done.4, s32[8,8]{1,0:T(8,128)S(1)} %copy-done.6, f32[8,3,256]{2,1,0:T(4,128)S(1)} %copy.17.place_ref, f32[8,256,3]{2,1,0:T(8,128)S(1)} %bitcast.2, f32[64,3,256]{2,1,0:T(4,128)S(1)} %bitcast.3), custom_call_target="tpu_custom_call" | custom-call | tf_op jit(solution)/shard_map/pallas_call | solution.py:175
  71.7 0.0 collective-permute-done.6.refs_1_
  71.7 0.0 collective-permute-done.7.refs_2_
  71.7 0.0 collective-permute-done.8.refs_3_
  71.7 0.0 copy-start.1
  71.7 1.0 %copy-done.1 = f32[8,64,256]{2,1,0:T(8,128)S(1)} copy-done((f32[8,64,256]{2,1,0:T(8,128)S(1)}, f32[8,64,256]{2,1,0:T(8,128)}, u32[]{:S(2)}) %copy-start.1) | copy-done | bytes 524312
  72.7 0.0 copy-start.5
  72.7 0.7 copy-done.5
  73.4 0.0 copy-start.7
  73.4 0.7 copy-done.7
  74.1 9.1 %shard_map.116 = (f32[8,64,256]{2,1,0:T(8,128)}, f32[8,64,256]{2,1,0:T(8,128)}) custom-call(s32[8,8]{1,0:T(8,128)S(1)} %copy-done.5, s32[8,8]{1,0:T(8,128)S(1)} %copy-done.7, f32[64,256]{1,0:T(8,128)S(1)} %reshape.11.charge_ref, f32[8,8,256,256]{3,2,1,0:T(8,128)} %get-tuple-element.26.near_part, f32[8,8,8,256]{3,2,1,0:T(8,128)S(1)} %get-tuple-element.27.far_part, ...), custom_call_target="tpu_custom_call" | custom-call | tf_op jit(solution)/shard_map/pallas_call | solution.py:175
  (1 shorter events, 0.0 us)
Async XLA Ops:
  0.6 1.0 %copy-start = (f32[8,64,256]{2,1,0:T(8,128)S(1)}, f32[8,64,256]{2,1,0:T(8,128)}, u32[]{:S(2)}) copy-start(f32[8,64,256]{2,1,0:T(8,128)} %over_ref.3) | copy-start | bytes 1572868
  1.7 1.0 %copy-start.2 = (f32[8,64,256]{2,1,0:T(8,128)S(1)}, f32[8,64,256]{2,1,0:T(8,128)}, u32[]{:S(2)}) copy-start(f32[8,64,256]{2,1,0:T(8,128)} %core_ref.1) | copy-start | bytes 1572868
  2.7 1.0 %copy-start.3 = (f32[8,64,256]{2,1,0:T(8,128)S(1)}, f32[8,64,256]{2,1,0:T(8,128)}, u32[]{:S(2)}) copy-start(f32[8,64,256]{2,1,0:T(8,128)} %gamma_ref.1) | copy-start | bytes 1572868
  3.8 0.7 copy-start.8
  4.5 0.7 copy-start.9
  5.3 5.6 %collective-permute-start = (f32[2,64,256]{2,1,0:T(8,128)S(1)}, f32[2,64,256]{2,1,0:T(8,128)S(1)}, u32[]{:S(2)}, u32[]{:S(2)}) collective-permute-start(f32[2,64,256]{2,1,0:T(8,128)S(1)} %get-tuple-element.18), channel_id=1, source_target_pairs={{0,1},{1,2},{2,3},{3,0},{4,5},{5,6},{6,7},{7,4},{8,9},{9,10},{10,1... | collective-permute-start | bytes 393224 | tf_op jit(solution)/shard_map/ppermute | solution.py:190
  5.8 6.8 %collective-permute-start.1 = (f32[2,64,256]{2,1,0:T(8,128)S(1)}, f32[2,64,256]{2,1,0:T(8,128)S(1)}, u32[]{:S(2)}, u32[]{:S(2)}) collective-permute-start(f32[2,64,256]{2,1,0:T(8,128)S(1)} %get-tuple-element.19), channel_id=1, source_target_pairs={{0,2},{1,3},{2,0},{3,1},{4,6},{5,7},{6,4},{7,5},{8,10},{9,11},{10,... | collective-permute-start | bytes 393224 | tf_op jit(solution)/shard_map/ppermute | solution.py:190
  8.4 6.6 %collective-permute-start.2 = (f32[2,64,256]{2,1,0:T(8,128)S(1)}, f32[2,64,256]{2,1,0:T(8,128)S(1)}, u32[]{:S(2)}, u32[]{:S(2)}) collective-permute-start(f32[2,64,256]{2,1,0:T(8,128)S(1)} %get-tuple-element.20), channel_id=1, source_target_pairs={{0,3},{1,0},{2,1},{3,2},{4,7},{5,4},{6,5},{7,6},{8,11},{9,8},{10,9... | collective-permute-start | bytes 393224 | tf_op jit(solution)/shard_map/ppermute | solution.py:190
  9.8 6.9 %collective-permute-start.3 = (f32[2,64,256]{2,1,0:T(8,128)S(1)}, f32[2,64,256]{2,1,0:T(8,128)S(1)}, u32[]{:S(2)}, u32[]{:S(2)}) collective-permute-start(f32[2,64,256]{2,1,0:T(8,128)S(1)} %get-tuple-element.22), channel_id=1, source_target_pairs={{0,1},{1,2},{2,3},{3,0},{4,5},{5,6},{6,7},{7,4},{8,9},{9,10},{10,1... | collective-permute-start | bytes 393224 | tf_op jit(solution)/shard_map/ppermute | solution.py:190
  9.8 8.4 %collective-permute-start.4 = (f32[2,64,256]{2,1,0:T(8,128)S(1)}, f32[2,64,256]{2,1,0:T(8,128)S(1)}, u32[]{:S(2)}, u32[]{:S(2)}) collective-permute-start(f32[2,64,256]{2,1,0:T(8,128)S(1)} %get-tuple-element.23), channel_id=1, source_target_pairs={{0,2},{1,3},{2,0},{3,1},{4,6},{5,7},{6,4},{7,5},{8,10},{9,11},{10,... | collective-permute-start | bytes 393224 | tf_op jit(solution)/shard_map/ppermute | solution.py:190
  10.9 9.2 %collective-permute-start.5 = (f32[2,64,256]{2,1,0:T(8,128)S(1)}, f32[2,64,256]{2,1,0:T(8,128)S(1)}, u32[]{:S(2)}, u32[]{:S(2)}) collective-permute-start(f32[2,64,256]{2,1,0:T(8,128)S(1)} %get-tuple-element.24), channel_id=1, source_target_pairs={{0,3},{1,0},{2,1},{3,2},{4,7},{5,4},{6,5},{7,6},{8,11},{9,8},{10,9... | collective-permute-start | bytes 393224 | tf_op jit(solution)/shard_map/ppermute | solution.py:190
  20.1 0.7 copy-start.10
  20.7 0.7 copy-start.11
  45.5 11.8 %all-to-all-start.1 = ((f32[8,8,3,256]{3,1,2,0:T(8,128)}), f32[8,8,3,256]{3,1,2,0:T(8,128)S(1)}, u32[]{:S(2)}, u32[]{:S(2)}) async-start(f32[8,8,3,256]{3,1,2,0:T(8,128)} %broadcast_in_dim.2), calls=%async_computation.1 | async-start | bytes 393216 | tf_op jit(solution)/shard_map/all_to_all | solution.py:219
  48.9 22.8 %collective-permute-start.6 = (f32[2,64,256]{2,1,0:T(8,128)S(1)}, f32[2,64,256]{2,1,0:T(8,128)S(1)}, u32[]{:S(2)}, u32[]{:S(2)}) collective-permute-start(f32[2,64,256]{2,1,0:T(8,128)S(1)} %get-tuple-element.29), channel_id=1, source_target_pairs={{0,1},{1,2},{2,3},{3,0},{4,5},{5,6},{6,7},{7,4},{8,9},{9,10},{10,1... | collective-permute-start | bytes 393224 | tf_op jit(solution)/shard_map/ppermute | solution.py:190
  49.0 22.6 %collective-permute-start.7 = (f32[2,64,256]{2,1,0:T(8,128)S(1)}, f32[2,64,256]{2,1,0:T(8,128)S(1)}, u32[]{:S(2)}, u32[]{:S(2)}) collective-permute-start(f32[2,64,256]{2,1,0:T(8,128)S(1)} %get-tuple-element.30), channel_id=1, source_target_pairs={{0,2},{1,3},{2,0},{3,1},{4,6},{5,7},{6,4},{7,5},{8,10},{9,11},{10,... | collective-permute-start | bytes 393224 | tf_op jit(solution)/shard_map/ppermute | solution.py:190
  49.5 22.2 %collective-permute-start.8 = (f32[2,64,256]{2,1,0:T(8,128)S(1)}, f32[2,64,256]{2,1,0:T(8,128)S(1)}, u32[]{:S(2)}, u32[]{:S(2)}) collective-permute-start(f32[2,64,256]{2,1,0:T(8,128)S(1)} %get-tuple-element.31), channel_id=1, source_target_pairs={{0,3},{1,0},{2,1},{3,2},{4,7},{5,4},{6,5},{7,6},{8,11},{9,8},{10,9... | collective-permute-start | bytes 393224 | tf_op jit(solution)/shard_map/ppermute | solution.py:190
  57.4 0.7 copy-start.4
  58.1 0.7 copy-start.6
  71.7 1.0 %copy-start.1 = (f32[8,64,256]{2,1,0:T(8,128)S(1)}, f32[8,64,256]{2,1,0:T(8,128)}, u32[]{:S(2)}) copy-start(f32[8,64,256]{2,1,0:T(8,128)} %over_ref.3) | copy-start | bytes 1572868
  72.7 0.7 copy-start.5
  73.4 0.7 copy-start.7

commit v2 on v1

v2 whole, which is shorter than its diff:
```python
import functools

import jax
import jax.numpy as jnp
from jax import lax
from jax.experimental import pallas as pl
from jax.experimental.pallas import tpu as pltpu
from jax.sharding import PartitionSpec as P

PC = 8
ITERS = 12
SCREENING = 0.25
SPAN = 8
VMEM = pl.BlockSpec(memory_space=pltpu.VMEM)
SMEM = pl.BlockSpec(memory_space=pltpu.SMEM)
HBM = pl.BlockSpec(memory_space=pltpu.HBM)
ANY = pl.BlockSpec(memory_space=pl.ANY)


def floats(*shape):
    return jax.ShapeDtypeStruct(shape, jnp.float32)


def own_rows(rows, basis, tile_at):
    row = lax.broadcasted_iota(jnp.int32, (rows, basis), 0)
    column = lax.broadcasted_iota(jnp.int32, (rows, basis), 1)
    return column == row + tile_at * rows


def half_fock_kernel(*refs):
    inputs, outs, buffers, sems = refs[:8], refs[8:-9], refs[-9:-1], refs[-1]
    copies = [
        pltpu.make_async_copy(source, buffer, sems.at[at])
        for at, (source, buffer) in enumerate(zip(inputs, buffers))
    ]
    for copy in copies:
        copy.start()
    for copy in copies:
        copy.wait()
    sizes_ref, charge_ref, embed_ref, pop_ref, place_ref, gamma_ref, over_ref, core_ref = buffers
    tiles = lax.axis_size("tile")
    tile_at = lax.axis_index("tile")
    frag_dev, rows, basis = core_ref.shape
    share = frag_dev // tiles
    for peer in range(outs[-1].shape[0]):
        outs[-1][peer] = place_ref[...]
    pick = own_rows(rows, basis, tile_at)
    row = lax.broadcasted_iota(jnp.int32, (rows, basis), 0) + tile_at * rows
    column = lax.broadcasted_iota(jnp.int32, (rows, basis), 1)
    lane = lax.broadcasted_iota(jnp.int32, (1, basis), 1)
    for shift in range(tiles):
        target = lax.rem(tile_at + shift, tiles)
        for place in range(share):
            frag = target * share + place
            over = over_ref[frag]
            terms = gamma_ref[frag] * charge_ref[pl.ds(frag, 1), :]
            terms = terms + jnp.where(pick, embed_ref[pl.ds(frag, 1), :], 0.0)
            field = jnp.sum(terms, axis=1, keepdims=True)
            half = 0.5 * (core_ref[frag] + over * field)
            size = sizes_ref[frag]
            outs[shift][place] = jnp.where((row < size) & (column < size), half, 0.0)
            outs[tiles + shift][place] = over
            if shift == 0:
                outs[-2][place : place + 1, :] = (lane >= size).astype(jnp.float32)
                outs[-2][share + place : share + place + 1, :] = pop_ref[pl.ds(frag, 1), :]


def split(x):
    high = x.astype(jnp.bfloat16)
    low = (x - high.astype(jnp.float32)).astype(jnp.bfloat16)
    return high, low


def product(left, right):
    lh, ll = left
    rh, rl = right
    dot = functools.partial(jnp.dot, preferred_element_type=jnp.float32)
    return dot(lh, rh) + (dot(lh, rl) + dot(ll, rh))


def density_kernel(tiles, facts_ref, *refs):
    halves, chunks, x_ref = refs[:tiles], refs[-tiles - 1 : -1], refs[-1]
    tile_at = lax.axis_index("tile")
    share, rows, basis = halves[0].shape
    for shift in range(tiles):
        source = lax.rem(tile_at + tiles - shift, tiles)
        span = pl.ds(pl.multiple_of(source * rows, rows), rows)
        for place in range(share):
            x_ref[place, span, :] = halves[shift][place]
    row = lax.broadcasted_iota(jnp.int32, (basis, basis), 0)
    column = lax.broadcasted_iota(jnp.int32, (basis, basis), 1)
    for place in range(share):
        half = x_ref[place]
        masked = half + half.T
        frob = jnp.sqrt(jnp.sum(masked * masked, keepdims=True) + 1e-06)
        x_ref[place] = masked / frob + jnp.where(row == column, facts_ref[place : place + 1, :], 0.0)

    def sweep(index, carry):
        estimates = [x_ref[place] for place in range(share)]
        parts = [split(x) for x in estimates]
        squares = [split(0.5 * product(p, p)) for p in parts]
        cubes = [product(y, p) for y, p in zip(squares, parts)]
        for place in range(share):
            x_ref[place] = 1.5 * estimates[place] - cubes[place]
        return carry

    lax.fori_loop(0, ITERS, sweep, 0)
    for place in range(share):
        x_ref[place] = jnp.where(row == column, 0.5, 0.0) - 0.5 * x_ref[place]
    for shift in range(tiles):
        target = lax.rem(tile_at + shift, tiles)
        span = pl.ds(pl.multiple_of(target * rows, rows), rows)
        for place in range(share):
            chunks[shift][place] = x_ref[place, span, :]


def charge_kernel(tiles, facts_ref, *refs):
    overs, chunks, charge_ref = refs[:tiles], refs[tiles : 2 * tiles], refs[-1]
    share, rows, basis = overs[0].shape
    devices = charge_ref.shape[0]
    for place in range(share):
        terms = chunks[0][place] * overs[0][place]
        for shift in range(1, tiles):
            terms = terms + chunks[shift][place] * overs[tiles - shift][place]
        charge = jnp.sum(terms, axis=0, keepdims=True) - facts_ref[share + place : share + place + 1, :]
        charge_ref[:, place : place + 1, :] = jnp.broadcast_to(charge[None], (devices, 1, basis))


def block_mask(group, basis):
    block = lax.broadcasted_iota(jnp.int32, (PC, basis), 0)
    column = lax.broadcasted_iota(jnp.int32, (PC, basis), 1)
    return (column >= block * group) & (column < (block + 1) * group)


def pieces_of(x):
    out = []
    for _ in range(3):
        piece = x.astype(jnp.bfloat16).astype(jnp.float32)
        out.append(piece)
        x = x - piece
    return out


PAIRS = ((0, 0), (0, 1), (1, 0), (0, 2), (1, 1), (2, 0))
DEPTH = 32


def geometry_kernel(near_ref, far_ref, own_ref, table_ref, *refs):
    left_out, right_out, far_out, near_hot, far_hot, side_ref, table_side = refs[-7:]
    frag_dev, near = near_ref.shape
    far = far_ref.shape[1]
    peers, _, _, basis = table_ref.shape
    group = basis // PC
    mask = block_mask(group, basis)
    frags = peers * frag_dev
    lane = lax.broadcasted_iota(jnp.int32, (1, frags), 1)
    ones = jnp.ones((frag_dev, basis), jnp.float32)
    frag_at = lax.axis_index("frag")
    reach = table_side.shape[0] // frag_dev // 2

    def fill(target, first, places, scale, extra, which):
        rows = []
        for place in places:
            parts = pieces_of(place)
            rows += [scale * parts[pair[which]] for pair in PAIRS]
        norm = places[0] * places[0] + places[1] * places[1] + places[2] * places[2] + extra
        sides = [pieces_of(norm), [ones] * 3]
        rows += sides[which] + sides[1 - which]
        rows += [0.0 * ones] * (DEPTH - len(rows))
        for at, row in enumerate(rows):
            for frag in range(frag_dev):
                target[first + frag, at : at + 1, :] = row[frag : frag + 1, :]

    fill(side_ref, 0, [own_ref[axis] for axis in range(3)], -2.0, 1.0, 0)
    for frag in range(frag_dev):
        left_out[frag] = side_ref[frag].astype(jnp.bfloat16)
    for step in range(2 * reach + 1):
        peer = jnp.clip(frag_at + step - reach, 0, peers - 1)
        fill(table_side, step * frag_dev, [table_ref[peer, axis] for axis in range(3)], 1.0, 0.0, 1)

    def one_fragment(frag, carry):
        rows = [own_ref[axis, pl.ds(frag, 1), :] for axis in range(3)]
        for k in range(near):
            other = near_ref[frag, k]
            near_hot[frag, k : k + 1, :] = (lane == other).astype(jnp.float32)
            slot = other - (frag_at - reach) * frag_dev
            right_out[frag, k] = table_side[slot].astype(jnp.bfloat16)
        for m in range(far):
            other = far_ref[frag, m]
            far_hot[frag, m : m + 1, :] = (lane == other).astype(jnp.float32)
            peer, place = other // frag_dev, lax.rem(other, frag_dev)
            total = 1.0
            for axis in range(3):
                inside = jnp.where(mask, table_ref[peer, axis, pl.ds(place, 1), :], 0.0)
                spot = jnp.sum(inside, axis=1, keepdims=True) * (1.0 / group)
                gap = rows[axis] - spot
                total = total + gap * gap
            far_out[frag, m] = lax.rsqrt(total)
        return carry

    lax.fori_loop(0, frag_dev, one_fragment, 0)


def potential_kernel(tiles, charge_ref, left_ref, right_ref, far_part, near_hot, far_hot, *refs):
    overs, chunks = refs[:tiles], refs[tiles : 2 * tiles]
    density_ref, esp_ref, near_charge, far_charge, esp_rows, sems = refs[2 * tiles :]
    tile_at = lax.axis_index("tile")
    share, rows, basis = overs[0].shape
    frag_dev, near = near_hot.shape[:2]
    far = far_hot.shape[1]
    copies = []
    for shift in range(tiles):
        source = lax.rem(tile_at + tiles - shift, tiles)
        target = density_ref.at[pl.ds(source * share, share)]
        copies.append(pltpu.make_async_copy(chunks[shift], target, sems.at[shift]))
    for copy in copies:
        copy.start()
    pick = own_rows(rows, basis, tile_at)
    mask = block_mask(basis // PC, basis)
    charges = charge_ref[...].reshape(-1, basis)
    for hot, gathered in ((near_hot, near_charge), (far_hot, far_charge)):
        every = hot[...].reshape(-1, hot.shape[2])
        picked = jnp.dot(every, charges, precision=lax.Precision.HIGHEST, preferred_element_type=jnp.float32)
        gathered[...] = picked.reshape(gathered.shape)
    for shift in range(tiles):
        target = lax.rem(tile_at + shift, tiles)
        for place in range(share):
            frag = target * share + place
            folded = jnp.zeros((basis, 128), jnp.float32)
            for k in range(near):
                square = lax.dot_general(
                    left_ref[frag],
                    right_ref[frag, k],
                    (((0,), (0,)), ((), ())),
                    preferred_element_type=jnp.float32,
                )
                terms = lax.rsqrt(square) * near_charge[frag, k : k + 1, :]
                for start in range(0, basis, 128):
                    folded = folded + terms[:, start : start + 128]
            blocks = jnp.zeros((PC, basis), jnp.float32)
            for m in range(far):
                inside = jnp.where(mask, far_charge[frag, m : m + 1, :], 0.0)
                blocks = blocks + jnp.sum(inside, axis=1, keepdims=True) * far_part[frag, m]
            potential = jnp.sum(folded.T, axis=0, keepdims=True) + jnp.sum(blocks, axis=0, keepdims=True)
            potential = (0.5 * SCREENING) * potential
            mine = jnp.sum(jnp.where(pick, potential, 0.0), axis=1, keepdims=True)
            esp_rows[shift, place] = overs[shift][place] * (mine + potential)
        copies.append(
            pltpu.make_async_copy(
                esp_rows.at[shift], esp_ref.at[pl.ds(target * share, share)], sems.at[tiles + shift]
            )
        )
        copies[-1].start()
    for copy in copies:
        copy.wait()


def call(kernel, outs, inputs, specs, scratch=(), cost=None, out_spec=VMEM):
    return pl.pallas_call(
        kernel,
        out_shape=outs,
        in_specs=specs,
        out_specs=[out_spec] * len(outs),
        scratch_shapes=list(scratch),
        cost_estimate=cost,
        compiler_params=pltpu.CompilerParams(vmem_limit_bytes=24 * 1024 * 1024),
    )(*inputs)


def shifted(chunks, axis):
    peers = lax.axis_size(axis)
    moved = [chunks[0]]
    for shift in range(1, peers):
        pairs = [(i, (i + shift) % peers) for i in range(peers)]
        moved.append(lax.ppermute(chunks[shift], axis, pairs))
    return moved


def per_device(
    core_fock,
    intersection,
    gamma_tile,
    charge_old,
    embed_old,
    core_pop,
    centres,
    frag_sizes,
    near_list,
    far_list,
):
    frag_dev, rows, basis = core_fock.shape
    tiles, peers = lax.axis_size("tile"), lax.axis_size("frag")
    devices, share = tiles * peers, frag_dev // tiles
    chunk = floats(share, rows, basis)
    places = jnp.transpose(centres, (1, 0, 2))
    inputs = (frag_sizes, charge_old, embed_old, core_pop, places, gamma_tile, intersection, core_fock)
    *sent, facts, copies = call(
        half_fock_kernel,
        [chunk] * (2 * tiles) + [floats(2 * share, basis), floats(peers, *places.shape)],
        [pltpu.with_memory_space_constraint(x, pltpu.HBM) for x in inputs],
        [HBM] * len(inputs),
        [pltpu.SMEM(frag_sizes.shape, jnp.int32)]
        + [pltpu.VMEM(x.shape, jnp.float32) for x in inputs[1:]]
        + [pltpu.SemaphoreType.DMA((len(inputs),))],
    )
    halves = shifted(sent[:tiles], "tile")
    table = lax.all_to_all(copies, "frag", split_axis=0, concat_axis=0, tiled=True)
    overs = shifted(sent[tiles:], "tile")
    pieces = call(
        functools.partial(density_kernel, tiles),
        [chunk] * tiles,
        (facts, *halves, table),
        [VMEM] * (1 + tiles) + [ANY],
        [pltpu.VMEM((share, basis, basis), jnp.float32)],
        pl.CostEstimate(flops=12 * ITERS * share * basis**3, bytes_accessed=0, transcendentals=0),
    )
    (charges,) = call(
        functools.partial(charge_kernel, tiles),
        [floats(devices, share, basis)],
        (facts, *overs, *pieces),
        [VMEM] * (1 + 2 * tiles),
    )
    near, far, frags = near_list.shape[1], far_list.shape[1], peers * frag_dev
    reach = -(-SPAN // frag_dev)
    parts = call(
        geometry_kernel,
        [
            jax.ShapeDtypeStruct((frag_dev, DEPTH, basis), jnp.bfloat16),
            jax.ShapeDtypeStruct((frag_dev, near, DEPTH, basis), jnp.bfloat16),
            floats(frag_dev, far, PC, basis),
            floats(frag_dev, near, frags),
            floats(frag_dev, far, frags),
        ],
        (near_list, far_list, places, table, pieces[0]),
        [SMEM, SMEM, VMEM, VMEM, ANY],
        [
            pltpu.VMEM((frag_dev, DEPTH, basis), jnp.float32),
            pltpu.VMEM(((2 * reach + 1) * frag_dev, DEPTH, basis), jnp.float32),
        ],
        pl.CostEstimate(flops=10**7, bytes_accessed=10**7, transcendentals=0),
    )
    charges, *pieces = lax.optimization_barrier((charges, *pieces))
    charges = lax.all_to_all(charges, ("frag", "tile"), split_axis=0, concat_axis=0, tiled=True)
    moved = shifted(pieces, "tile")
    density, esp_matrix = call(
        functools.partial(potential_kernel, tiles),
        [floats(frag_dev, rows, basis)] * 2,
        (charges, *parts, *sent[tiles:], *moved),
        [VMEM] * (6 + 2 * tiles),
        [
            pltpu.VMEM((frag_dev, near, basis), jnp.float32),
            pltpu.VMEM((frag_dev, far, basis), jnp.float32),
            pltpu.VMEM((tiles, share, rows, basis), jnp.float32),
            pltpu.SemaphoreType.DMA((2 * tiles,)),
        ],
        out_spec=HBM,
    )
    return (density, esp_matrix)


def solution(mesh):
    in_specs = (
        P("frag", "tile", None),
        P("frag", "tile", None),
        P("frag", "tile", None),
        P("frag", None),
        P("frag", None),
        P("frag", None),
        P("frag", None, None),
        P("frag"),
        P("frag", None),
        P("frag", None),
    )
    out_specs = (P("frag", "tile", None), P("frag", "tile", None))
    return jax.shard_map(
        per_device, mesh=mesh, in_specs=in_specs, out_specs=out_specs, check_vma=False
    )
```

time: 84.2 us -> 47.4 us (0.56)
  Pallas kernels: 31.3 us -> 17.3 us
  blocking collectives: 13.5 us -> 0 us
  local copies, waits for them, and re-layouts: 13.1 us -> 0.01 us
  starting transfers between devices: 10.9 us -> 19.3 us
  waiting for transfers between devices: 13.8 us -> 9.76 us
    pallas_call x4 -> x5, Pallas kernels: 31.3 us -> 17.3 us  [call(): pl.pallas_call(kernel, out_shape=outs, in_specs=specs, out_specs=[out_spe...]
    all_to_all x1 -> x0, blocking collectives: 13.5 us -> none  [per_device(): lax.all_to_all(charges, ('frag', 'tile'), split_axis=0, concat_axis=0, ti...]
    unnamed x26 -> x6, local copies, waits for them, and re-layouts: 11.5 us -> 0.01 us
    all_to_all x0 -> x1, starting transfers between devices: none -> 5.8 us  [per_device(): lax.all_to_all(charges, ('frag', 'tile'), split_axis=0, concat_axis=0, ti...]
    all_to_all x0 -> x1, waiting for transfers between devices: none -> 5.05 us  [per_device(): lax.all_to_all(charges, ('frag', 'tile'), split_axis=0, concat_axis=0, ti...]
    all_to_all x1, waiting for transfers between devices: 4.57 us -> 0.01 us  [per_device(): lax.all_to_all(copies, 'frag', split_axis=0, concat_axis=0, tiled=True)]
    ppermute x9, waiting for transfers between devices: 9.18 us -> 4.7 us  [shifted(): moved.append(lax.ppermute(chunks[shift], axis, pairs))]
    all_to_all x1, starting transfers between devices: 3.39 us -> 7.29 us  [per_device(): lax.all_to_all(copies, 'frag', split_axis=0, concat_axis=0, tiled=True)]
  transfers between devices with their start and end apart: 10 -> 11, of which waited for: 7 -> 4; matrix products, arithmetic and copies ran while one was open for 2% -> 0% of each run, Pallas kernels for 15% -> 23%
where the time goes in v2:
time: 47.4 us; the launch traced here: 47.1 us
  starting transfers between devices  19.3 us (41%)
  Pallas kernels  17.3 us (36%)
  waiting for transfers between devices  9.76 us (21%)
  between operations  0.73 us (2%)
    pallas_call x5, Pallas kernels, call(): pl.pallas_call(kernel, out_shape=outs, in_specs=specs, out_specs=[out_spe...  17.3 us
    all_to_all x1, starting transfers between devices, per_device(): lax.all_to_all(copies, 'frag', split_axis=0, concat_axis=0, tiled=True)  7.29 us
    ppermute x9, starting transfers between devices, shifted(): moved.append(lax.ppermute(chunks[shift], axis, pairs))  6.22 us
    all_to_all x1, starting transfers between devices, per_device(): lax.all_to_all(charges, ('frag', 'tile'), split_axis=0, concat_axis=0, ti...  5.8 us
    all_to_all x1, waiting for transfers between devices, per_device(): lax.all_to_all(charges, ('frag', 'tile'), split_axis=0, concat_axis=0, ti...  5.05 us
    ppermute x9, waiting for transfers between devices, shifted(): moved.append(lax.ppermute(chunks[shift], axis, pairs))  4.7 us
  transfers between devices with their start and end apart: 11, of which 4 were waited for; matrix products, arithmetic and copies ran while one was open for 0% of the time, Pallas kernels for 23%

profile of v2, /device:TPU:0, one launch (start us, length us, event | category | flops | bytes accessed | tf_op | source)
XLA Modules:
  0.0 47.1 jit_solution(2117269392608958130)
XLA Ops:
  0.6 2.3 %shard_map.113 = (f32[2,64,256]{2,1,0:T(8,128)S(1)}, f32[2,64,256]{2,1,0:T(8,128)S(1)}, f32[2,64,256]{2,1,0:T(8,128)S(1)}, f32[2,64,256]{2,1,0:T(8,128)S(1)}, f3...) custom-call(s32[8]{0:T(128)} %refs_0_.1, ...), custom_call_target="tpu_custom_call" | custom-call | tf_op jit(solution)/shard_map/pallas_call | solution.py:259
  2.9 7.3 %all-to-all-start = ((f32[8,3,8,256]{3,2,1,0:T(8,128)}), f32[8,3,8,256]{3,2,1,0:T(8,128)S(1)}, u32[]{:S(2)}, u32[]{:S(2)}) async-start(f32[8,3,8,256]{3,2,1,0:T(8,128)} %get-tuple-element.35), calls=%async_computation | async-start | bytes 393216 | tf_op jit(solution)/shard_map/all_to_all | solution.py:307
  10.2 0.0 collective-permute-start.3
  10.2 1.6 %collective-permute-start.4 = (f32[2,64,256]{2,1,0:T(8,128)S(1)}, f32[2,64,256]{2,1,0:T(8,128)S(1)}, u32[]{:S(2)}, u32[]{:S(2)}) collective-permute-start(f32[2,64,256]{2,1,0:T(8,128)S(1)} %get-tuple-element.33), channel_id=1, source_target_pairs={{0,2},{1,3},{2,0},{3,1},{4,6},{5,7},{6,4},{7,5},{8,10},{9,11},{10,... | collective-permute-start | bytes 393224 | tf_op jit(solution)/shard_map/ppermute | solution.py:275
  11.8 1.4 %collective-permute-start.5 = (f32[2,64,256]{2,1,0:T(8,128)S(1)}, f32[2,64,256]{2,1,0:T(8,128)S(1)}, u32[]{:S(2)}, u32[]{:S(2)}) collective-permute-start(f32[2,64,256]{2,1,0:T(8,128)S(1)} %get-tuple-element.34), channel_id=1, source_target_pairs={{0,3},{1,0},{2,1},{3,2},{4,7},{5,4},{6,5},{7,6},{8,11},{9,8},{10,9... | collective-permute-start | bytes 393224 | tf_op jit(solution)/shard_map/ppermute | solution.py:275
  13.2 0.0 collective-permute-start
  13.2 0.6 %collective-permute-start.1 = (f32[2,64,256]{2,1,0:T(8,128)S(1)}, f32[2,64,256]{2,1,0:T(8,128)S(1)}, u32[]{:S(2)}, u32[]{:S(2)}) collective-permute-start(f32[2,64,256]{2,1,0:T(8,128)S(1)} %get-tuple-element.29.refs_2_), channel_id=1, source_target_pairs={{0,2},{1,3},{2,0},{3,1},{4,6},{5,7},{6,4},{7,5},{8,10},{9,11},{10,... | collective-permute-start | bytes 393224 | tf_op jit(solution)/shard_map/ppermute | solution.py:275
  13.8 1.7 %collective-permute-done.3.refs_1_ = f32[2,64,256]{2,1,0:T(8,128)S(1)} collective-permute-done((f32[2,64,256]{2,1,0:T(8,128)S(1)}, f32[2,64,256]{2,1,0:T(8,128)S(1)}, u32[]{:S(2)}, u32[]{:S(2)}) %collective-permute-start.3) | collective-permute-done | bytes 131104 | tf_op jit(solution)/shard_map/ppermute | solution.py:275
  15.4 0.0 collective-permute-start.2
  15.4 1.2 %collective-permute-done.4.refs_2_ = f32[2,64,256]{2,1,0:T(8,128)S(1)} collective-permute-done((f32[2,64,256]{2,1,0:T(8,128)S(1)}, f32[2,64,256]{2,1,0:T(8,128)S(1)}, u32[]{:S(2)}, u32[]{:S(2)}) %collective-permute-start.4) | collective-permute-done | bytes 131104 | tf_op jit(solution)/shard_map/ppermute | solution.py:275
  16.6 1.8 %collective-permute-done.5.refs_3_ = f32[2,64,256]{2,1,0:T(8,128)S(1)} collective-permute-done((f32[2,64,256]{2,1,0:T(8,128)S(1)}, f32[2,64,256]{2,1,0:T(8,128)S(1)}, u32[]{:S(2)}, u32[]{:S(2)}) %collective-permute-start.5) | collective-permute-done | bytes 131104 | tf_op jit(solution)/shard_map/ppermute | solution.py:275
  18.5 0.0 all-to-all-done.refs_4_.table_ref
  18.5 8.5 %shard_map.114 = (f32[2,64,256]{2,1,0:T(8,128)S(1)}, f32[2,64,256]{2,1,0:T(8,128)S(1)}, f32[2,64,256]{2,1,0:T(8,128)S(1)}, f32[2,64,256]{2,1,0:T(8,128)S(1)}) custom-call(f32[4,256]{1,0:T(4,128)S(1)} %get-tuple-element.26.facts_ref, f32[2,64,256]{2,1,0:T(8,128)S(1)} %get-tuple-element.31.refs_0_, f32[2,64,256]{2,1,0:T(8,128)S(1)} %collective-permute-done.3.refs_1_, ...), custom_call_target="tpu_custom_call" | custom-call | flops 4831838208 | tf_op jit(solution)/shard_map/pallas_call | solution.py:259
  26.9 0.0 collective-permute-done.refs_1_
  26.9 0.0 collective-permute-done.1.refs_2_
  26.9 0.0 collective-permute-done.2.refs_3_
  27.0 0.7 %shard_map.115 = f32[32,2,256]{2,1,0:T(2,128)} custom-call(f32[4,256]{1,0:T(4,128)S(1)} %get-tuple-element.26.facts_ref, f32[2,64,256]{2,1,0:T(8,128)S(1)} %get-tuple-element.27.refs_0_, f32[2,64,256]{2,1,0:T(8,128)S(1)} %collective-permute-done.refs_1_, f32[2,64,256]{2,1,0:T(8,128)S(1)} %collective-permute-done.1.refs_2_, ...), custom_call_target="tpu_custom_call" | custom-call | tf_op jit(solution)/shard_map/pallas_call | solution.py:259
  27.7 0.0 copy-start
  27.7 0.0 copy-start.1
  27.7 0.0 copy-start.2
  27.7 1.1 %collective-permute-start.6 = (f32[2,64,256]{2,1,0:T(8,128)S(1)}, f32[2,64,256]{2,1,0:T(8,128)S(1)}, u32[]{:S(2)}, u32[]{:S(2)}) collective-permute-start(f32[2,64,256]{2,1,0:T(8,128)S(1)} %get-tuple-element.47.refs_5_), channel_id=1, source_target_pairs={{0,1},{1,2},{2,3},{3,0},{4,5},{5,6},{6,7},{7,4},{8,9},{9,10},{10,1... | collective-permute-start | bytes 393224 | tf_op jit(solution)/shard_map/ppermute | solution.py:275
  28.8 1.5 %collective-permute-start.7 = (f32[2,64,256]{2,1,0:T(8,128)S(1)}, f32[2,64,256]{2,1,0:T(8,128)S(1)}, u32[]{:S(2)}, u32[]{:S(2)}) collective-permute-start(f32[2,64,256]{2,1,0:T(8,128)S(1)} %get-tuple-element.48.refs_6_), channel_id=1, source_target_pairs={{0,2},{1,3},{2,0},{3,1},{4,6},{5,7},{6,4},{7,5},{8,10},{9,11},{10,... | collective-permute-start | bytes 393224 | tf_op jit(solution)/shard_map/ppermute | solution.py:275
  30.3 0.1 collective-permute-start.8
  30.4 5.8 %all-to-all-start.1 = ((f32[32,2,256]{2,1,0:T(2,128)}), f32[32,2,256]{2,1,0:T(2,128)S(1)}, u32[]{:S(2)}, u32[]{:S(2)}) async-start(f32[32,2,256]{2,1,0:T(2,128)} %shard_map.115), calls=%async_computation.1 | async-start | bytes 131072 | tf_op jit(solution)/shard_map/all_to_all | solution.py:343
  36.2 0.0 copy-done
  36.2 0.0 copy-done.1
  36.2 0.0 copy-done.2
  36.2 2.3 %shard_map.116 = (bf16[8,32,256]{2,1,0:T(8,128)(2,1)S(1)}, bf16[8,8,32,256]{3,2,1,0:T(8,128)(2,1)S(1)}, f32[8,8,8,256]{3,2,1,0:T(8,128)S(1)}, f32[8,8,64]{2,1,0:T(8,128)S(1)}, f32[8,8,64]{2,1,0:T(8,128)S(1)}) custom-call(s32[8,8]{1,0:T(8,128)S(1)} %copy-done.1, s32[8,8]{1,0:T(8,128)S(1)} %copy-done.2, f32[3,8,256]{2,1,0:T(8,128)S(1)} %bitcast.2, ...), custom_call_target="tpu_custom_call" | custom-call | flops 10000000 | bytes 10000000 | tf_op jit(solution)/shard_map/pallas_call | solution.py:259
  38.5 5.1 %all-to-all-done.1.charge_ref = f32[32,2,256]{2,1,0:T(2,128)S(1)} async-done(((f32[32,2,256]{2,1,0:T(2,128)}), f32[32,2,256]{2,1,0:T(2,128)S(1)}, u32[]{:S(2)}, u32[]{:S(2)}) %all-to-all-start.1) | async-done | bytes 65568 | tf_op jit(solution)/shard_map/all_to_all | solution.py:343
  43.6 0.0 collective-permute-done.6.refs_5_
  43.6 0.0 collective-permute-done.7.refs_6_
  43.6 0.0 collective-permute-done.8.refs_7_
  43.6 3.5 %shard_map.117 = (f32[8,64,256]{2,1,0:T(8,128)}, f32[8,64,256]{2,1,0:T(8,128)}) custom-call(f32[32,2,256]{2,1,0:T(2,128)S(1)} %all-to-all-done.1.charge_ref, bf16[8,32,256]{2,1,0:T(8,128)(2,1)S(1)} %get-tuple-element.41.left_ref, bf16[8,8,32,256]{3,2,1,0:T(8,128)(2,1)S(1)} %get-tuple-element.42.right_ref, f32[8,8,8,256]{3,2,1,0:T(8,128)S(1)} %get-tuple-element.43.far_part, ...), custom_call_target="tpu_custom_call" | custom-call | tf_op jit(solution)/shard_map/pallas_call | solution.py:259
Async XLA Ops:
  2.9 15.5 %all-to-all-start = ((f32[8,3,8,256]{3,2,1,0:T(8,128)}), f32[8,3,8,256]{3,2,1,0:T(8,128)S(1)}, u32[]{:S(2)}, u32[]{:S(2)}) async-start(f32[8,3,8,256]{3,2,1,0:T(8,128)} %get-tuple-element.35), calls=%async_computation | async-start | bytes 393216 | tf_op jit(solution)/shard_map/all_to_all | solution.py:307
  10.2 5.2 %collective-permute-start.3 = (f32[2,64,256]{2,1,0:T(8,128)S(1)}, f32[2,64,256]{2,1,0:T(8,128)S(1)}, u32[]{:S(2)}, u32[]{:S(2)}) collective-permute-start(f32[2,64,256]{2,1,0:T(8,128)S(1)} %get-tuple-element.32), channel_id=1, source_target_pairs={{0,1},{1,2},{2,3},{3,0},{4,5},{5,6},{6,7},{7,4},{8,9},{9,10},{10,1... | collective-permute-start | bytes 393224 | tf_op jit(solution)/shard_map/ppermute | solution.py:275
  10.2 6.4 %collective-permute-start.4 = (f32[2,64,256]{2,1,0:T(8,128)S(1)}, f32[2,64,256]{2,1,0:T(8,128)S(1)}, u32[]{:S(2)}, u32[]{:S(2)}) collective-permute-start(f32[2,64,256]{2,1,0:T(8,128)S(1)} %get-tuple-element.33), channel_id=1, source_target_pairs={{0,2},{1,3},{2,0},{3,1},{4,6},{5,7},{6,4},{7,5},{8,10},{9,11},{10,... | collective-permute-start | bytes 393224 | tf_op jit(solution)/shard_map/ppermute | solution.py:275
  11.8 6.6 %collective-permute-start.5 = (f32[2,64,256]{2,1,0:T(8,128)S(1)}, f32[2,64,256]{2,1,0:T(8,128)S(1)}, u32[]{:S(2)}, u32[]{:S(2)}) collective-permute-start(f32[2,64,256]{2,1,0:T(8,128)S(1)} %get-tuple-element.34), channel_id=1, source_target_pairs={{0,3},{1,0},{2,1},{3,2},{4,7},{5,4},{6,5},{7,6},{8,11},{9,8},{10,9... | collective-permute-start | bytes 393224 | tf_op jit(solution)/shard_map/ppermute | solution.py:275
  13.2 13.7 %collective-permute-start = (f32[2,64,256]{2,1,0:T(8,128)S(1)}, f32[2,64,256]{2,1,0:T(8,128)S(1)}, u32[]{:S(2)}, u32[]{:S(2)}) collective-permute-start(f32[2,64,256]{2,1,0:T(8,128)S(1)} %get-tuple-element.28.refs_1_), channel_id=1, source_target_pairs={{0,1},{1,2},{2,3},{3,0},{4,5},{5,6},{6,7},{7,4},{8,9},{9,10},{10,1... | collective-permute-start | bytes 393224 | tf_op jit(solution)/shard_map/ppermute | solution.py:275
  13.2 13.7 %collective-permute-start.1 = (f32[2,64,256]{2,1,0:T(8,128)S(1)}, f32[2,64,256]{2,1,0:T(8,128)S(1)}, u32[]{:S(2)}, u32[]{:S(2)}) collective-permute-start(f32[2,64,256]{2,1,0:T(8,128)S(1)} %get-tuple-element.29.refs_2_), channel_id=1, source_target_pairs={{0,2},{1,3},{2,0},{3,1},{4,6},{5,7},{6,4},{7,5},{8,10},{9,11},{10,... | collective-permute-start | bytes 393224 | tf_op jit(solution)/shard_map/ppermute | solution.py:275
  15.4 11.5 %collective-permute-start.2 = (f32[2,64,256]{2,1,0:T(8,128)S(1)}, f32[2,64,256]{2,1,0:T(8,128)S(1)}, u32[]{:S(2)}, u32[]{:S(2)}) collective-permute-start(f32[2,64,256]{2,1,0:T(8,128)S(1)} %get-tuple-element.30.refs_3_), channel_id=1, source_target_pairs={{0,3},{1,0},{2,1},{3,2},{4,7},{5,4},{6,5},{7,6},{8,11},{9,8},{10,9... | collective-permute-start | bytes 393224 | tf_op jit(solution)/shard_map/ppermute | solution.py:275
  27.7 8.5 %copy-start = (f32[8,3,256]{2,0,1:T(8,128)S(1)}, f32[8,3,256]{2,0,1:T(8,128)}, u32[]{:S(2)}) copy-start(f32[8,3,256]{2,0,1:T(8,128)} %param.16) | copy-start | bytes 73732
  27.7 8.5 %copy-start.1 = (s32[8,8]{1,0:T(8,128)S(1)}, s32[8,8]{1,0:T(8,128)}, u32[]{:S(2)}) copy-start(s32[8,8]{1,0:T(8,128)} %near_ref.1) | copy-start | bytes 772
  27.7 8.5 %copy-start.2 = (s32[8,8]{1,0:T(8,128)S(1)}, s32[8,8]{1,0:T(8,128)}, u32[]{:S(2)}) copy-start(s32[8,8]{1,0:T(8,128)} %far_ref.1) | copy-start | bytes 772
  27.7 15.9 %collective-permute-start.6 = (f32[2,64,256]{2,1,0:T(8,128)S(1)}, f32[2,64,256]{2,1,0:T(8,128)S(1)}, u32[]{:S(2)}, u32[]{:S(2)}) collective-permute-start(f32[2,64,256]{2,1,0:T(8,128)S(1)} %get-tuple-element.47.refs_5_), channel_id=1, source_target_pairs={{0,1},{1,2},{2,3},{3,0},{4,5},{5,6},{6,7},{7,4},{8,9},{9,10},{10,1... | collective-permute-start | bytes 393224 | tf_op jit(solution)/shard_map/ppermute | solution.py:275
  28.8 14.8 %collective-permute-start.7 = (f32[2,64,256]{2,1,0:T(8,128)S(1)}, f32[2,64,256]{2,1,0:T(8,128)S(1)}, u32[]{:S(2)}, u32[]{:S(2)}) collective-permute-start(f32[2,64,256]{2,1,0:T(8,128)S(1)} %get-tuple-element.48.refs_6_), channel_id=1, source_target_pairs={{0,2},{1,3},{2,0},{3,1},{4,6},{5,7},{6,4},{7,5},{8,10},{9,11},{10,... | collective-permute-start | bytes 393224 | tf_op jit(solution)/shard_map/ppermute | solution.py:275
  30.3 13.3 %collective-permute-start.8 = (f32[2,64,256]{2,1,0:T(8,128)S(1)}, f32[2,64,256]{2,1,0:T(8,128)S(1)}, u32[]{:S(2)}, u32[]{:S(2)}) collective-permute-start(f32[2,64,256]{2,1,0:T(8,128)S(1)} %get-tuple-element.49.refs_7_), channel_id=1, source_target_pairs={{0,3},{1,0},{2,1},{3,2},{4,7},{5,4},{6,5},{7,6},{8,11},{9,8},{10,9... | collective-permute-start | bytes 393224 | tf_op jit(solution)/shard_map/ppermute | solution.py:275
  30.4 13.2 %all-to-all-start.1 = ((f32[32,2,256]{2,1,0:T(2,128)}), f32[32,2,256]{2,1,0:T(2,128)S(1)}, u32[]{:S(2)}, u32[]{:S(2)}) async-start(f32[32,2,256]{2,1,0:T(2,128)} %shard_map.115), calls=%async_computation.1 | async-start | bytes 131072 | tf_op jit(solution)/shard_map/all_to_all | solution.py:343

commit v3 on v2

v3 whole, which is shorter than its diff:
```python
import functools

import jax
import jax.numpy as jnp
from jax import lax
from jax.experimental import pallas as pl
from jax.experimental.pallas import tpu as pltpu
from jax.sharding import PartitionSpec as P

PC = 8
ITERS = 12
SCREENING = 0.25
SPAN = 8
LANES = 128
CHUNK = 128
VMEM = pl.BlockSpec(memory_space=pltpu.VMEM)
SMEM = pl.BlockSpec(memory_space=pltpu.SMEM)
HBM = pl.BlockSpec(memory_space=pltpu.HBM)
ANY = pl.BlockSpec(memory_space=pl.ANY)


def floats(*shape):
    return jax.ShapeDtypeStruct(shape, jnp.float32)


def block_mask(basis):
    group = basis // PC
    block = lax.broadcasted_iota(jnp.int32, (PC, basis), 0)
    column = lax.broadcasted_iota(jnp.int32, (PC, basis), 1)
    return (column >= block * group) & (column < (block + 1) * group)


def block_lanes(at):
    block = lax.broadcasted_iota(jnp.int32, (PC, LANES), 0)
    lane = lax.broadcasted_iota(jnp.int32, (PC, LANES), 1)
    return lane == block + at * PC


def block_row(rows, first):
    mask = block_mask(rows[0].shape[1])
    total = jnp.zeros((PC, LANES), jnp.float32)
    for at, row in enumerate(rows):
        sums = jnp.sum(jnp.where(mask, row, 0.0), axis=1, keepdims=True)
        total = total + jnp.where(block_lanes(first + at), sums, 0.0)
    return jnp.sum(total, axis=0, keepdims=True)


def own_rows(rows, basis, first):
    row = lax.broadcasted_iota(jnp.int32, (rows, basis), 0)
    column = lax.broadcasted_iota(jnp.int32, (rows, basis), 1)
    return column == row + first


def seat(tiles):
    places = tiles // 2
    tile_at = lax.axis_index("tile")
    return tile_at // places, lax.rem(tile_at, places), places


def partner(shift, tiles, sign=1):
    half, place, places = seat(tiles)
    other = half if shift < places else 1 - half
    return other * places + lax.rem(place + places + sign * (shift % places), places)


def swapped(half, x):
    middle = x.shape[-1] // 2
    left, right = x[..., :middle], x[..., middle:]
    return jnp.where(half == 0, left, right), jnp.where(half == 0, right, left)


def half_fock_kernel(tiles, *refs):
    inputs, outs, buffers, sems = refs[:8], refs[8:-9], refs[-9:-1], refs[-1]
    copies = [
        pltpu.make_async_copy(source, buffer, sems.at[at])
        for at, (source, buffer) in enumerate(zip(inputs, buffers))
    ]
    for copy in copies:
        copy.start()
    for copy in copies:
        copy.wait()
    sizes_ref, charge_ref, embed_ref, pop_ref, place_ref, gamma_ref, over_ref, core_ref = buffers
    half, place_at, places = seat(tiles)
    frag_dev, rows, basis = core_ref.shape
    share, middle = frag_dev // tiles, basis // 2
    pick = own_rows(rows, basis, lax.axis_index("tile") * rows)
    pick_half = own_rows(rows, middle, place_at * rows)
    row = lax.broadcasted_iota(jnp.int32, (rows, middle), 0) + lax.axis_index("tile") * rows
    column = lax.broadcasted_iota(jnp.int32, (rows, middle), 1)
    mine, others = column + half * middle, column + (1 - half) * middle
    lane = lax.broadcasted_iota(jnp.int32, (1, basis), 1)
    for shift in range(tiles):
        target = partner(shift, tiles)
        for spot in range(share):
            frag = target * share + spot
            size = sizes_ref[frag]
            terms = gamma_ref[frag] * charge_ref[pl.ds(frag, 1), :]
            terms = terms + jnp.where(pick, embed_ref[pl.ds(frag, 1), :], 0.0)
            field = jnp.sum(terms, axis=1, keepdims=True)
            core, core_far = swapped(half, core_ref[frag])
            over, over_far = swapped(half, over_ref[frag])
            inside = (row < size) & (mine < size)
            over = jnp.where(inside, over, 0.0)
            near_part = jnp.where(inside, 0.5 * core, 0.0) + over * (0.5 * field)
            out = outs[shift]
            if shift < places:
                inside = (row < size) & (others < size)
                over_far = jnp.where(inside, over_far, 0.0)
                out[0, spot, :, :middle] = near_part
                out[0, spot, :, middle:] = jnp.where(inside, core_far, 0.0) + over_far * (0.5 * field)
                out[1, spot, :, :middle] = over
                out[1, spot, :, middle:] = over_far
            else:
                out[spot, :rows] = near_part
                out[spot, rows : 2 * rows] = over
                field_row = jnp.sum(jnp.where(pick_half, field, 0.0), axis=0, keepdims=True)
                out[spot, 2 * rows :] = jnp.broadcast_to(field_row, (out.shape[1] - 2 * rows, middle))
            if shift == 0:
                facts = outs[-1]
                idle = swapped(half, (lane >= size).astype(jnp.float32))
                facts[spot : spot + 1, :middle] = idle[0]
                facts[spot : spot + 1, middle:] = idle[1]
                facts[share + spot : share + spot + 1, :] = pop_ref[pl.ds(frag, 1), :]
                spots = [place_ref[axis, pl.ds(frag, 1), :] for axis in range(3)]
                means = block_row(spots, 0) * (PC / basis)
                facts[2 * share + spot : 2 * share + spot + 1, :LANES] = means


def split(x):
    high = x.astype(jnp.bfloat16)
    low = (x - high.astype(jnp.float32)).astype(jnp.bfloat16)
    return high, low


def product(left, right):
    lh, ll = left
    rh, rl = right
    dot = functools.partial(jnp.dot, preferred_element_type=jnp.float32)
    return dot(lh, rh) + (dot(lh, rl) + dot(ll, rh))


def density_kernel(tiles, facts_ref, *refs):
    places = tiles // 2
    near_parts, far_parts = refs[:places], refs[places:tiles]
    chunks, charge_ref = refs[tiles : 2 * tiles], refs[2 * tiles]
    x_ref, s_ref = refs[2 * tiles + 1 :]
    half, place_at, _ = seat(tiles)
    _, share, rows, basis = near_parts[0].shape
    middle = basis // 2
    for shift in range(places):
        source = lax.rem(place_at + places - shift, places) * rows
        span = pl.ds(pl.multiple_of(source, rows), rows)
        far_span = pl.ds(pl.multiple_of(source + middle, rows), rows)
        for spot in range(share):
            x_ref[spot, span, :] = near_parts[shift][0, spot]
            s_ref[spot, span, :] = near_parts[shift][1, spot]
            x_ref[spot, far_span, middle:] = far_parts[shift][spot, :rows]
            s_ref[spot, far_span, middle:] = far_parts[shift][spot, rows : 2 * rows]
    row = lax.broadcasted_iota(jnp.int32, (basis, basis), 0)
    column = lax.broadcasted_iota(jnp.int32, (basis, basis), 1)
    near, far = slice(0, middle), slice(middle, basis)
    for spot in range(share):
        field = far_parts[0][spot, 2 * rows : 2 * rows + 1, :]
        for part in far_parts[1:]:
            field = field + part[spot, 2 * rows : 2 * rows + 1, :]
        corner, last = x_ref[spot, near, near], x_ref[spot, far, far]
        side = x_ref[spot, near, far] + s_ref[spot, near, far] * (0.5 * field)
        corner, last = corner + corner.T, last + last.T
        total = corner * corner + last * last + 2.0 * (side * side)
        scale = 1.0 / jnp.sqrt(jnp.sum(total, keepdims=True) + 1e-06)
        idle = jnp.where(row == column, facts_ref[spot : spot + 1, :], 0.0)
        x_ref[spot, near, near] = corner * scale + idle[near, near]
        x_ref[spot, near, far] = side * scale
        x_ref[spot, far, near] = side.T * scale
        x_ref[spot, far, far] = last * scale + idle[far, far]

    chunk = min(CHUNK, basis)
    spans = [(spot, slice(at, at + chunk)) for spot in range(share) for at in range(0, basis, chunk)]
    for _ in range(ITERS):
        estimates = [x_ref[spot] for spot in range(share)]
        parts = [split(x) for x in estimates]
        squares = []
        for spot, span in spans:
            left = [part[span] for part in parts[spot]]
            squares.append(split(0.5 * product(left, parts[spot])))
        for square, (spot, span) in zip(squares, spans):
            x_ref[spot, span] = 1.5 * estimates[spot][span] - product(square, parts[spot])

    for spot in range(share):
        density = jnp.where(row == column, 0.5, 0.0) - 0.5 * x_ref[spot]
        x_ref[spot] = density
        side = density[near, far] * s_ref[spot, near, far]
        corner = density[near, near] * s_ref[spot, near, near] + side.T
        last = density[far, far] * s_ref[spot, far, far] + side
        sums = [jnp.sum(block, axis=0, keepdims=True) for block in (corner, last)]
        charge = jnp.concatenate(swapped(half, jnp.concatenate(sums, axis=1)), axis=1)
        charge = charge - facts_ref[share + spot : share + spot + 1, :]
        blocks = block_row([charge], 3) + facts_ref[2 * share + spot : 2 * share + spot + 1, :LANES]
        whole = jnp.concatenate([charge, blocks], axis=1)
        charge_ref[:, spot : spot + 1, :] = jnp.broadcast_to(whole[None], (charge_ref.shape[0],) + whole.shape)
    for shift in range(tiles):
        first = partner(shift, tiles) % places * rows + (0 if shift < places else middle)
        span = pl.ds(pl.multiple_of(first, rows), rows)
        for spot in range(share):
            left, right = swapped(half, x_ref[spot, span, :])
            chunks[shift][spot, :, :middle] = left
            chunks[shift][spot, :, middle:] = right


def pieces_of(x):
    out = []
    for _ in range(3):
        piece = x.astype(jnp.bfloat16).astype(jnp.float32)
        out.append(piece)
        x = x - piece
    return out


PAIRS = ((0, 0), (0, 1), (1, 0), (0, 2), (1, 1), (2, 0))
DEPTH = 32


def geometry_kernel(around, near_ref, far_ref, own_ref, *refs):
    sources = refs[:around]
    left_out, right_out, near_hot, far_hot, side_ref, table_side = refs[-6:]
    frag_dev, near = near_ref.shape
    far = far_ref.shape[1]
    basis = own_ref.shape[2]
    lane = lax.broadcasted_iota(jnp.int32, (1, near_hot.shape[2]), 1)
    ones = jnp.ones((frag_dev, basis), jnp.float32)
    first_frag = (lax.axis_index("frag") - around // 2) * frag_dev

    def fill(target, first, place_ref, scale, extra, which):
        places = [place_ref[axis] for axis in range(3)]
        rows = []
        for place in places:
            parts = pieces_of(place)
            rows += [scale * parts[pair[which]] for pair in PAIRS]
        norm = places[0] * places[0] + places[1] * places[1] + places[2] * places[2] + extra
        sides = [pieces_of(norm), [ones] * 3]
        rows += sides[which] + sides[1 - which]
        rows += [0.0 * ones] * (DEPTH - len(rows))
        for at, row in enumerate(rows):
            for frag in range(frag_dev):
                target[first + frag, at : at + 1, :] = row[frag : frag + 1, :]

    fill(side_ref, 0, own_ref, -2.0, 1.0, 0)
    left_out[...] = side_ref[...].astype(jnp.bfloat16)
    for step in range(around):
        fill(table_side, step * frag_dev, sources[step], 1.0, 0.0, 1)
    for frag in range(frag_dev):
        for k in range(near):
            other = near_ref[frag, k]
            near_hot[frag, k : k + 1, :] = (lane == other).astype(jnp.float32)
            right_out[frag, k] = table_side[other - first_frag].astype(jnp.bfloat16)
        for m in range(far):
            far_hot[frag, m : m + 1, :] = (lane == far_ref[frag, m]).astype(jnp.float32)


def gather_kernel(tiles, *refs):
    chunks, density_ref, sems = refs[:tiles], refs[tiles], refs[tiles + 1]
    share = chunks[0].shape[0]
    copies = []
    for shift in range(tiles):
        target = density_ref.at[pl.ds(partner(shift, tiles, -1) * share, share)]
        copies.append(pltpu.make_async_copy(chunks[shift], target, sems.at[shift]))
        copies[-1].start()
    for copy in copies:
        copy.wait()


def potential_kernel(tiles, charge_ref, own_ref, left_ref, right_ref, near_hot, far_hot, over_ref, *refs):
    esp_ref, near_charge, far_block, esp_rows, sems = refs[1:]
    frag_dev, rows, basis = over_ref.shape
    share = frag_dev // tiles
    near, far = near_hot.shape[1], far_hot.shape[1]
    copies = []
    pick = own_rows(rows, basis, lax.axis_index("tile") * rows)
    table = charge_ref[...].reshape(-1, basis + LANES)
    for hot, gathered, part in (
        (near_hot, near_charge, table[:, :basis]),
        (far_hot, far_block, table[:, basis:]),
    ):
        every = hot[...].reshape(-1, hot.shape[2])
        picked = jnp.dot(every, part, precision=lax.Precision.HIGHEST, preferred_element_type=jnp.float32)
        gathered[...] = picked.reshape(gathered.shape)
    quantities = [block_lanes(at) for at in range(4)]
    for part in range(tiles):
        for frag in range(part * share, (part + 1) * share):
            folded = jnp.zeros((basis, 128), jnp.float32)
            for k in range(near):
                square = lax.dot_general(
                    left_ref[frag],
                    right_ref[frag, k],
                    (((0,), (0,)), ((), ())),
                    preferred_element_type=jnp.float32,
                )
                terms = lax.rsqrt(square) * near_charge[frag, k : k + 1, :]
                for start in range(0, basis, 128):
                    folded = folded + terms[:, start : start + 128]
            blocks = jnp.zeros((PC, basis), jnp.float32)
            spots = [own_ref[axis, frag : frag + 1, :] for axis in range(3)]
            for m in range(far):
                row = far_block[frag, m : m + 1, :]
                x, y, z, charge = [
                    jnp.sum(jnp.where(lanes, row, 0.0), axis=1, keepdims=True) for lanes in quantities
                ]
                total = (spots[0] - x) ** 2 + (spots[1] - y) ** 2 + (spots[2] - z) ** 2
                blocks = blocks + charge * lax.rsqrt(total + 1.0)
            potential = jnp.sum(folded.T, axis=0, keepdims=True) + jnp.sum(blocks, axis=0, keepdims=True)
            potential = (0.5 * SCREENING) * potential
            mine = jnp.sum(jnp.where(pick, potential, 0.0), axis=1, keepdims=True)
            esp_rows[frag] = over_ref[frag] * (mine + potential)
        span = pl.ds(part * share, share)
        copies.append(pltpu.make_async_copy(esp_rows.at[span], esp_ref.at[span], sems.at[part]))
        copies[-1].start()
    for copy in copies:
        copy.wait()


def call(kernel, outs, inputs, specs, scratch=(), cost=None, out_spec=VMEM):
    return pl.pallas_call(
        kernel,
        out_shape=outs,
        in_specs=specs,
        out_specs=[out_spec] * len(outs),
        scratch_shapes=list(scratch),
        cost_estimate=cost,
        compiler_params=pltpu.CompilerParams(vmem_limit_bytes=24 * 1024 * 1024),
    )(*inputs)


def exchanged(chunks):
    tiles = lax.axis_size("tile")
    places = tiles // 2
    moved = [chunks[0]]
    for shift in range(1, tiles):
        pairs = []
        for tile in range(tiles):
            half = tile // places if shift < places else 1 - tile // places
            pairs.append((tile, half * places + (tile + shift) % places))
        moved.append(lax.ppermute(chunks[shift], "tile", pairs))
    return moved


def neighbours(x, axis, reach):
    peers = lax.axis_size(axis)
    found = []
    for step in range(-reach, reach + 1):
        pairs = [(i, i - step) for i in range(peers) if 0 <= i - step < peers]
        found.append(x if step == 0 else lax.ppermute(x, axis, pairs))
    return found


def per_device(
    core_fock,
    intersection,
    gamma_tile,
    charge_old,
    embed_old,
    core_pop,
    centres,
    frag_sizes,
    near_list,
    far_list,
):
    frag_dev, rows, basis = core_fock.shape
    tiles, peers = lax.axis_size("tile"), lax.axis_size("frag")
    devices, share = tiles * peers, frag_dev // tiles
    chunk = floats(share, rows, basis)
    places = jnp.transpose(centres, (1, 0, 2))
    inputs = (frag_sizes, charge_old, embed_old, core_pop, places, gamma_tile, intersection, core_fock)
    near_part = floats(2, share, rows, basis)
    far_part = floats(share, 2 * rows + 8, basis // 2)
    *sent, facts = call(
        functools.partial(half_fock_kernel, tiles),
        [near_part] * (tiles // 2) + [far_part] * (tiles // 2) + [floats(3 * share, basis)],
        [pltpu.with_memory_space_constraint(x, pltpu.HBM) for x in inputs],
        [HBM] * len(inputs),
        [pltpu.SMEM(frag_sizes.shape, jnp.int32)]
        + [pltpu.VMEM(x.shape, jnp.float32) for x in inputs[1:]]
        + [pltpu.SemaphoreType.DMA((len(inputs),))],
    )
    sent = exchanged(sent)
    sources = neighbours(places, "frag", -(-SPAN // frag_dev))
    sent, sources = lax.optimization_barrier((sent, sources))
    *pieces, charges = call(
        functools.partial(density_kernel, tiles),
        [chunk] * tiles + [floats(devices, share, basis + LANES)],
        (facts, *sent),
        [VMEM] * (1 + tiles),
        [pltpu.VMEM((share, basis, basis), jnp.float32)] * 2,
        pl.CostEstimate(flops=12 * ITERS * share * basis**3, bytes_accessed=0, transcendentals=0),
    )
    near, far, frags = near_list.shape[1], far_list.shape[1], peers * frag_dev
    parts = call(
        functools.partial(geometry_kernel, len(sources)),
        [
            jax.ShapeDtypeStruct((frag_dev, DEPTH, basis), jnp.bfloat16),
            jax.ShapeDtypeStruct((frag_dev, near, DEPTH, basis), jnp.bfloat16),
            floats(frag_dev, near, frags),
            floats(frag_dev, far, frags),
        ],
        (near_list, far_list, places, *sources, pieces[0]),
        [SMEM, SMEM] + [VMEM] * (1 + len(sources)) + [ANY],
        [
            pltpu.VMEM((frag_dev, DEPTH, basis), jnp.float32),
            pltpu.VMEM((len(sources) * frag_dev, DEPTH, basis), jnp.float32),
        ],
        pl.CostEstimate(flops=10**9, bytes_accessed=10**7, transcendentals=0),
    )
    moved = exchanged(pieces)
    charges = lax.all_to_all(charges, ("frag", "tile"), split_axis=0, concat_axis=0, tiled=True)
    (density,) = call(
        functools.partial(gather_kernel, tiles),
        [floats(frag_dev, rows, basis)],
        moved,
        [VMEM] * tiles,
        [pltpu.SemaphoreType.DMA((tiles,))],
        pl.CostEstimate(flops=10**11, bytes_accessed=10**7, transcendentals=0),
        HBM,
    )
    (esp_matrix,) = call(
        functools.partial(potential_kernel, tiles),
        [floats(frag_dev, rows, basis)],
        (charges, places, *parts, intersection, pltpu.with_memory_space_constraint(density, pltpu.HBM)),
        [VMEM] * 7 + [HBM],
        [
            pltpu.VMEM((frag_dev, near, basis), jnp.float32),
            pltpu.VMEM((frag_dev, far, LANES), jnp.float32),
            pltpu.VMEM((frag_dev, rows, basis), jnp.float32),
            pltpu.SemaphoreType.DMA((tiles,)),
        ],
        out_spec=HBM,
    )
    return (density, esp_matrix)


def solution(mesh):
    in_specs = (
        P("frag", "tile", None),
        P("frag", "tile", None),
        P("frag", "tile", None),
        P("frag", None),
        P("frag", None),
        P("frag", None),
        P("frag", None, None),
        P("frag"),
        P("frag", None),
        P("frag", None),
    )
    out_specs = (P("frag", "tile", None), P("frag", "tile", None))
    return jax.shard_map(
        per_device, mesh=mesh, in_specs=in_specs, out_specs=out_specs, check_vma=False
    )
```

time: 47.4 us -> 41.3 us (0.87)
  Pallas kernels: 17.3 us -> 14.5 us
  waiting for transfers between devices: 9.76 us -> 7.29 us
  starting transfers between devices: 19.3 us -> 18.6 us
    all_to_all x1 -> x0, starting transfers between devices: 7.29 us -> none  [per_device(): lax.all_to_all(copies, 'frag', split_axis=0, concat_axis=0, tiled=True)]
    ppermute x9 -> x8, starting transfers between devices: 6.22 us -> 10.9 us  [the longest x2 5.83 us: neighbours(): found.append(x if step == 0 else lax.ppermute(x, axis, pairs))]
    ppermute x9 -> x8, waiting for transfers between devices: 4.7 us -> 1.51 us  [the longest x2 1.49 us: neighbours(): found.append(x if step == 0 else lax.ppermute(x, axis, pairs))]
    pallas_call x5, Pallas kernels: 17.3 us -> 14.5 us  [call(): pl.pallas_call(kernel, out_shape=outs, in_specs=specs, out_specs=[out_spe...]
    all_to_all x1, starting transfers between devices: 5.8 us -> 7.7 us  [per_device(): lax.all_to_all(charges, ('frag', 'tile'), split_axis=0, concat_axis=0, ti...]
    all_to_all x1, waiting for transfers between devices: 5.05 us -> 5.78 us  [per_device(): lax.all_to_all(charges, ('frag', 'tile'), split_axis=0, concat_axis=0, ti...]
  transfers between devices with their start and end apart: 11 -> 9, of which waited for: 4 -> 2; matrix products, arithmetic and copies ran while one was open for 0% -> 0% of each run, Pallas kernels for 23% -> 5%
where the time goes in v3:
time: 41.3 us; the launch traced here: 41.1 us
  starting transfers between devices  18.6 us (45%)
  Pallas kernels  14.5 us (35%)
  waiting for transfers between devices  7.29 us (18%)
  between operations  0.75 us (2%)
    pallas_call x5, Pallas kernels, call(): pl.pallas_call(kernel, out_shape=outs, in_specs=specs, out_specs=[out_spe...  14.5 us
    all_to_all x1, starting transfers between devices, per_device(): lax.all_to_all(charges, ('frag', 'tile'), split_axis=0, concat_axis=0, ti...  7.7 us
    ppermute x2, starting transfers between devices, neighbours(): found.append(x if step == 0 else lax.ppermute(x, axis, pairs))  5.83 us
    all_to_all x1, waiting for transfers between devices, per_device(): lax.all_to_all(charges, ('frag', 'tile'), split_axis=0, concat_axis=0, ti...  5.78 us
    ppermute x6, starting transfers between devices, exchanged(): moved.append(lax.ppermute(chunks[shift], 'tile', pairs))  5.03 us
    ppermute x2, waiting for transfers between devices, neighbours(): found.append(x if step == 0 else lax.ppermute(x, axis, pairs))  1.49 us
  transfers between devices with their start and end apart: 9, of which 2 were waited for; matrix products, arithmetic and copies ran while one was open for 0% of the time, Pallas kernels for 5%

profile of v3, /device:TPU:0, one launch (start us, length us, event | category | flops | bytes accessed | tf_op | source)
XLA Modules:
  0.0 41.1 jit_solution(1013825061255173709)
XLA Ops:
  0.6 0.0 copy-start.1
  0.6 1.7 %shard_map.113 = (f32[2,2,64,256]{3,2,1,0:T(8,128)S(1)}, f32[2,2,64,256]{3,2,1,0:T(8,128)S(1)}, f32[2,136,128]{2,1,0:T(8,128)S(1)}, f32[2,136,128]{2,1,0:T(8,128)S(1)}, f32[6,256]{1,0:T(8,128)S(1)}) custom-call(s32[8]{0:T(128)} %refs_0_.1, f32[8,256]{1,0:T(8,128)} %refs_1_.1, f32[8,256]{1,0:T(8,128)} %refs_2_.1, f32[8,256]{1,0:T(8,128)} %refs_3_.1, ...), custom_call_target="tpu_custom_call" | custom-call | tf_op jit(solution)/shard_map/pallas_call | solution.py:322
  2.4 0.5 %collective-permute-start = (f32[2,2,64,256]{3,2,1,0:T(8,128)S(1)}, f32[2,2,64,256]{3,2,1,0:T(8,128)S(1)}, u32[]{:S(2)}, u32[]{:S(2)}) collective-permute-start(f32[2,2,64,256]{3,2,1,0:T(8,128)S(1)} %get-tuple-element.25), channel_id=1, source_target_pairs={{0,1},{1,0},{2,3},{3,2},{4,5},{5,4},{6,7},{7,6},{8,9},{9,8},{10,11... | collective-permute-start | bytes 786440 | tf_op jit(solution)/shard_map/ppermute | solution.py:342
  2.9 2.6 %collective-permute-start.1 = (f32[2,136,128]{2,1,0:T(8,128)S(1)}, f32[2,136,128]{2,1,0:T(8,128)S(1)}, u32[]{:S(2)}, u32[]{:S(2)}) collective-permute-start(f32[2,136,128]{2,1,0:T(8,128)S(1)} %get-tuple-element.26), channel_id=1, source_target_pairs={{0,2},{1,3},{2,0},{3,1},{4,6},{5,7},{6,4},{7,5},{8,10},{9,11},{10,... | collective-permute-start | bytes 417800 | tf_op jit(solution)/shard_map/ppermute | solution.py:342
  5.5 0.1 collective-permute-start.2
  5.5 0.0 copy-done.1
  5.5 1.3 %collective-permute-start.4 = (f32[3,8,256]{2,1,0:T(8,128)S(1)}, f32[3,8,256]{2,1,0:T(8,128)S(1)}, u32[]{:S(2)}, u32[]{:S(2)}) collective-permute-start(f32[3,8,256]{2,1,0:T(8,128)S(1)} %bitcast.2), channel_id=1, source_target_pairs={{4,0},{8,4},{12,8},{16,12},{20,16},{24,20},{28,24},{5,1},{9,5},{13... | collective-permute-start | bytes 73736 | tf_op jit(solution)/shard_map/ppermute | solution.py:351
  6.8 4.5 %collective-permute-start.3 = (f32[3,8,256]{2,1,0:T(8,128)S(1)}, f32[3,8,256]{2,1,0:T(8,128)S(1)}, u32[]{:S(2)}, u32[]{:S(2)}) collective-permute-start(f32[3,8,256]{2,1,0:T(8,128)S(1)} %bitcast.3), channel_id=1, source_target_pairs={{0,4},{4,8},{8,12},{12,16},{16,20},{20,24},{24,28},{1,5},{5,9},{9,... | collective-permute-start | bytes 73736 | tf_op jit(solution)/shard_map/ppermute | solution.py:351
  11.4 0.0 collective-permute-done.4.refs_2_
  11.4 1.5 %collective-permute-done.3.refs_0_ = f32[3,8,256]{2,1,0:T(8,128)S(1)} collective-permute-done((f32[3,8,256]{2,1,0:T(8,128)S(1)}, f32[3,8,256]{2,1,0:T(8,128)S(1)}, u32[]{:S(2)}, u32[]{:S(2)}) %collective-permute-start.3) | collective-permute-done | bytes 24608 | tf_op jit(solution)/shard_map/ppermute | solution.py:351
  12.9 0.0 collective-permute-done.1.refs_2_
  12.9 0.0 collective-permute-done.2.refs_3_
  12.9 0.0 collective-permute-done.refs_1_
  12.9 7.1 %shard_map.114 = (f32[2,64,256]{2,1,0:T(8,128)S(1)}, f32[2,64,256]{2,1,0:T(8,128)S(1)}, f32[2,64,256]{2,1,0:T(8,128)S(1)}, f32[2,64,256]{2,1,0:T(8,128)S(1)}, f32[32,2,384]{2,1,0:T(2,128)}) custom-call(f32[6,256]{1,0:T(8,128)S(1)} %get-tuple-element.23.facts_ref, f32[2,2,64,256]{3,2,1,0:T(8,128)S(1)} %get-tuple-element.28.refs_0_, ...), custom_call_target="tpu_custom_call" | custom-call | flops 4831838208 | tf_op jit(solution)/shard_map/pallas_call | solution.py:322
  20.0 0.0 collective-permute-start.5
  20.0 1.7 %collective-permute-start.6 = (f32[2,64,256]{2,1,0:T(8,128)S(1)}, f32[2,64,256]{2,1,0:T(8,128)S(1)}, u32[]{:S(2)}, u32[]{:S(2)}) collective-permute-start(f32[2,64,256]{2,1,0:T(8,128)S(1)} %get-tuple-element.34), channel_id=1, source_target_pairs={{0,2},{1,3},{2,0},{3,1},{4,6},{5,7},{6,4},{7,5},{8,10},{9,11},{10,... | collective-permute-start | bytes 393224 | tf_op jit(solution)/shard_map/ppermute | solution.py:342
  21.8 0.1 collective-permute-start.7
  21.9 0.0 copy-start.2
  21.9 0.0 copy-start.3
  21.9 7.7 %all-to-all-start = ((f32[32,2,384]{2,1,0:T(2,128)}), f32[32,2,384]{2,1,0:T(2,128)S(1)}, u32[]{:S(2)}, u32[]{:S(2)}) async-start(f32[32,2,384]{2,1,0:T(2,128)} %get-tuple-element.36), calls=%async_computation | async-start | bytes 196608 | tf_op jit(solution)/shard_map/all_to_all | solution.py:413
  29.6 0.0 copy-done.2
  29.6 0.0 copy-done.3
  29.6 1.1 %shard_map.116 = (bf16[8,32,256]{2,1,0:T(8,128)(2,1)S(1)}, bf16[8,8,32,256]{3,2,1,0:T(8,128)(2,1)S(1)}, f32[8,8,64]{2,1,0:T(8,128)S(1)}, f32[8,8,64]{2,1,0:T(8,128)S(1)}) custom-call(s32[8,8]{1,0:T(8,128)S(1)} %copy-done.2, s32[8,8]{1,0:T(8,128)S(1)} %copy-done.3, f32[3,8,256]{2,1,0:T(8,128)S(1)} %bitcast.4, ...), custom_call_target="tpu_custom_call" | custom-call | flops 1000000000 | bytes 10000000 | tf_op jit(solution)/shard_map/pallas_call | solution.py:322
  30.8 0.0 copy-start
  30.8 0.0 collective-permute-done.5.refs_1_
  30.8 0.0 collective-permute-done.6.refs_2_
  30.8 0.0 collective-permute-done.7.refs_3_
  30.8 0.8 %shard_map.115.refs_0_ = f32[8,64,256]{2,1,0:T(8,128)} custom-call(f32[2,64,256]{2,1,0:T(8,128)S(1)} %get-tuple-element.32.refs_0_.refs_3_, f32[2,64,256]{2,1,0:T(8,128)S(1)} %collective-permute-done.5.refs_1_, f32[2,64,256]{2,1,0:T(8,128)S(1)} %collective-permute-done.6.refs_2_, f32[2,64,256]{2,1,0:T(8,128)S(1)} %collective-permute-done.7.refs_3_), custom_call_target="tpu_custom_call" | custom-call | flops 99999997952 | bytes 10000000 | tf_op jit(solution)/shard_map/pallas_call | solution.py:322
  31.7 5.8 %all-to-all-done.charge_ref = f32[32,2,384]{2,1,0:T(2,128)S(1)} async-done(((f32[32,2,384]{2,1,0:T(2,128)}), f32[32,2,384]{2,1,0:T(2,128)S(1)}, u32[]{:S(2)}, u32[]{:S(2)}) %all-to-all-start) | async-done | bytes 98336 | tf_op jit(solution)/shard_map/all_to_all | solution.py:413
  37.4 0.0 copy-done
  37.4 3.6 %shard_map.117 = f32[8,64,256]{2,1,0:T(8,128)} custom-call(f32[32,2,384]{2,1,0:T(2,128)S(1)} %all-to-all-done.charge_ref, f32[3,8,256]{2,1,0:T(8,128)S(1)} %bitcast.6, bf16[8,32,256]{2,1,0:T(8,128)(2,1)S(1)} %get-tuple-element.40.left_ref, bf16[8,8,32,256]{3,2,1,0:T(8,128)(2,1)S(1)} %get-tuple-element.41.right_ref, ...), custom_call_target="tpu_custom_call" | custom-call | tf_op jit(solution)/shard_map/pallas_call | solution.py:322
Async XLA Ops:
  0.6 4.9 %copy-start.1 = (f32[8,3,256]{2,0,1:T(8,128)S(1)}, f32[8,3,256]{2,0,1:T(8,128)}, u32[]{:S(2)}) copy-start(f32[8,3,256]{2,0,1:T(8,128)} %param.16) | copy-start | bytes 73732
  2.4 10.5 %collective-permute-start = (f32[2,2,64,256]{3,2,1,0:T(8,128)S(1)}, f32[2,2,64,256]{3,2,1,0:T(8,128)S(1)}, u32[]{:S(2)}, u32[]{:S(2)}) collective-permute-start(f32[2,2,64,256]{3,2,1,0:T(8,128)S(1)} %get-tuple-element.25), channel_id=1, source_target_pairs={{0,1},{1,0},{2,3},{3,2},{4,5},{5,4},{6,7},{7,6},{8,9},{9,8},{10,11... | collective-permute-start | bytes 786440 | tf_op jit(solution)/shard_map/ppermute | solution.py:342
  2.9 10.0 %collective-permute-start.1 = (f32[2,136,128]{2,1,0:T(8,128)S(1)}, f32[2,136,128]{2,1,0:T(8,128)S(1)}, u32[]{:S(2)}, u32[]{:S(2)}) collective-permute-start(f32[2,136,128]{2,1,0:T(8,128)S(1)} %get-tuple-element.26), channel_id=1, source_target_pairs={{0,2},{1,3},{2,0},{3,1},{4,6},{5,7},{6,4},{7,5},{8,10},{9,11},{10,... | collective-permute-start | bytes 417800 | tf_op jit(solution)/shard_map/ppermute | solution.py:342
  5.5 7.4 %collective-permute-start.2 = (f32[2,136,128]{2,1,0:T(8,128)S(1)}, f32[2,136,128]{2,1,0:T(8,128)S(1)}, u32[]{:S(2)}, u32[]{:S(2)}) collective-permute-start(f32[2,136,128]{2,1,0:T(8,128)S(1)} %get-tuple-element.27), channel_id=1, source_target_pairs={{0,3},{1,2},{2,1},{3,0},{4,7},{5,6},{6,5},{7,4},{8,11},{9,10},{10,... | collective-permute-start | bytes 417800 | tf_op jit(solution)/shard_map/ppermute | solution.py:342
  5.5 5.8 %collective-permute-start.4 = (f32[3,8,256]{2,1,0:T(8,128)S(1)}, f32[3,8,256]{2,1,0:T(8,128)S(1)}, u32[]{:S(2)}, u32[]{:S(2)}) collective-permute-start(f32[3,8,256]{2,1,0:T(8,128)S(1)} %bitcast.2), channel_id=1, source_target_pairs={{4,0},{8,4},{12,8},{16,12},{20,16},{24,20},{28,24},{5,1},{9,5},{13... | collective-permute-start | bytes 73736 | tf_op jit(solution)/shard_map/ppermute | solution.py:351
  6.8 6.1 %collective-permute-start.3 = (f32[3,8,256]{2,1,0:T(8,128)S(1)}, f32[3,8,256]{2,1,0:T(8,128)S(1)}, u32[]{:S(2)}, u32[]{:S(2)}) collective-permute-start(f32[3,8,256]{2,1,0:T(8,128)S(1)} %bitcast.3), channel_id=1, source_target_pairs={{0,4},{4,8},{8,12},{12,16},{16,20},{20,24},{24,28},{1,5},{5,9},{9,... | collective-permute-start | bytes 73736 | tf_op jit(solution)/shard_map/ppermute | solution.py:351
  20.0 10.8 %collective-permute-start.5 = (f32[2,64,256]{2,1,0:T(8,128)S(1)}, f32[2,64,256]{2,1,0:T(8,128)S(1)}, u32[]{:S(2)}, u32[]{:S(2)}) collective-permute-start(f32[2,64,256]{2,1,0:T(8,128)S(1)} %get-tuple-element.33), channel_id=1, source_target_pairs={{0,1},{1,0},{2,3},{3,2},{4,5},{5,4},{6,7},{7,6},{8,9},{9,8},{10,11... | collective-permute-start | bytes 393224 | tf_op jit(solution)/shard_map/ppermute | solution.py:342
  20.0 10.8 %collective-permute-start.6 = (f32[2,64,256]{2,1,0:T(8,128)S(1)}, f32[2,64,256]{2,1,0:T(8,128)S(1)}, u32[]{:S(2)}, u32[]{:S(2)}) collective-permute-start(f32[2,64,256]{2,1,0:T(8,128)S(1)} %get-tuple-element.34), channel_id=1, source_target_pairs={{0,2},{1,3},{2,0},{3,1},{4,6},{5,7},{6,4},{7,5},{8,10},{9,11},{10,... | collective-permute-start | bytes 393224 | tf_op jit(solution)/shard_map/ppermute | solution.py:342
  21.8 9.0 %collective-permute-start.7 = (f32[2,64,256]{2,1,0:T(8,128)S(1)}, f32[2,64,256]{2,1,0:T(8,128)S(1)}, u32[]{:S(2)}, u32[]{:S(2)}) collective-permute-start(f32[2,64,256]{2,1,0:T(8,128)S(1)} %get-tuple-element.35), channel_id=1, source_target_pairs={{0,3},{1,2},{2,1},{3,0},{4,7},{5,6},{6,5},{7,4},{8,11},{9,10},{10,... | collective-permute-start | bytes 393224 | tf_op jit(solution)/shard_map/ppermute | solution.py:342
  21.9 7.7 %copy-start.2 = (s32[8,8]{1,0:T(8,128)S(1)}, s32[8,8]{1,0:T(8,128)}, u32[]{:S(2)}) copy-start(s32[8,8]{1,0:T(8,128)} %near_ref.1) | copy-start | bytes 772
  21.9 7.7 %copy-start.3 = (s32[8,8]{1,0:T(8,128)S(1)}, s32[8,8]{1,0:T(8,128)}, u32[]{:S(2)}) copy-start(s32[8,8]{1,0:T(8,128)} %far_ref.1) | copy-start | bytes 772
  21.9 15.5 %all-to-all-start = ((f32[32,2,384]{2,1,0:T(2,128)}), f32[32,2,384]{2,1,0:T(2,128)S(1)}, u32[]{:S(2)}, u32[]{:S(2)}) async-start(f32[32,2,384]{2,1,0:T(2,128)} %get-tuple-element.36), calls=%async_computation | async-start | bytes 196608 | tf_op jit(solution)/shard_map/all_to_all | solution.py:413
  30.8 6.7 %copy-start = (f32[8,64,256]{2,1,0:T(8,128)S(1)}, f32[8,64,256]{2,1,0:T(8,128)}, u32[]{:S(2)}) copy-start(f32[8,64,256]{2,1,0:T(8,128)} %over_ref.1) | copy-start | bytes 1572868

commit v4 on v3

--- a/solution.py
+++ b/solution.py
@@ -100,21 +100,21 @@
             core, core_far = swapped(half, core_ref[frag])
             over, over_far = swapped(half, over_ref[frag])
             inside = (row < size) & (mine < size)
-            over = jnp.where(inside, over, 0.0)
-            near_part = jnp.where(inside, 0.5 * core, 0.0) + over * (0.5 * field)
+            core, over = jnp.where(inside, core, 0.0), jnp.where(inside, over, 0.0)
             out = outs[shift]
             if shift < places:
                 inside = (row < size) & (others < size)
                 over_far = jnp.where(inside, over_far, 0.0)
-                out[0, spot, :, :middle] = near_part
+                out[0, spot, :, :middle] = 0.5 * (core + over * field)
                 out[0, spot, :, middle:] = jnp.where(inside, core_far, 0.0) + over_far * (0.5 * field)
                 out[1, spot, :, :middle] = over
                 out[1, spot, :, middle:] = over_far
             else:
-                out[spot, :rows] = near_part
-                out[spot, rows : 2 * rows] = over
+                out[spot, :rows] = jnp.where(mine >= row, core, over)
                 field_row = jnp.sum(jnp.where(pick_half, field, 0.0), axis=0, keepdims=True)
-                out[spot, 2 * rows :] = jnp.broadcast_to(field_row, (out.shape[1] - 2 * rows, middle))
+                diagonal = jnp.sum(jnp.where(pick_half, over, 0.0), axis=0, keepdims=True)
+                rest = jnp.zeros((out.shape[1] - rows - 2, middle), jnp.float32)
+                out[spot, rows:] = jnp.concatenate([field_row, diagonal, rest], axis=0)
             if shift == 0:
                 facts = outs[-1]
                 idle = swapped(half, (lane >= size).astype(jnp.float32))
@@ -155,15 +155,20 @@
             x_ref[spot, span, :] = near_parts[shift][0, spot]
             s_ref[spot, span, :] = near_parts[shift][1, spot]
             x_ref[spot, far_span, middle:] = far_parts[shift][spot, :rows]
-            s_ref[spot, far_span, middle:] = far_parts[shift][spot, rows : 2 * rows]
     row = lax.broadcasted_iota(jnp.int32, (basis, basis), 0)
     column = lax.broadcasted_iota(jnp.int32, (basis, basis), 1)
     near, far = slice(0, middle), slice(middle, basis)
     for spot in range(share):
-        field = far_parts[0][spot, 2 * rows : 2 * rows + 1, :]
+        extra = far_parts[0][spot, rows:]
         for part in far_parts[1:]:
-            field = field + part[spot, 2 * rows : 2 * rows + 1, :]
-        corner, last = x_ref[spot, near, near], x_ref[spot, far, far]
+            extra = extra + part[spot, rows:]
+        field = extra[:1]
+        corner, packed = x_ref[spot, near, near], x_ref[spot, far, far]
+        turned = packed.T
+        down, along = row[near, near], column[near, near]
+        over = jnp.where(along < down, packed, jnp.where(along == down, extra[1:2], turned))
+        last = 0.5 * (jnp.where(along >= down, packed, turned) + over * field)
+        s_ref[spot, far, far] = over
         side = x_ref[spot, near, far] + s_ref[spot, near, far] * (0.5 * field)
         corner, last = corner + corner.T, last + last.T
         total = corner * corner + last * last + 2.0 * (side * side)
@@ -228,7 +233,8 @@
     basis = own_ref.shape[2]
     lane = lax.broadcasted_iota(jnp.int32, (1, near_hot.shape[2]), 1)
     ones = jnp.ones((frag_dev, basis), jnp.float32)
-    first_frag = (lax.axis_index("frag") - around // 2) * frag_dev
+    frag_at, reach = lax.axis_index("frag"), around // 2
+    first_frag = (frag_at - reach) * frag_dev
 
     def fill(target, first, place_ref, scale, extra, which):
         places = [place_ref[axis] for axis in range(3)]
@@ -246,8 +252,12 @@
 
     fill(side_ref, 0, own_ref, -2.0, 1.0, 0)
     left_out[...] = side_ref[...].astype(jnp.bfloat16)
-    for step in range(around):
-        fill(table_side, step * frag_dev, sources[step], 1.0, 0.0, 1)
+    fill(table_side, reach * frag_dev, sources[0], 1.0, 0.0, 1)
+    for at in range(1, around):
+        step = (at + 1) // 2
+        side = lax.rem(frag_at // step + at + 1, 2)
+        spot = reach + step * (1 - 2 * side)
+        fill(table_side, spot * frag_dev, sources[at], 1.0, 0.0, 1)
     for frag in range(frag_dev):
         for k in range(near):
             other = near_ref[frag, k]
@@ -258,7 +268,7 @@
 
 
 def gather_kernel(tiles, *refs):
-    chunks, density_ref, sems = refs[:tiles], refs[tiles], refs[tiles + 1]
+    chunks, (density_ref, sems) = refs[:tiles], refs[tiles + 1 :]
     share = chunks[0].shape[0]
     copies = []
     for shift in range(tiles):
@@ -270,7 +280,7 @@
 
 
 def potential_kernel(tiles, charge_ref, own_ref, left_ref, right_ref, near_hot, far_hot, over_ref, *refs):
-    esp_ref, near_charge, far_block, esp_rows, sems = refs[1:]
+    esp_ref, near_charge, far_block, esp_rows, sems = refs
     frag_dev, rows, basis = over_ref.shape
     share = frag_dev // tiles
     near, far = near_hot.shape[1], far_hot.shape[1]
@@ -345,10 +355,11 @@
 
 def neighbours(x, axis, reach):
     peers = lax.axis_size(axis)
-    found = []
-    for step in range(-reach, reach + 1):
-        pairs = [(i, i - step) for i in range(peers) if 0 <= i - step < peers]
-        found.append(x if step == 0 else lax.ppermute(x, axis, pairs))
+    found = [x]
+    for step in range(1, reach + 1):
+        for parity in range(2):
+            ups = [(i, i + step) for i in range(peers - step) if (i // step) % 2 == parity]
+            found.append(lax.ppermute(x, axis, ups + [(j, i) for i, j in ups]))
     return found
 
 
@@ -371,7 +382,7 @@
     places = jnp.transpose(centres, (1, 0, 2))
     inputs = (frag_sizes, charge_old, embed_old, core_pop, places, gamma_tile, intersection, core_fock)
     near_part = floats(2, share, rows, basis)
-    far_part = floats(share, 2 * rows + 8, basis // 2)
+    far_part = floats(share, rows + 8, basis // 2)
     *sent, facts = call(
         functools.partial(half_fock_kernel, tiles),
         [near_part] * (tiles // 2) + [far_part] * (tiles // 2) + [floats(3 * share, basis)],
@@ -383,15 +394,17 @@
     )
     sent = exchanged(sent)
     sources = neighbours(places, "frag", -(-SPAN // frag_dev))
-    sent, sources = lax.optimization_barrier((sent, sources))
     *pieces, charges = call(
         functools.partial(density_kernel, tiles),
         [chunk] * tiles + [floats(devices, share, basis + LANES)],
         (facts, *sent),
         [VMEM] * (1 + tiles),
         [pltpu.VMEM((share, basis, basis), jnp.float32)] * 2,
-        pl.CostEstimate(flops=12 * ITERS * share * basis**3, bytes_accessed=0, transcendentals=0),
-    )
+        pl.CostEstimate(flops=0, bytes_accessed=0, transcendentals=0),
+    )
+    moved = exchanged(pieces)
+    charges, sources = lax.optimization_barrier((charges, sources))
+    charges = lax.all_to_all(charges, ("frag", "tile"), split_axis=0, concat_axis=0, tiled=True)
     near, far, frags = near_list.shape[1], far_list.shape[1], peers * frag_dev
     parts = call(
         functools.partial(geometry_kernel, len(sources)),
@@ -407,31 +420,30 @@
             pltpu.VMEM((frag_dev, DEPTH, basis), jnp.float32),
             pltpu.VMEM((len(sources) * frag_dev, DEPTH, basis), jnp.float32),
         ],
-        pl.CostEstimate(flops=10**9, bytes_accessed=10**7, transcendentals=0),
-    )
-    moved = exchanged(pieces)
-    charges = lax.all_to_all(charges, ("frag", "tile"), split_axis=0, concat_axis=0, tiled=True)
-    (density,) = call(
-        functools.partial(gather_kernel, tiles),
-        [floats(frag_dev, rows, basis)],
-        moved,
-        [VMEM] * tiles,
-        [pltpu.SemaphoreType.DMA((tiles,))],
-        pl.CostEstimate(flops=10**11, bytes_accessed=10**7, transcendentals=0),
-        HBM,
+        pl.CostEstimate(flops=0, bytes_accessed=0, transcendentals=0),
     )
     (esp_matrix,) = call(
         functools.partial(potential_kernel, tiles),
         [floats(frag_dev, rows, basis)],
-        (charges, places, *parts, intersection, pltpu.with_memory_space_constraint(density, pltpu.HBM)),
-        [VMEM] * 7 + [HBM],
+        (charges, places, *parts, intersection),
+        [VMEM] * 7,
         [
             pltpu.VMEM((frag_dev, near, basis), jnp.float32),
             pltpu.VMEM((frag_dev, far, LANES), jnp.float32),
             pltpu.VMEM((frag_dev, rows, basis), jnp.float32),
             pltpu.SemaphoreType.DMA((tiles,)),
         ],
-        out_spec=HBM,
+        pl.CostEstimate(flops=0, bytes_accessed=0, transcendentals=0),
+        HBM,
+    )
+    (density,) = call(
+        functools.partial(gather_kernel, tiles),
+        [floats(frag_dev, rows, basis)],
+        (*moved, pltpu.with_memory_space_constraint(esp_matrix, pltpu.HBM)),
+        [VMEM] * tiles + [HBM],
+        [pltpu.SemaphoreType.DMA((tiles,))],
+        pl.CostEstimate(flops=0, bytes_accessed=0, transcendentals=0),
+        HBM,
     )
     return (density, esp_matrix)
 

time: 41.3 us -> 35.4 us (0.86)
  starting transfers between devices: 18.6 us -> 15.1 us
  waiting for transfers between devices: 7.29 us -> 4.69 us
    all_to_all x1, starting transfers between devices: 7.7 us -> 4.76 us  [per_device(): lax.all_to_all(charges, ('frag', 'tile'), split_axis=0, concat_axis=0, ti...]
    ppermute x2, waiting for transfers between devices: 1.49 us -> 0.01 us  [neighbours(): found.append(lax.ppermute(x, axis, ups + [(j, i) for i, j in ups]))]
    all_to_all x1, waiting for transfers between devices: 5.78 us -> 4.67 us  [per_device(): lax.all_to_all(charges, ('frag', 'tile'), split_axis=0, concat_axis=0, ti...]
    ppermute x2, starting transfers between devices: 5.83 us -> 5.24 us  [neighbours(): found.append(lax.ppermute(x, axis, ups + [(j, i) for i, j in ups]))]
  transfers between devices with their start and end apart: 9 -> 9, of which waited for: 2 -> 1; matrix products, arithmetic and copies ran while one was open for 0% -> 0% of each run, Pallas kernels for 5% -> 34%
where the time goes in v4:
time: 35.4 us; the launch traced here: 35.2 us
  starting transfers between devices  15.1 us (43%)
  Pallas kernels  14.6 us (41%)
  waiting for transfers between devices  4.69 us (13%)
  between operations  0.74 us (2%)
    pallas_call x5, Pallas kernels, call(): pl.pallas_call(kernel, out_shape=outs, in_specs=specs, out_specs=[out_spe...  14.6 us
    ppermute x2, starting transfers between devices, neighbours(): found.append(lax.ppermute(x, axis, ups + [(j, i) for i, j in ups]))  5.24 us
    ppermute x6, starting transfers between devices, exchanged(): moved.append(lax.ppermute(chunks[shift], 'tile', pairs))  5.15 us
    all_to_all x1, starting transfers between devices, per_device(): lax.all_to_all(charges, ('frag', 'tile'), split_axis=0, concat_axis=0, ti...  4.76 us
    all_to_all x1, waiting for transfers between devices, per_device(): lax.all_to_all(charges, ('frag', 'tile'), split_axis=0, concat_axis=0, ti...  4.67 us
  transfers between devices with their start and end apart: 9, of which 1 were waited for; matrix products, arithmetic and copies ran while one was open for 0% of the time, Pallas kernels for 34%

profile of v4, /device:TPU:0, one launch (start us, length us, event | category | flops | bytes accessed | tf_op | source)
XLA Modules:
  0.0 35.2 jit_solution(4427252808604800731)
XLA Ops:
  0.6 0.0 copy-start.1
  0.6 1.7 %shard_map.113 = (f32[2,2,64,256]{3,2,1,0:T(8,128)S(1)}, f32[2,2,64,256]{3,2,1,0:T(8,128)S(1)}, f32[2,72,128]{2,1,0:T(8,128)S(1)}, f32[2,72,128]{2,1,0:T(8,128)S(1)}, f32[6,256]{1,0:T(8,128)S(1)}) custom-call(s32[8]{0:T(128)} %refs_0_.1, f32[8,256]{1,0:T(8,128)} %refs_1_.1, f32[8,256]{1,0:T(8,128)} %refs_2_.1, f32[8,256]{1,0:T(8,128)} %refs_3_.1, ...), custom_call_target="tpu_custom_call" | custom-call | tf_op jit(solution)/shard_map/pallas_call | solution.py:332
  2.4 0.5 %collective-permute-start = (f32[2,2,64,256]{3,2,1,0:T(8,128)S(1)}, f32[2,2,64,256]{3,2,1,0:T(8,128)S(1)}, u32[]{:S(2)}, u32[]{:S(2)}) collective-permute-start(f32[2,2,64,256]{3,2,1,0:T(8,128)S(1)} %get-tuple-element.22), channel_id=1, source_target_pairs={{0,1},{1,0},{2,3},{3,2},{4,5},{5,4},{6,7},{7,6},{8,9},{9,8},{10,11... | collective-permute-start | bytes 786440 | tf_op jit(solution)/shard_map/ppermute | solution.py:352
  2.9 2.6 %collective-permute-start.1 = (f32[2,72,128]{2,1,0:T(8,128)S(1)}, f32[2,72,128]{2,1,0:T(8,128)S(1)}, u32[]{:S(2)}, u32[]{:S(2)}) collective-permute-start(f32[2,72,128]{2,1,0:T(8,128)S(1)} %get-tuple-element.23), channel_id=1, source_target_pairs={{0,2},{1,3},{2,0},{3,1},{4,6},{5,7},{6,4},{7,5},{8,10},{9,11},{10,... | collective-permute-start | bytes 221192 | tf_op jit(solution)/shard_map/ppermute | solution.py:352
  5.5 0.1 collective-permute-start.2
  5.5 0.0 copy-done.1
  5.5 0.7 %collective-permute-start.7 = (f32[3,8,256]{2,1,0:T(8,128)S(1)}, f32[3,8,256]{2,1,0:T(8,128)S(1)}, u32[]{:S(2)}, u32[]{:S(2)}) collective-permute-start(f32[3,8,256]{2,1,0:T(8,128)S(1)} %bitcast.2), channel_id=1, source_target_pairs={{4,8},{12,16},{20,24},{8,4},{16,12},{24,20},{5,9},{13,17},{21,25},... | collective-permute-start | bytes 73736 | tf_op jit(solution)/shard_map/ppermute | solution.py:362
  6.2 4.6 %collective-permute-start.6 = (f32[3,8,256]{2,1,0:T(8,128)S(1)}, f32[3,8,256]{2,1,0:T(8,128)S(1)}, u32[]{:S(2)}, u32[]{:S(2)}) collective-permute-start(f32[3,8,256]{2,1,0:T(8,128)S(1)} %bitcast.3), channel_id=1, source_target_pairs={{0,4},{8,12},{16,20},{24,28},{4,0},{12,8},{20,16},{28,24},{1,5},{9... | collective-permute-start | bytes 73736 | tf_op jit(solution)/shard_map/ppermute | solution.py:362
  10.8 0.0 collective-permute-done.1.refs_2_
  10.8 0.0 collective-permute-done.2.refs_3_
  10.8 0.0 collective-permute-done.refs_1_
  10.8 0.0 copy-start
  10.8 7.3 %shard_map.114 = (f32[2,64,256]{2,1,0:T(8,128)S(1)}, f32[2,64,256]{2,1,0:T(8,128)S(1)}, f32[2,64,256]{2,1,0:T(8,128)S(1)}, f32[2,64,256]{2,1,0:T(8,128)S(1)}, f32[32,2,384]{2,1,0:T(2,128)}) custom-call(f32[6,256]{1,0:T(8,128)S(1)} %get-tuple-element.20.facts_ref, f32[2,2,64,256]{3,2,1,0:T(8,128)S(1)} %get-tuple-element.21.refs_0_, ...), custom_call_target="tpu_custom_call" | custom-call | tf_op jit(solution)/shard_map/pallas_call | solution.py:332
  18.1 0.0 collective-permute-done.7.refs_2_
  18.1 0.0 collective-permute-done.6.refs_1_
  18.1 0.0 copy-start.3
  18.1 4.8 %all-to-all-start = ((f32[32,2,384]{2,1,0:T(2,128)}), f32[32,2,384]{2,1,0:T(2,128)S(1)}, u32[]{:S(2)}, u32[]{:S(2)}) async-start(f32[32,2,384]{2,1,0:T(2,128)} %get-tuple-element.30), calls=%async_computation | async-start | bytes 196608 | tf_op jit(solution)/shard_map/all_to_all | solution.py:407
  22.9 0.0 copy-start.2
  22.9 0.3 collective-permute-start.3
  23.2 1.7 %collective-permute-start.4 = (f32[2,64,256]{2,1,0:T(8,128)S(1)}, f32[2,64,256]{2,1,0:T(8,128)S(1)}, u32[]{:S(2)}, u32[]{:S(2)}) collective-permute-start(f32[2,64,256]{2,1,0:T(8,128)S(1)} %get-tuple-element.27), channel_id=1, source_target_pairs={{0,2},{1,3},{2,0},{3,1},{4,6},{5,7},{6,4},{7,5},{8,10},{9,11},{10,... | collective-permute-start | bytes 393224 | tf_op jit(solution)/shard_map/ppermute | solution.py:352
  24.9 0.0 collective-permute-start.5
  24.9 0.0 copy-done.3
  24.9 0.0 copy-done.2
  24.9 1.1 %shard_map.115 = (bf16[8,32,256]{2,1,0:T(8,128)(2,1)S(1)}, bf16[8,8,32,256]{3,2,1,0:T(8,128)(2,1)S(1)}, f32[8,8,64]{2,1,0:T(8,128)S(1)}, f32[8,8,64]{2,1,0:T(8,128)S(1)}) custom-call(s32[8,8]{1,0:T(8,128)S(1)} %copy-done.2, s32[8,8]{1,0:T(8,128)S(1)} %copy-done.3, f32[3,8,256]{2,1,0:T(8,128)S(1)} %bitcast.4, f32[3,8,256]{2,1,0:T(8,128)S(1)} %bitcast.5, ...), custom_call_target="tpu_custom_call" | custom-call | tf_op jit(solution)/shard_map/pallas_call | solution.py:332
  26.0 4.7 %all-to-all-done.charge_ref = f32[32,2,384]{2,1,0:T(2,128)S(1)} async-done(((f32[32,2,384]{2,1,0:T(2,128)}), f32[32,2,384]{2,1,0:T(2,128)S(1)}, u32[]{:S(2)}, u32[]{:S(2)}) %all-to-all-start) | async-done | bytes 98336 | tf_op jit(solution)/shard_map/all_to_all | solution.py:407
  30.7 0.0 copy-done
  30.7 3.6 %shard_map.116.refs_4_ = f32[8,64,256]{2,1,0:T(8,128)} custom-call(f32[32,2,384]{2,1,0:T(2,128)S(1)} %all-to-all-done.charge_ref, f32[3,8,256]{2,1,0:T(8,128)S(1)} %bitcast.6, bf16[8,32,256]{2,1,0:T(8,128)(2,1)S(1)} %get-tuple-element.34.left_ref, bf16[8,8,32,256]{3,2,1,0:T(8,128)(2,1)S(1)} %get-tuple-element.35.right_ref, ...), custom_call_target="tpu_custom_call" | custom-call | tf_op jit(solution)/shard_map/pallas_call | solution.py:332
  34.3 0.0 collective-permute-done.3.refs_1_
  34.3 0.0 collective-permute-done.4.refs_2_
  34.3 0.0 collective-permute-done.5.refs_3_
  34.4 0.8 %shard_map.117 = f32[8,64,256]{2,1,0:T(8,128)} custom-call(f32[2,64,256]{2,1,0:T(8,128)S(1)} %get-tuple-element.25.refs_3_.refs_0_, f32[2,64,256]{2,1,0:T(8,128)S(1)} %collective-permute-done.3.refs_1_, f32[2,64,256]{2,1,0:T(8,128)S(1)} %collective-permute-done.4.refs_2_, f32[2,64,256]{2,1,0:T(8,128)S(1)} %collective-permute-done.5.refs_3_, ...), custom_call_target="tpu_custom_call" | custom-call | tf_op jit(solution)/shard_map/pallas_call | solution.py:332
Async XLA Ops:
  0.6 4.9 %copy-start.1 = (f32[8,3,256]{2,0,1:T(8,128)S(1)}, f32[8,3,256]{2,0,1:T(8,128)}, u32[]{:S(2)}) copy-start(f32[8,3,256]{2,0,1:T(8,128)} %param.16) | copy-start | bytes 73732
  2.4 8.4 %collective-permute-start = (f32[2,2,64,256]{3,2,1,0:T(8,128)S(1)}, f32[2,2,64,256]{3,2,1,0:T(8,128)S(1)}, u32[]{:S(2)}, u32[]{:S(2)}) collective-permute-start(f32[2,2,64,256]{3,2,1,0:T(8,128)S(1)} %get-tuple-element.22), channel_id=1, source_target_pairs={{0,1},{1,0},{2,3},{3,2},{4,5},{5,4},{6,7},{7,6},{8,9},{9,8},{10,11... | collective-permute-start | bytes 786440 | tf_op jit(solution)/shard_map/ppermute | solution.py:352
  2.9 7.9 %collective-permute-start.1 = (f32[2,72,128]{2,1,0:T(8,128)S(1)}, f32[2,72,128]{2,1,0:T(8,128)S(1)}, u32[]{:S(2)}, u32[]{:S(2)}) collective-permute-start(f32[2,72,128]{2,1,0:T(8,128)S(1)} %get-tuple-element.23), channel_id=1, source_target_pairs={{0,2},{1,3},{2,0},{3,1},{4,6},{5,7},{6,4},{7,5},{8,10},{9,11},{10,... | collective-permute-start | bytes 221192 | tf_op jit(solution)/shard_map/ppermute | solution.py:352
  5.5 5.3 %collective-permute-start.2 = (f32[2,72,128]{2,1,0:T(8,128)S(1)}, f32[2,72,128]{2,1,0:T(8,128)S(1)}, u32[]{:S(2)}, u32[]{:S(2)}) collective-permute-start(f32[2,72,128]{2,1,0:T(8,128)S(1)} %get-tuple-element.24), channel_id=1, source_target_pairs={{0,3},{1,2},{2,1},{3,0},{4,7},{5,6},{6,5},{7,4},{8,11},{9,10},{10,... | collective-permute-start | bytes 221192 | tf_op jit(solution)/shard_map/ppermute | solution.py:352
  5.5 12.6 %collective-permute-start.7 = (f32[3,8,256]{2,1,0:T(8,128)S(1)}, f32[3,8,256]{2,1,0:T(8,128)S(1)}, u32[]{:S(2)}, u32[]{:S(2)}) collective-permute-start(f32[3,8,256]{2,1,0:T(8,128)S(1)} %bitcast.2), channel_id=1, source_target_pairs={{4,8},{12,16},{20,24},{8,4},{16,12},{24,20},{5,9},{13,17},{21,25},... | collective-permute-start | bytes 73736 | tf_op jit(solution)/shard_map/ppermute | solution.py:362
  6.2 11.9 %collective-permute-start.6 = (f32[3,8,256]{2,1,0:T(8,128)S(1)}, f32[3,8,256]{2,1,0:T(8,128)S(1)}, u32[]{:S(2)}, u32[]{:S(2)}) collective-permute-start(f32[3,8,256]{2,1,0:T(8,128)S(1)} %bitcast.3), channel_id=1, source_target_pairs={{0,4},{8,12},{16,20},{24,28},{4,0},{12,8},{20,16},{28,24},{1,5},{9... | collective-permute-start | bytes 73736 | tf_op jit(solution)/shard_map/ppermute | solution.py:362
  10.8 19.9 %copy-start = (f32[8,64,256]{2,1,0:T(8,128)S(1)}, f32[8,64,256]{2,1,0:T(8,128)}, u32[]{:S(2)}) copy-start(f32[8,64,256]{2,1,0:T(8,128)} %over_ref.1) | copy-start | bytes 1572868
  18.1 6.8 %copy-start.3 = (s32[8,8]{1,0:T(8,128)S(1)}, s32[8,8]{1,0:T(8,128)}, u32[]{:S(2)}) copy-start(s32[8,8]{1,0:T(8,128)} %far_ref.1) | copy-start | bytes 772
  18.1 12.6 %all-to-all-start = ((f32[32,2,384]{2,1,0:T(2,128)}), f32[32,2,384]{2,1,0:T(2,128)S(1)}, u32[]{:S(2)}, u32[]{:S(2)}) async-start(f32[32,2,384]{2,1,0:T(2,128)} %get-tuple-element.30), calls=%async_computation | async-start | bytes 196608 | tf_op jit(solution)/shard_map/all_to_all | solution.py:407
  22.9 2.0 %copy-start.2 = (s32[8,8]{1,0:T(8,128)S(1)}, s32[8,8]{1,0:T(8,128)}, u32[]{:S(2)}) copy-start(s32[8,8]{1,0:T(8,128)} %near_ref.1) | copy-start | bytes 772
  22.9 11.4 %collective-permute-start.3 = (f32[2,64,256]{2,1,0:T(8,128)S(1)}, f32[2,64,256]{2,1,0:T(8,128)S(1)}, u32[]{:S(2)}, u32[]{:S(2)}) collective-permute-start(f32[2,64,256]{2,1,0:T(8,128)S(1)} %get-tuple-element.26), channel_id=1, source_target_pairs={{0,1},{1,0},{2,3},{3,2},{4,5},{5,4},{6,7},{7,6},{8,9},{9,8},{10,11... | collective-permute-start | bytes 393224 | tf_op jit(solution)/shard_map/ppermute | solution.py:352
  23.2 11.1 %collective-permute-start.4 = (f32[2,64,256]{2,1,0:T(8,128)S(1)}, f32[2,64,256]{2,1,0:T(8,128)S(1)}, u32[]{:S(2)}, u32[]{:S(2)}) collective-permute-start(f32[2,64,256]{2,1,0:T(8,128)S(1)} %get-tuple-element.27), channel_id=1, source_target_pairs={{0,2},{1,3},{2,0},{3,1},{4,6},{5,7},{6,4},{7,5},{8,10},{9,11},{10,... | collective-permute-start | bytes 393224 | tf_op jit(solution)/shard_map/ppermute | solution.py:352
  24.9 9.5 %collective-permute-start.5 = (f32[2,64,256]{2,1,0:T(8,128)S(1)}, f32[2,64,256]{2,1,0:T(8,128)S(1)}, u32[]{:S(2)}, u32[]{:S(2)}) collective-permute-start(f32[2,64,256]{2,1,0:T(8,128)S(1)} %get-tuple-element.28), channel_id=1, source_target_pairs={{0,3},{1,2},{2,1},{3,0},{4,7},{5,6},{6,5},{7,4},{8,11},{9,10},{10,... | collective-permute-start | bytes 393224 | tf_op jit(solution)/shard_map/ppermute | solution.py:352

commit v5 on v4

--- a/solution.py
+++ b/solution.py
@@ -13,6 +13,9 @@
 SPAN = 8
 LANES = 128
 CHUNK = 128
+COARSE = jnp.float8_e4m3fn
+WHOLE_SCALE = 256.0
+REST_SCALE = 65536.0
 VMEM = pl.BlockSpec(memory_space=pltpu.VMEM)
 SMEM = pl.BlockSpec(memory_space=pltpu.SMEM)
 HBM = pl.BlockSpec(memory_space=pltpu.HBM)
@@ -128,15 +131,14 @@
 
 def split(x):
     high = x.astype(jnp.bfloat16)
-    low = (x - high.astype(jnp.float32)).astype(jnp.bfloat16)
-    return high, low
+    low = x - high.astype(jnp.float32)
+    return high, (x * WHOLE_SCALE).astype(COARSE), (low * REST_SCALE).astype(COARSE)
 
 
 def product(left, right):
-    lh, ll = left
-    rh, rl = right
     dot = functools.partial(jnp.dot, preferred_element_type=jnp.float32)
-    return dot(lh, rh) + (dot(lh, rl) + dot(ll, rh))
+    rest = dot(left[1], right[2]) + dot(left[2], right[1])
+    return dot(left[0], right[0]) + rest * (1.0 / (WHOLE_SCALE * REST_SCALE))
 
 
 def density_kernel(tiles, facts_ref, *refs):
@@ -267,63 +269,68 @@
             far_hot[frag, m : m + 1, :] = (lane == far_ref[frag, m]).astype(jnp.float32)
 
 
-def gather_kernel(tiles, *refs):
-    chunks, (density_ref, sems) = refs[:tiles], refs[tiles + 1 :]
-    share = chunks[0].shape[0]
-    copies = []
-    for shift in range(tiles):
-        target = density_ref.at[pl.ds(partner(shift, tiles, -1) * share, share)]
-        copies.append(pltpu.make_async_copy(chunks[shift], target, sems.at[shift]))
-        copies[-1].start()
-    for copy in copies:
-        copy.wait()
-
-
-def potential_kernel(tiles, charge_ref, own_ref, left_ref, right_ref, near_hot, far_hot, over_ref, *refs):
-    esp_ref, near_charge, far_block, esp_rows, sems = refs
-    frag_dev, rows, basis = over_ref.shape
-    share = frag_dev // tiles
+def esp_rows_of(first, count, charge_ref, own_ref, left_ref, right_ref, near_hot, far_hot, over_ref, near_charge, far_block):
+    _, rows, basis = over_ref.shape
     near, far = near_hot.shape[1], far_hot.shape[1]
-    copies = []
     pick = own_rows(rows, basis, lax.axis_index("tile") * rows)
     table = charge_ref[...].reshape(-1, basis + LANES)
     for hot, gathered, part in (
         (near_hot, near_charge, table[:, :basis]),
         (far_hot, far_block, table[:, basis:]),
     ):
-        every = hot[...].reshape(-1, hot.shape[2])
+        every = hot[first : first + count].reshape(-1, hot.shape[2])
         picked = jnp.dot(every, part, precision=lax.Precision.HIGHEST, preferred_element_type=jnp.float32)
         gathered[...] = picked.reshape(gathered.shape)
     quantities = [block_lanes(at) for at in range(4)]
-    for part in range(tiles):
-        for frag in range(part * share, (part + 1) * share):
-            folded = jnp.zeros((basis, 128), jnp.float32)
-            for k in range(near):
-                square = lax.dot_general(
-                    left_ref[frag],
-                    right_ref[frag, k],
-                    (((0,), (0,)), ((), ())),
-                    preferred_element_type=jnp.float32,
-                )
-                terms = lax.rsqrt(square) * near_charge[frag, k : k + 1, :]
-                for start in range(0, basis, 128):
-                    folded = folded + terms[:, start : start + 128]
-            blocks = jnp.zeros((PC, basis), jnp.float32)
-            spots = [own_ref[axis, frag : frag + 1, :] for axis in range(3)]
-            for m in range(far):
-                row = far_block[frag, m : m + 1, :]
-                x, y, z, charge = [
-                    jnp.sum(jnp.where(lanes, row, 0.0), axis=1, keepdims=True) for lanes in quantities
-                ]
-                total = (spots[0] - x) ** 2 + (spots[1] - y) ** 2 + (spots[2] - z) ** 2
-                blocks = blocks + charge * lax.rsqrt(total + 1.0)
-            potential = jnp.sum(folded.T, axis=0, keepdims=True) + jnp.sum(blocks, axis=0, keepdims=True)
-            potential = (0.5 * SCREENING) * potential
-            mine = jnp.sum(jnp.where(pick, potential, 0.0), axis=1, keepdims=True)
-            esp_rows[frag] = over_ref[frag] * (mine + potential)
-        span = pl.ds(part * share, share)
-        copies.append(pltpu.make_async_copy(esp_rows.at[span], esp_ref.at[span], sems.at[part]))
-        copies[-1].start()
+    for at in range(count):
+        frag = first + at
+        folded = jnp.zeros((basis, LANES), jnp.float32)
+        for k in range(near):
+            square = lax.dot_general(
+                left_ref[frag],
+                right_ref[frag, k],
+                (((0,), (0,)), ((), ())),
+                preferred_element_type=jnp.float32,
+            )
+            terms = lax.rsqrt(square) * near_charge[at, k : k + 1, :]
+            for start in range(0, basis, LANES):
+                folded = folded + terms[:, start : start + LANES]
+        blocks = jnp.zeros((PC, basis), jnp.float32)
+        spots = [own_ref[axis, frag : frag + 1, :] for axis in range(3)]
+        for m in range(far):
+            row = far_block[at, m : m + 1, :]
+            x, y, z, charge = [
+                jnp.sum(jnp.where(lanes, row, 0.0), axis=1, keepdims=True) for lanes in quantities
+            ]
+            total = (spots[0] - x) ** 2 + (spots[1] - y) ** 2 + (spots[2] - z) ** 2
+            blocks = blocks + charge * lax.rsqrt(total + 1.0)
+        potential = jnp.sum(folded.T, axis=0, keepdims=True) + jnp.sum(blocks, axis=0, keepdims=True)
+        potential = (0.5 * SCREENING) * potential
+        mine = jnp.sum(jnp.where(pick, potential, 0.0), axis=1, keepdims=True)
+        yield frag, over_ref[frag] * (mine + potential)
+
+
+def first_esp_kernel(*refs):
+    inputs, esp_ref, scratch = refs[:7], refs[7], refs[8:]
+    for frag, rows in esp_rows_of(0, esp_ref.shape[0], *inputs, *scratch):
+        esp_ref[frag] = rows
+
+
+def last_esp_kernel(tiles, *refs):
+    inputs, done_ref, chunks = refs[:7], refs[7], refs[8 : 8 + tiles]
+    density_ref, esp_ref, rest_ref, near_charge, far_block, sems = refs[8 + tiles :]
+    share, done = chunks[0].shape[0], done_ref.shape[0]
+    copies = [pltpu.make_async_copy(done_ref, esp_ref.at[pl.ds(0, done)], sems.at[tiles])]
+    for shift in range(tiles):
+        target = density_ref.at[pl.ds(partner(shift, tiles, -1) * share, share)]
+        copies.append(pltpu.make_async_copy(chunks[shift], target, sems.at[shift]))
+    for copy in copies:
+        copy.start()
+    rest = rest_ref.shape[0]
+    for frag, rows in esp_rows_of(done, rest, *inputs, near_charge, far_block):
+        rest_ref[frag - done] = rows
+    copies.append(pltpu.make_async_copy(rest_ref, esp_ref.at[pl.ds(done, rest)], sems.at[tiles + 1]))
+    copies[-1].start()
     for copy in copies:
         copy.wait()
 
@@ -422,26 +429,28 @@
         ],
         pl.CostEstimate(flops=0, bytes_accessed=0, transcendentals=0),
     )
-    (esp_matrix,) = call(
-        functools.partial(potential_kernel, tiles),
-        [floats(frag_dev, rows, basis)],
-        (charges, places, *parts, intersection),
+    inputs = (charges, places, *parts, intersection)
+    done = frag_dev // 2
+    rest = frag_dev - done
+    (esp_rows,) = call(
+        first_esp_kernel,
+        [floats(done, rows, basis)],
+        inputs,
         [VMEM] * 7,
+        [pltpu.VMEM((done, near, basis), jnp.float32), pltpu.VMEM((done, far, LANES), jnp.float32)],
+        pl.CostEstimate(flops=0, bytes_accessed=0, transcendentals=0),
+    )
+    density, esp_matrix = call(
+        functools.partial(last_esp_kernel, tiles),
+        [floats(frag_dev, rows, basis)] * 2,
+        (*inputs, esp_rows, *moved),
+        [VMEM] * (8 + tiles),
         [
-            pltpu.VMEM((frag_dev, near, basis), jnp.float32),
-            pltpu.VMEM((frag_dev, far, LANES), jnp.float32),
-            pltpu.VMEM((frag_dev, rows, basis), jnp.float32),
-            pltpu.SemaphoreType.DMA((tiles,)),
+            pltpu.VMEM((rest, rows, basis), jnp.float32),
+            pltpu.VMEM((rest, near, basis), jnp.float32),
+            pltpu.VMEM((rest, far, LANES), jnp.float32),
+            pltpu.SemaphoreType.DMA((tiles + 2,)),
         ],
-        pl.CostEstimate(flops=0, bytes_accessed=0, transcendentals=0),
-        HBM,
-    )
-    (density,) = call(
-        functools.partial(gather_kernel, tiles),
-        [floats(frag_dev, rows, basis)],
-        (*moved, pltpu.with_memory_space_constraint(esp_matrix, pltpu.HBM)),
-        [VMEM] * tiles + [HBM],
-        [pltpu.SemaphoreType.DMA((tiles,))],
         pl.CostEstimate(flops=0, bytes_accessed=0, transcendentals=0),
         HBM,
     )

time: 35.4 us -> 33.8 us (0.955)
  Pallas kernels: 14.6 us -> 13 us
    pallas_call x5, Pallas kernels: 14.6 us -> 13 us  [call(): pl.pallas_call(kernel, out_shape=outs, in_specs=specs, out_specs=[out_spe...]
  transfers between devices with their start and end apart: 9 -> 9, of which waited for: 1 -> 1; matrix products, arithmetic and copies ran while one was open for 0% -> 0% of each run, Pallas kernels for 34% -> 27%
where the time goes in v5:
time: 33.8 us; the launch traced here: 33.6 us
  starting transfers between devices  15.2 us (45%)
  Pallas kernels  13 us (38%)
  waiting for transfers between devices  4.69 us (14%)
  between operations  0.73 us (2%)
    pallas_call x5, Pallas kernels, call(): pl.pallas_call(kernel, out_shape=outs, in_specs=specs, out_specs=[out_spe...  13 us
    ppermute x2, starting transfers between devices, neighbours(): found.append(lax.ppermute(x, axis, ups + [(j, i) for i, j in ups]))  5.24 us
    ppermute x6, starting transfers between devices, exchanged(): moved.append(lax.ppermute(chunks[shift], 'tile', pairs))  5.15 us
    all_to_all x1, starting transfers between devices, per_device(): lax.all_to_all(charges, ('frag', 'tile'), split_axis=0, concat_axis=0, ti...  4.76 us
    all_to_all x1, waiting for transfers between devices, per_device(): lax.all_to_all(charges, ('frag', 'tile'), split_axis=0, concat_axis=0, ti...  4.67 us
  transfers between devices with their start and end apart: 9, of which 1 were waited for; matrix products, arithmetic and copies ran while one was open for 0% of the time, Pallas kernels for 27%

profile of v5, /device:TPU:0, one launch (start us, length us, event | category | flops | bytes accessed | tf_op | source)
XLA Modules:
  0.0 33.6 jit_solution(15871435792348262896)
XLA Ops:
  0.6 0.0 copy-start.1
  0.6 1.7 %shard_map.113 = (f32[2,2,64,256]{3,2,1,0:T(8,128)S(1)}, f32[2,2,64,256]{3,2,1,0:T(8,128)S(1)}, f32[2,72,128]{2,1,0:T(8,128)S(1)}, f32[2,72,128]{2,1,0:T(8,128)S(1)}, f32[6,256]{1,0:T(8,128)S(1)}) custom-call(s32[8]{0:T(128)} %refs_0_.1, f32[8,256]{1,0:T(8,128)} %refs_1_.1, f32[8,256]{1,0:T(8,128)} %refs_2_.1, f32[8,256]{1,0:T(8,128)} %refs_3_.1, ...), custom_call_target="tpu_custom_call" | custom-call | tf_op jit(solution)/shard_map/pallas_call | solution.py:339
  2.4 0.5 %collective-permute-start = (f32[2,2,64,256]{3,2,1,0:T(8,128)S(1)}, f32[2,2,64,256]{3,2,1,0:T(8,128)S(1)}, u32[]{:S(2)}, u32[]{:S(2)}) collective-permute-start(f32[2,2,64,256]{3,2,1,0:T(8,128)S(1)} %get-tuple-element.22), channel_id=1, source_target_pairs={{0,1},{1,0},{2,3},{3,2},{4,5},{5,4},{6,7},{7,6},{8,9},{9,8},{10,11... | collective-permute-start | bytes 786440 | tf_op jit(solution)/shard_map/ppermute | solution.py:359
  2.9 2.6 %collective-permute-start.1 = (f32[2,72,128]{2,1,0:T(8,128)S(1)}, f32[2,72,128]{2,1,0:T(8,128)S(1)}, u32[]{:S(2)}, u32[]{:S(2)}) collective-permute-start(f32[2,72,128]{2,1,0:T(8,128)S(1)} %get-tuple-element.23), channel_id=1, source_target_pairs={{0,2},{1,3},{2,0},{3,1},{4,6},{5,7},{6,4},{7,5},{8,10},{9,11},{10,... | collective-permute-start | bytes 221192 | tf_op jit(solution)/shard_map/ppermute | solution.py:359
  5.5 0.1 collective-permute-start.2
  5.5 0.0 copy-done.1
  5.5 0.7 %collective-permute-start.4 = (f32[3,8,256]{2,1,0:T(8,128)S(1)}, f32[3,8,256]{2,1,0:T(8,128)S(1)}, u32[]{:S(2)}, u32[]{:S(2)}) collective-permute-start(f32[3,8,256]{2,1,0:T(8,128)S(1)} %bitcast.2), channel_id=1, source_target_pairs={{4,8},{12,16},{20,24},{8,4},{16,12},{24,20},{5,9},{13,17},{21,25},... | collective-permute-start | bytes 73736 | tf_op jit(solution)/shard_map/ppermute | solution.py:369
  6.2 4.6 %collective-permute-start.3 = (f32[3,8,256]{2,1,0:T(8,128)S(1)}, f32[3,8,256]{2,1,0:T(8,128)S(1)}, u32[]{:S(2)}, u32[]{:S(2)}) collective-permute-start(f32[3,8,256]{2,1,0:T(8,128)S(1)} %bitcast.3), channel_id=1, source_target_pairs={{0,4},{8,12},{16,20},{24,28},{4,0},{12,8},{20,16},{28,24},{1,5},{9... | collective-permute-start | bytes 73736 | tf_op jit(solution)/shard_map/ppermute | solution.py:369
  10.8 0.0 collective-permute-done.1.refs_2_
  10.8 0.0 collective-permute-done.2.refs_3_
  10.8 0.0 collective-permute-done.refs_1_
  10.8 0.0 copy-start
  10.8 6.2 %shard_map.114 = (f32[2,64,256]{2,1,0:T(8,128)S(1)}, f32[2,64,256]{2,1,0:T(8,128)S(1)}, f32[2,64,256]{2,1,0:T(8,128)S(1)}, f32[2,64,256]{2,1,0:T(8,128)S(1)}, f32[32,2,384]{2,1,0:T(2,128)}) custom-call(f32[6,256]{1,0:T(8,128)S(1)} %get-tuple-element.20.facts_ref, f32[2,2,64,256]{3,2,1,0:T(8,128)S(1)} %get-tuple-element.21.refs_0_, ...), custom_call_target="tpu_custom_call" | custom-call | tf_op jit(solution)/shard_map/pallas_call | solution.py:339
  17.0 0.0 collective-permute-done.4.refs_2_
  17.0 0.0 collective-permute-done.3.refs_1_
  17.0 0.0 copy-start.3
  17.0 4.8 %all-to-all-start = ((f32[32,2,384]{2,1,0:T(2,128)}), f32[32,2,384]{2,1,0:T(2,128)S(1)}, u32[]{:S(2)}, u32[]{:S(2)}) async-start(f32[32,2,384]{2,1,0:T(2,128)} %get-tuple-element.26), calls=%async_computation | async-start | bytes 196608 | tf_op jit(solution)/shard_map/all_to_all | solution.py:414
  21.8 0.0 copy-start.2
  21.8 0.3 collective-permute-start.5
  22.1 1.7 %collective-permute-start.6 = (f32[2,64,256]{2,1,0:T(8,128)S(1)}, f32[2,64,256]{2,1,0:T(8,128)S(1)}, u32[]{:S(2)}, u32[]{:S(2)}) collective-permute-start(f32[2,64,256]{2,1,0:T(8,128)S(1)} %get-tuple-element.36), channel_id=1, source_target_pairs={{0,2},{1,3},{2,0},{3,1},{4,6},{5,7},{6,4},{7,5},{8,10},{9,11},{10,... | collective-permute-start | bytes 393224 | tf_op jit(solution)/shard_map/ppermute | solution.py:359
  23.8 0.0 collective-permute-start.7
  23.8 0.0 copy-done.3
  23.8 0.0 copy-done.2
  23.8 1.1 %shard_map.115 = (bf16[8,32,256]{2,1,0:T(8,128)(2,1)S(1)}, bf16[8,8,32,256]{3,2,1,0:T(8,128)(2,1)S(1)}, f32[8,8,64]{2,1,0:T(8,128)S(1)}, f32[8,8,64]{2,1,0:T(8,128)S(1)}) custom-call(s32[8,8]{1,0:T(8,128)S(1)} %copy-done.2, s32[8,8]{1,0:T(8,128)S(1)} %copy-done.3, f32[3,8,256]{2,1,0:T(8,128)S(1)} %bitcast.4, f32[3,8,256]{2,1,0:T(8,128)S(1)} %bitcast.5, ...), custom_call_target="tpu_custom_call" | custom-call | tf_op jit(solution)/shard_map/pallas_call | solution.py:339
  24.9 4.7 %all-to-all-done.refs_0_ = f32[32,2,384]{2,1,0:T(2,128)S(1)} async-done(((f32[32,2,384]{2,1,0:T(2,128)}), f32[32,2,384]{2,1,0:T(2,128)S(1)}, u32[]{:S(2)}, u32[]{:S(2)}) %all-to-all-start) | async-done | bytes 98336 | tf_op jit(solution)/shard_map/all_to_all | solution.py:414
  29.6 0.0 copy-done
  29.6 1.6 %shard_map.116.refs_7_ = f32[4,64,256]{2,1,0:T(8,128)S(1)} custom-call(f32[32,2,384]{2,1,0:T(2,128)S(1)} %all-to-all-done.refs_0_, f32[3,8,256]{2,1,0:T(8,128)S(1)} %bitcast.6, bf16[8,32,256]{2,1,0:T(8,128)(2,1)S(1)} %get-tuple-element.31.refs_2_, bf16[8,8,32,256]{3,2,1,0:T(8,128)(2,1)S(1)} %get-tuple-element.32.refs_3_, ...), custom_call_target="tpu_custom_call" | custom-call | tf_op jit(solution)/shard_map/pallas_call | solution.py:339
  31.2 0.0 collective-permute-done.5.refs_9_
  31.2 0.0 collective-permute-done.6.refs_10_
  31.2 0.0 collective-permute-done.7.refs_11_
  31.2 2.4 %shard_map.117 = (f32[8,64,256]{2,1,0:T(8,128)}, f32[8,64,256]{2,1,0:T(8,128)}) custom-call(f32[32,2,384]{2,1,0:T(2,128)S(1)} %all-to-all-done.refs_0_, f32[3,8,256]{2,1,0:T(8,128)S(1)} %bitcast.7, bf16[8,32,256]{2,1,0:T(8,128)(2,1)S(1)} %get-tuple-element.31.refs_2_, bf16[8,8,32,256]{3,2,1,0:T(8,128)(2,1)S(1)} %get-tuple-element.32.refs_3_, ...), custom_call_target="tpu_custom_call" | custom-call | tf_op jit(solution)/shard_map/pallas_call | solution.py:339
Async XLA Ops:
  0.6 4.9 %copy-start.1 = (f32[8,3,256]{2,0,1:T(8,128)S(1)}, f32[8,3,256]{2,0,1:T(8,128)}, u32[]{:S(2)}) copy-start(f32[8,3,256]{2,0,1:T(8,128)} %param.16) | copy-start | bytes 73732
  2.4 8.4 %collective-permute-start = (f32[2,2,64,256]{3,2,1,0:T(8,128)S(1)}, f32[2,2,64,256]{3,2,1,0:T(8,128)S(1)}, u32[]{:S(2)}, u32[]{:S(2)}) collective-permute-start(f32[2,2,64,256]{3,2,1,0:T(8,128)S(1)} %get-tuple-element.22), channel_id=1, source_target_pairs={{0,1},{1,0},{2,3},{3,2},{4,5},{5,4},{6,7},{7,6},{8,9},{9,8},{10,11... | collective-permute-start | bytes 786440 | tf_op jit(solution)/shard_map/ppermute | solution.py:359
  2.9 7.9 %collective-permute-start.1 = (f32[2,72,128]{2,1,0:T(8,128)S(1)}, f32[2,72,128]{2,1,0:T(8,128)S(1)}, u32[]{:S(2)}, u32[]{:S(2)}) collective-permute-start(f32[2,72,128]{2,1,0:T(8,128)S(1)} %get-tuple-element.23), channel_id=1, source_target_pairs={{0,2},{1,3},{2,0},{3,1},{4,6},{5,7},{6,4},{7,5},{8,10},{9,11},{10,... | collective-permute-start | bytes 221192 | tf_op jit(solution)/shard_map/ppermute | solution.py:359
  5.5 5.3 %collective-permute-start.2 = (f32[2,72,128]{2,1,0:T(8,128)S(1)}, f32[2,72,128]{2,1,0:T(8,128)S(1)}, u32[]{:S(2)}, u32[]{:S(2)}) collective-permute-start(f32[2,72,128]{2,1,0:T(8,128)S(1)} %get-tuple-element.24), channel_id=1, source_target_pairs={{0,3},{1,2},{2,1},{3,0},{4,7},{5,6},{6,5},{7,4},{8,11},{9,10},{10,... | collective-permute-start | bytes 221192 | tf_op jit(solution)/shard_map/ppermute | solution.py:359
  5.5 11.5 %collective-permute-start.4 = (f32[3,8,256]{2,1,0:T(8,128)S(1)}, f32[3,8,256]{2,1,0:T(8,128)S(1)}, u32[]{:S(2)}, u32[]{:S(2)}) collective-permute-start(f32[3,8,256]{2,1,0:T(8,128)S(1)} %bitcast.2), channel_id=1, source_target_pairs={{4,8},{12,16},{20,24},{8,4},{16,12},{24,20},{5,9},{13,17},{21,25},... | collective-permute-start | bytes 73736 | tf_op jit(solution)/shard_map/ppermute | solution.py:369
  6.2 10.8 %collective-permute-start.3 = (f32[3,8,256]{2,1,0:T(8,128)S(1)}, f32[3,8,256]{2,1,0:T(8,128)S(1)}, u32[]{:S(2)}, u32[]{:S(2)}) collective-permute-start(f32[3,8,256]{2,1,0:T(8,128)S(1)} %bitcast.3), channel_id=1, source_target_pairs={{0,4},{8,12},{16,20},{24,28},{4,0},{12,8},{20,16},{28,24},{1,5},{9... | collective-permute-start | bytes 73736 | tf_op jit(solution)/shard_map/ppermute | solution.py:369
  10.8 18.8 %copy-start = (f32[8,64,256]{2,1,0:T(8,128)S(1)}, f32[8,64,256]{2,1,0:T(8,128)}, u32[]{:S(2)}) copy-start(f32[8,64,256]{2,1,0:T(8,128)} %refs_6_.5) | copy-start | bytes 1572868
  17.0 6.8 %copy-start.3 = (s32[8,8]{1,0:T(8,128)S(1)}, s32[8,8]{1,0:T(8,128)}, u32[]{:S(2)}) copy-start(s32[8,8]{1,0:T(8,128)} %far_ref.1) | copy-start | bytes 772
  17.0 12.6 %all-to-all-start = ((f32[32,2,384]{2,1,0:T(2,128)}), f32[32,2,384]{2,1,0:T(2,128)S(1)}, u32[]{:S(2)}, u32[]{:S(2)}) async-start(f32[32,2,384]{2,1,0:T(2,128)} %get-tuple-element.26), calls=%async_computation | async-start | bytes 196608 | tf_op jit(solution)/shard_map/all_to_all | solution.py:414
  21.8 2.0 %copy-start.2 = (s32[8,8]{1,0:T(8,128)S(1)}, s32[8,8]{1,0:T(8,128)}, u32[]{:S(2)}) copy-start(s32[8,8]{1,0:T(8,128)} %near_ref.1) | copy-start | bytes 772
  21.8 9.4 %collective-permute-start.5 = (f32[2,64,256]{2,1,0:T(8,128)S(1)}, f32[2,64,256]{2,1,0:T(8,128)S(1)}, u32[]{:S(2)}, u32[]{:S(2)}) collective-permute-start(f32[2,64,256]{2,1,0:T(8,128)S(1)} %get-tuple-element.35), channel_id=1, source_target_pairs={{0,1},{1,0},{2,3},{3,2},{4,5},{5,4},{6,7},{7,6},{8,9},{9,8},{10,11... | collective-permute-start | bytes 393224 | tf_op jit(solution)/shard_map/ppermute | solution.py:359
  22.1 9.1 %collective-permute-start.6 = (f32[2,64,256]{2,1,0:T(8,128)S(1)}, f32[2,64,256]{2,1,0:T(8,128)S(1)}, u32[]{:S(2)}, u32[]{:S(2)}) collective-permute-start(f32[2,64,256]{2,1,0:T(8,128)S(1)} %get-tuple-element.36), channel_id=1, source_target_pairs={{0,2},{1,3},{2,0},{3,1},{4,6},{5,7},{6,4},{7,5},{8,10},{9,11},{10,... | collective-permute-start | bytes 393224 | tf_op jit(solution)/shard_map/ppermute | solution.py:359
  23.8 7.4 %collective-permute-start.7 = (f32[2,64,256]{2,1,0:T(8,128)S(1)}, f32[2,64,256]{2,1,0:T(8,128)S(1)}, u32[]{:S(2)}, u32[]{:S(2)}) collective-permute-start(f32[2,64,256]{2,1,0:T(8,128)S(1)} %get-tuple-element.37), channel_id=1, source_target_pairs={{0,3},{1,2},{2,1},{3,0},{4,7},{5,6},{6,5},{7,4},{8,11},{9,10},{10,... | collective-permute-start | bytes 393224 | tf_op jit(solution)/shard_map/ppermute | solution.py:359

commit v6 on v5

--- a/solution.py
+++ b/solution.py
@@ -131,8 +131,9 @@
 
 def split(x):
     high = x.astype(jnp.bfloat16)
-    low = x - high.astype(jnp.float32)
-    return high, (x * WHOLE_SCALE).astype(COARSE), (low * REST_SCALE).astype(COARSE)
+    rest = (x - high.astype(jnp.float32)).astype(jnp.bfloat16)
+    coarse = (high * jnp.bfloat16(WHOLE_SCALE)).astype(COARSE)
+    return high, coarse, (rest * jnp.bfloat16(REST_SCALE)).astype(COARSE)
 
 
 def product(left, right):
@@ -430,7 +431,7 @@
         pl.CostEstimate(flops=0, bytes_accessed=0, transcendentals=0),
     )
     inputs = (charges, places, *parts, intersection)
-    done = frag_dev // 2
+    done = frag_dev * 3 // 4
     rest = frag_dev - done
     (esp_rows,) = call(
         first_esp_kernel,

time: 33.8 us -> 33.5 us (level)
    pallas_call x5, Pallas kernels: 13 us -> 12.7 us  [call(): pl.pallas_call(kernel, out_shape=outs, in_specs=specs, out_specs=[out_spe...]
  transfers between devices with their start and end apart: 9 -> 9, of which waited for: 1 -> 1; matrix products, arithmetic and copies ran while one was open for 0% -> 0% of each run, Pallas kernels for 27% -> 28%
where the time goes in v6:
time: 33.5 us; the launch traced here: 33.3 us
  starting transfers between devices  15.2 us (45%)
  Pallas kernels  12.7 us (38%)
  waiting for transfers between devices  4.69 us (14%)
  between operations  0.73 us (2%)
    pallas_call x5, Pallas kernels, call(): pl.pallas_call(kernel, out_shape=outs, in_specs=specs, out_specs=[out_spe...  12.7 us
    ppermute x2, starting transfers between devices, neighbours(): found.append(lax.ppermute(x, axis, ups + [(j, i) for i, j in ups]))  5.24 us
    ppermute x6, starting transfers between devices, exchanged(): moved.append(lax.ppermute(chunks[shift], 'tile', pairs))  5.15 us
    all_to_all x1, starting transfers between devices, per_device(): lax.all_to_all(charges, ('frag', 'tile'), split_axis=0, concat_axis=0, ti...  4.76 us
    all_to_all x1, waiting for transfers between devices, per_device(): lax.all_to_all(charges, ('frag', 'tile'), split_axis=0, concat_axis=0, ti...  4.67 us
  transfers between devices with their start and end apart: 9, of which 1 were waited for; matrix products, arithmetic and copies ran while one was open for 0% of the time, Pallas kernels for 28%

profile of v6, /device:TPU:0, one launch (start us, length us, event | category | flops | bytes accessed | tf_op | source)
XLA Modules:
  0.0 33.3 jit_solution(305229223425998026)
XLA Ops:
  0.6 0.0 copy-start.1
  0.6 1.7 %shard_map.113 = (f32[2,2,64,256]{3,2,1,0:T(8,128)S(1)}, f32[2,2,64,256]{3,2,1,0:T(8,128)S(1)}, f32[2,72,128]{2,1,0:T(8,128)S(1)}, f32[2,72,128]{2,1,0:T(8,128)S(1)}, f32[6,256]{1,0:T(8,128)S(1)}) custom-call(s32[8]{0:T(128)} %refs_0_.1, f32[8,256]{1,0:T(8,128)} %refs_1_.1, f32[8,256]{1,0:T(8,128)} %refs_2_.1, f32[8,256]{1,0:T(8,128)} %refs_3_.1, ...), custom_call_target="tpu_custom_call" | custom-call | tf_op jit(solution)/shard_map/pallas_call | solution.py:340
  2.4 0.5 %collective-permute-start = (f32[2,2,64,256]{3,2,1,0:T(8,128)S(1)}, f32[2,2,64,256]{3,2,1,0:T(8,128)S(1)}, u32[]{:S(2)}, u32[]{:S(2)}) collective-permute-start(f32[2,2,64,256]{3,2,1,0:T(8,128)S(1)} %get-tuple-element.22), channel_id=1, source_target_pairs={{0,1},{1,0},{2,3},{3,2},{4,5},{5,4},{6,7},{7,6},{8,9},{9,8},{10,11... | collective-permute-start | bytes 786440 | tf_op jit(solution)/shard_map/ppermute | solution.py:360
  2.9 2.6 %collective-permute-start.1 = (f32[2,72,128]{2,1,0:T(8,128)S(1)}, f32[2,72,128]{2,1,0:T(8,128)S(1)}, u32[]{:S(2)}, u32[]{:S(2)}) collective-permute-start(f32[2,72,128]{2,1,0:T(8,128)S(1)} %get-tuple-element.23), channel_id=1, source_target_pairs={{0,2},{1,3},{2,0},{3,1},{4,6},{5,7},{6,4},{7,5},{8,10},{9,11},{10,... | collective-permute-start | bytes 221192 | tf_op jit(solution)/shard_map/ppermute | solution.py:360
  5.5 0.1 collective-permute-start.2
  5.5 0.0 copy-done.1
  5.5 0.7 %collective-permute-start.4 = (f32[3,8,256]{2,1,0:T(8,128)S(1)}, f32[3,8,256]{2,1,0:T(8,128)S(1)}, u32[]{:S(2)}, u32[]{:S(2)}) collective-permute-start(f32[3,8,256]{2,1,0:T(8,128)S(1)} %bitcast.2), channel_id=1, source_target_pairs={{4,8},{12,16},{20,24},{8,4},{16,12},{24,20},{5,9},{13,17},{21,25},... | collective-permute-start | bytes 73736 | tf_op jit(solution)/shard_map/ppermute | solution.py:370
  6.2 4.6 %collective-permute-start.3 = (f32[3,8,256]{2,1,0:T(8,128)S(1)}, f32[3,8,256]{2,1,0:T(8,128)S(1)}, u32[]{:S(2)}, u32[]{:S(2)}) collective-permute-start(f32[3,8,256]{2,1,0:T(8,128)S(1)} %bitcast.3), channel_id=1, source_target_pairs={{0,4},{8,12},{16,20},{24,28},{4,0},{12,8},{20,16},{28,24},{1,5},{9... | collective-permute-start | bytes 73736 | tf_op jit(solution)/shard_map/ppermute | solution.py:370
  10.8 0.0 collective-permute-done.1.refs_2_
  10.8 0.0 collective-permute-done.2.refs_3_
  10.8 0.0 collective-permute-done.refs_1_
  10.8 0.0 copy-start
  10.8 5.8 %shard_map.114 = (f32[2,64,256]{2,1,0:T(8,128)S(1)}, f32[2,64,256]{2,1,0:T(8,128)S(1)}, f32[2,64,256]{2,1,0:T(8,128)S(1)}, f32[2,64,256]{2,1,0:T(8,128)S(1)}, f32[32,2,384]{2,1,0:T(2,128)}) custom-call(f32[6,256]{1,0:T(8,128)S(1)} %get-tuple-element.20.facts_ref, f32[2,2,64,256]{3,2,1,0:T(8,128)S(1)} %get-tuple-element.21.refs_0_, ...), custom_call_target="tpu_custom_call" | custom-call | tf_op jit(solution)/shard_map/pallas_call | solution.py:340
  16.6 0.0 collective-permute-done.4.refs_2_
  16.6 0.0 collective-permute-done.3.refs_1_
  16.6 0.0 copy-start.3
  16.6 4.8 %all-to-all-start = ((f32[32,2,384]{2,1,0:T(2,128)}), f32[32,2,384]{2,1,0:T(2,128)S(1)}, u32[]{:S(2)}, u32[]{:S(2)}) async-start(f32[32,2,384]{2,1,0:T(2,128)} %get-tuple-element.26), calls=%async_computation | async-start | bytes 196608 | tf_op jit(solution)/shard_map/all_to_all | solution.py:415
  21.4 0.0 copy-start.2
  21.4 0.3 collective-permute-start.5
  21.7 1.7 %collective-permute-start.6 = (f32[2,64,256]{2,1,0:T(8,128)S(1)}, f32[2,64,256]{2,1,0:T(8,128)S(1)}, u32[]{:S(2)}, u32[]{:S(2)}) collective-permute-start(f32[2,64,256]{2,1,0:T(8,128)S(1)} %get-tuple-element.36), channel_id=1, source_target_pairs={{0,2},{1,3},{2,0},{3,1},{4,6},{5,7},{6,4},{7,5},{8,10},{9,11},{10,... | collective-permute-start | bytes 393224 | tf_op jit(solution)/shard_map/ppermute | solution.py:360
  23.4 0.0 collective-permute-start.7
  23.4 0.0 copy-done.3
  23.4 0.0 copy-done.2
  23.4 1.1 %shard_map.115 = (bf16[8,32,256]{2,1,0:T(8,128)(2,1)S(1)}, bf16[8,8,32,256]{3,2,1,0:T(8,128)(2,1)S(1)}, f32[8,8,64]{2,1,0:T(8,128)S(1)}, f32[8,8,64]{2,1,0:T(8,128)S(1)}) custom-call(s32[8,8]{1,0:T(8,128)S(1)} %copy-done.2, s32[8,8]{1,0:T(8,128)S(1)} %copy-done.3, f32[3,8,256]{2,1,0:T(8,128)S(1)} %bitcast.4, f32[3,8,256]{2,1,0:T(8,128)S(1)} %bitcast.5, ...), custom_call_target="tpu_custom_call" | custom-call | tf_op jit(solution)/shard_map/pallas_call | solution.py:340
  24.6 4.7 %all-to-all-done.refs_0_ = f32[32,2,384]{2,1,0:T(2,128)S(1)} async-done(((f32[32,2,384]{2,1,0:T(2,128)}), f32[32,2,384]{2,1,0:T(2,128)S(1)}, u32[]{:S(2)}, u32[]{:S(2)}) %all-to-all-start) | async-done | bytes 98336 | tf_op jit(solution)/shard_map/all_to_all | solution.py:415
  29.2 0.0 copy-done
  29.2 2.3 %shard_map.116.refs_7_ = f32[6,64,256]{2,1,0:T(8,128)S(1)} custom-call(f32[32,2,384]{2,1,0:T(2,128)S(1)} %all-to-all-done.refs_0_, f32[3,8,256]{2,1,0:T(8,128)S(1)} %bitcast.6, bf16[8,32,256]{2,1,0:T(8,128)(2,1)S(1)} %get-tuple-element.31.refs_2_, bf16[8,8,32,256]{3,2,1,0:T(8,128)(2,1)S(1)} %get-tuple-element.32.refs_3_, ...), custom_call_target="tpu_custom_call" | custom-call | tf_op jit(solution)/shard_map/pallas_call | solution.py:340
  31.5 0.0 collective-permute-done.5.refs_9_
  31.6 0.0 collective-permute-done.6.refs_10_
  31.6 0.0 collective-permute-done.7.refs_11_
  31.6 1.7 %shard_map.117 = (f32[8,64,256]{2,1,0:T(8,128)}, f32[8,64,256]{2,1,0:T(8,128)}) custom-call(f32[32,2,384]{2,1,0:T(2,128)S(1)} %all-to-all-done.refs_0_, f32[3,8,256]{2,1,0:T(8,128)S(1)} %bitcast.7, bf16[8,32,256]{2,1,0:T(8,128)(2,1)S(1)} %get-tuple-element.31.refs_2_, bf16[8,8,32,256]{3,2,1,0:T(8,128)(2,1)S(1)} %get-tuple-element.32.refs_3_, ...), custom_call_target="tpu_custom_call" | custom-call | tf_op jit(solution)/shard_map/pallas_call | solution.py:340
Async XLA Ops:
  0.6 4.9 %copy-start.1 = (f32[8,3,256]{2,0,1:T(8,128)S(1)}, f32[8,3,256]{2,0,1:T(8,128)}, u32[]{:S(2)}) copy-start(f32[8,3,256]{2,0,1:T(8,128)} %param.16) | copy-start | bytes 73732
  2.4 8.4 %collective-permute-start = (f32[2,2,64,256]{3,2,1,0:T(8,128)S(1)}, f32[2,2,64,256]{3,2,1,0:T(8,128)S(1)}, u32[]{:S(2)}, u32[]{:S(2)}) collective-permute-start(f32[2,2,64,256]{3,2,1,0:T(8,128)S(1)} %get-tuple-element.22), channel_id=1, source_target_pairs={{0,1},{1,0},{2,3},{3,2},{4,5},{5,4},{6,7},{7,6},{8,9},{9,8},{10,11... | collective-permute-start | bytes 786440 | tf_op jit(solution)/shard_map/ppermute | solution.py:360
  2.9 7.9 %collective-permute-start.1 = (f32[2,72,128]{2,1,0:T(8,128)S(1)}, f32[2,72,128]{2,1,0:T(8,128)S(1)}, u32[]{:S(2)}, u32[]{:S(2)}) collective-permute-start(f32[2,72,128]{2,1,0:T(8,128)S(1)} %get-tuple-element.23), channel_id=1, source_target_pairs={{0,2},{1,3},{2,0},{3,1},{4,6},{5,7},{6,4},{7,5},{8,10},{9,11},{10,... | collective-permute-start | bytes 221192 | tf_op jit(solution)/shard_map/ppermute | solution.py:360
  5.5 5.3 %collective-permute-start.2 = (f32[2,72,128]{2,1,0:T(8,128)S(1)}, f32[2,72,128]{2,1,0:T(8,128)S(1)}, u32[]{:S(2)}, u32[]{:S(2)}) collective-permute-start(f32[2,72,128]{2,1,0:T(8,128)S(1)} %get-tuple-element.24), channel_id=1, source_target_pairs={{0,3},{1,2},{2,1},{3,0},{4,7},{5,6},{6,5},{7,4},{8,11},{9,10},{10,... | collective-permute-start | bytes 221192 | tf_op jit(solution)/shard_map/ppermute | solution.py:360
  5.5 11.1 %collective-permute-start.4 = (f32[3,8,256]{2,1,0:T(8,128)S(1)}, f32[3,8,256]{2,1,0:T(8,128)S(1)}, u32[]{:S(2)}, u32[]{:S(2)}) collective-permute-start(f32[3,8,256]{2,1,0:T(8,128)S(1)} %bitcast.2), channel_id=1, source_target_pairs={{4,8},{12,16},{20,24},{8,4},{16,12},{24,20},{5,9},{13,17},{21,25},... | collective-permute-start | bytes 73736 | tf_op jit(solution)/shard_map/ppermute | solution.py:370
  6.2 10.5 %collective-permute-start.3 = (f32[3,8,256]{2,1,0:T(8,128)S(1)}, f32[3,8,256]{2,1,0:T(8,128)S(1)}, u32[]{:S(2)}, u32[]{:S(2)}) collective-permute-start(f32[3,8,256]{2,1,0:T(8,128)S(1)} %bitcast.3), channel_id=1, source_target_pairs={{0,4},{8,12},{16,20},{24,28},{4,0},{12,8},{20,16},{28,24},{1,5},{9... | collective-permute-start | bytes 73736 | tf_op jit(solution)/shard_map/ppermute | solution.py:370
  10.8 18.5 %copy-start = (f32[8,64,256]{2,1,0:T(8,128)S(1)}, f32[8,64,256]{2,1,0:T(8,128)}, u32[]{:S(2)}) copy-start(f32[8,64,256]{2,1,0:T(8,128)} %refs_6_.5) | copy-start | bytes 1572868
  16.6 6.8 %copy-start.3 = (s32[8,8]{1,0:T(8,128)S(1)}, s32[8,8]{1,0:T(8,128)}, u32[]{:S(2)}) copy-start(s32[8,8]{1,0:T(8,128)} %far_ref.1) | copy-start | bytes 772
  16.6 12.6 %all-to-all-start = ((f32[32,2,384]{2,1,0:T(2,128)}), f32[32,2,384]{2,1,0:T(2,128)S(1)}, u32[]{:S(2)}, u32[]{:S(2)}) async-start(f32[32,2,384]{2,1,0:T(2,128)} %get-tuple-element.26), calls=%async_computation | async-start | bytes 196608 | tf_op jit(solution)/shard_map/all_to_all | solution.py:415
  21.4 2.0 %copy-start.2 = (s32[8,8]{1,0:T(8,128)S(1)}, s32[8,8]{1,0:T(8,128)}, u32[]{:S(2)}) copy-start(s32[8,8]{1,0:T(8,128)} %near_ref.1) | copy-start | bytes 772
  21.4 10.1 %collective-permute-start.5 = (f32[2,64,256]{2,1,0:T(8,128)S(1)}, f32[2,64,256]{2,1,0:T(8,128)S(1)}, u32[]{:S(2)}, u32[]{:S(2)}) collective-permute-start(f32[2,64,256]{2,1,0:T(8,128)S(1)} %get-tuple-element.35), channel_id=1, source_target_pairs={{0,1},{1,0},{2,3},{3,2},{4,5},{5,4},{6,7},{7,6},{8,9},{9,8},{10,11... | collective-permute-start | bytes 393224 | tf_op jit(solution)/shard_map/ppermute | solution.py:360
  21.7 9.8 %collective-permute-start.6 = (f32[2,64,256]{2,1,0:T(8,128)S(1)}, f32[2,64,256]{2,1,0:T(8,128)S(1)}, u32[]{:S(2)}, u32[]{:S(2)}) collective-permute-start(f32[2,64,256]{2,1,0:T(8,128)S(1)} %get-tuple-element.36), channel_id=1, source_target_pairs={{0,2},{1,3},{2,0},{3,1},{4,6},{5,7},{6,4},{7,5},{8,10},{9,11},{10,... | collective-permute-start | bytes 393224 | tf_op jit(solution)/shard_map/ppermute | solution.py:360
  23.4 8.1 %collective-permute-start.7 = (f32[2,64,256]{2,1,0:T(8,128)S(1)}, f32[2,64,256]{2,1,0:T(8,128)S(1)}, u32[]{:S(2)}, u32[]{:S(2)}) collective-permute-start(f32[2,64,256]{2,1,0:T(8,128)S(1)} %get-tuple-element.37), channel_id=1, source_target_pairs={{0,3},{1,2},{2,1},{3,0},{4,7},{5,6},{6,5},{7,4},{8,11},{9,10},{10,... | collective-permute-start | bytes 393224 | tf_op jit(solution)/shard_map/ppermute | solution.py:360

commit v7 on v6

--- a/solution.py
+++ b/solution.py
@@ -257,8 +257,8 @@
     left_out[...] = side_ref[...].astype(jnp.bfloat16)
     fill(table_side, reach * frag_dev, sources[0], 1.0, 0.0, 1)
     for at in range(1, around):
-        step = (at + 1) // 2
-        side = lax.rem(frag_at // step + at + 1, 2)
+        step = (at - 1) % reach + 1
+        side = lax.rem(frag_at // step + lax.axis_index("tile") + (at - 1) // reach, 2)
         spot = reach + step * (1 - 2 * side)
         fill(table_side, spot * frag_dev, sources[at], 1.0, 0.0, 1)
     for frag in range(frag_dev):
@@ -270,21 +270,24 @@
             far_hot[frag, m : m + 1, :] = (lane == far_ref[frag, m]).astype(jnp.float32)
 
 
-def esp_rows_of(first, count, charge_ref, own_ref, left_ref, right_ref, near_hot, far_hot, over_ref, near_charge, far_block):
-    _, rows, basis = over_ref.shape
-    near, far = near_hot.shape[1], far_hot.shape[1]
-    pick = own_rows(rows, basis, lax.axis_index("tile") * rows)
+def gather_charges(charge_ref, near_hot, far_hot, near_charge, far_block):
+    basis = near_charge.shape[2]
     table = charge_ref[...].reshape(-1, basis + LANES)
     for hot, gathered, part in (
         (near_hot, near_charge, table[:, :basis]),
         (far_hot, far_block, table[:, basis:]),
     ):
-        every = hot[first : first + count].reshape(-1, hot.shape[2])
+        every = hot[...].reshape(-1, hot.shape[2])
         picked = jnp.dot(every, part, precision=lax.Precision.HIGHEST, preferred_element_type=jnp.float32)
         gathered[...] = picked.reshape(gathered.shape)
+
+
+def esp_rows_of(first, count, own_ref, left_ref, right_ref, over_ref, near_charge, far_block):
+    _, rows, basis = over_ref.shape
+    near, far = near_charge.shape[1], far_block.shape[1]
+    pick = own_rows(rows, basis, lax.axis_index("tile") * rows)
     quantities = [block_lanes(at) for at in range(4)]
-    for at in range(count):
-        frag = first + at
+    for frag in range(first, first + count):
         folded = jnp.zeros((basis, LANES), jnp.float32)
         for k in range(near):
             square = lax.dot_general(
@@ -293,13 +296,13 @@
                 (((0,), (0,)), ((), ())),
                 preferred_element_type=jnp.float32,
             )
-            terms = lax.rsqrt(square) * near_charge[at, k : k + 1, :]
+            terms = lax.rsqrt(square) * near_charge[frag, k : k + 1, :]
             for start in range(0, basis, LANES):
                 folded = folded + terms[:, start : start + LANES]
         blocks = jnp.zeros((PC, basis), jnp.float32)
         spots = [own_ref[axis, frag : frag + 1, :] for axis in range(3)]
         for m in range(far):
-            row = far_block[at, m : m + 1, :]
+            row = far_block[frag, m : m + 1, :]
             x, y, z, charge = [
                 jnp.sum(jnp.where(lanes, row, 0.0), axis=1, keepdims=True) for lanes in quantities
             ]
@@ -311,15 +314,16 @@
         yield frag, over_ref[frag] * (mine + potential)
 
 
-def first_esp_kernel(*refs):
-    inputs, esp_ref, scratch = refs[:7], refs[7], refs[8:]
-    for frag, rows in esp_rows_of(0, esp_ref.shape[0], *inputs, *scratch):
+def first_esp_kernel(charge_ref, near_hot, far_hot, *refs):
+    inputs, (esp_ref, near_charge, far_block) = refs[:4], refs[4:]
+    gather_charges(charge_ref, near_hot, far_hot, near_charge, far_block)
+    for frag, rows in esp_rows_of(0, esp_ref.shape[0], *inputs, near_charge, far_block):
         esp_ref[frag] = rows
 
 
 def last_esp_kernel(tiles, *refs):
-    inputs, done_ref, chunks = refs[:7], refs[7], refs[8 : 8 + tiles]
-    density_ref, esp_ref, rest_ref, near_charge, far_block, sems = refs[8 + tiles :]
+    inputs, done_ref, chunks = refs[:6], refs[6], refs[7 : 7 + tiles]
+    density_ref, esp_ref, rest_ref, sems = refs[7 + tiles :]
     share, done = chunks[0].shape[0], done_ref.shape[0]
     copies = [pltpu.make_async_copy(done_ref, esp_ref.at[pl.ds(0, done)], sems.at[tiles])]
     for shift in range(tiles):
@@ -328,7 +332,7 @@
     for copy in copies:
         copy.start()
     rest = rest_ref.shape[0]
-    for frag, rows in esp_rows_of(done, rest, *inputs, near_charge, far_block):
+    for frag, rows in esp_rows_of(done, rest, *inputs):
         rest_ref[frag - done] = rows
     copies.append(pltpu.make_async_copy(rest_ref, esp_ref.at[pl.ds(done, rest)], sems.at[tiles + 1]))
     copies[-1].start()
@@ -361,14 +365,22 @@
     return moved
 
 
-def neighbours(x, axis, reach):
-    peers = lax.axis_size(axis)
-    found = [x]
+def neighbours(x, reach):
+    peers, tiles = lax.axis_size("frag"), lax.axis_size("tile")
+    found = []
     for step in range(1, reach + 1):
-        for parity in range(2):
-            ups = [(i, i + step) for i in range(peers - step) if (i // step) % 2 == parity]
-            found.append(lax.ppermute(x, axis, ups + [(j, i) for i, j in ups]))
+        pairs = []
+        for low in range(peers - step):
+            for tile in range(low // step % 2, tiles, 2):
+                ends = low * tiles + tile, (low + step) * tiles + tile
+                pairs += [ends, ends[::-1]]
+        found.append(lax.ppermute(x, ("frag", "tile"), pairs))
     return found
+
+
+def from_next_tile(x):
+    tiles = lax.axis_size("tile")
+    return lax.ppermute(x, "tile", [(tile, tile ^ 1) for tile in range(tiles)])
 
 
 def per_device(
@@ -401,7 +413,7 @@
         + [pltpu.SemaphoreType.DMA((len(inputs),))],
     )
     sent = exchanged(sent)
-    sources = neighbours(places, "frag", -(-SPAN // frag_dev))
+    swaps = neighbours(places, -(-SPAN // frag_dev))
     *pieces, charges = call(
         functools.partial(density_kernel, tiles),
         [chunk] * tiles + [floats(devices, share, basis + LANES)],
@@ -411,7 +423,8 @@
         pl.CostEstimate(flops=0, bytes_accessed=0, transcendentals=0),
     )
     moved = exchanged(pieces)
-    charges, sources = lax.optimization_barrier((charges, sources))
+    charges, swaps = lax.optimization_barrier((charges, swaps))
+    sources = [places, *swaps, *[from_next_tile(x) for x in swaps]]
     charges = lax.all_to_all(charges, ("frag", "tile"), split_axis=0, concat_axis=0, tiled=True)
     near, far, frags = near_list.shape[1], far_list.shape[1], peers * frag_dev
     parts = call(
@@ -430,28 +443,23 @@
         ],
         pl.CostEstimate(flops=0, bytes_accessed=0, transcendentals=0),
     )
-    inputs = (charges, places, *parts, intersection)
+    left, right, near_hot, far_hot = parts
+    inputs = (places, left, right, intersection)
     done = frag_dev * 3 // 4
     rest = frag_dev - done
-    (esp_rows,) = call(
+    esp_rows, near_charge, far_block = call(
         first_esp_kernel,
-        [floats(done, rows, basis)],
-        inputs,
+        [floats(done, rows, basis), floats(frag_dev, near, basis), floats(frag_dev, far, LANES)],
+        (charges, near_hot, far_hot, *inputs),
         [VMEM] * 7,
-        [pltpu.VMEM((done, near, basis), jnp.float32), pltpu.VMEM((done, far, LANES), jnp.float32)],
-        pl.CostEstimate(flops=0, bytes_accessed=0, transcendentals=0),
+        cost=pl.CostEstimate(flops=0, bytes_accessed=0, transcendentals=0),
     )
     density, esp_matrix = call(
         functools.partial(last_esp_kernel, tiles),
         [floats(frag_dev, rows, basis)] * 2,
-        (*inputs, esp_rows, *moved),
-        [VMEM] * (8 + tiles),
-        [
-            pltpu.VMEM((rest, rows, basis), jnp.float32),
-            pltpu.VMEM((rest, near, basis), jnp.float32),
-            pltpu.VMEM((rest, far, LANES), jnp.float32),
-            pltpu.SemaphoreType.DMA((tiles + 2,)),
-        ],
+        (*inputs, near_charge, far_block, esp_rows, *moved),
+        [VMEM] * (7 + tiles),
+        [pltpu.VMEM((rest, rows, basis), jnp.float32), pltpu.SemaphoreType.DMA((tiles + 2,))],
         pl.CostEstimate(flops=0, bytes_accessed=0, transcendentals=0),
         HBM,
     )

time: 33.5 us -> 33.5 us (level)
    all_to_all x1, waiting for transfers between devices: 4.67 us -> 3.37 us  [per_device(): lax.all_to_all(charges, ('frag', 'tile'), split_axis=0, concat_axis=0, ti...]
    ppermute x2, starting transfers between devices: 5.24 us -> 4.11 us  [the longest x1 3.65 us: neighbours(): found.append(lax.ppermute(x, ('frag', 'tile'), pairs))]
    all_to_all x1, starting transfers between devices: 4.76 us -> 5.88 us  [per_device(): lax.all_to_all(charges, ('frag', 'tile'), split_axis=0, concat_axis=0, ti...]
    ppermute x2, waiting for transfers between devices: 0.01 us -> 0.85 us  [the longest x1 0.85 us: from_next_tile(): return lax.ppermute(x, 'tile', [(tile, tile ^ 1) for tile in range(tiles)])]
    ppermute x6, waiting for transfers between devices: 0.02 us -> 0.49 us  [exchanged(): moved.append(lax.ppermute(chunks[shift], 'tile', pairs))]
  transfers between devices with their start and end apart: 9 -> 9, of which waited for: 1 -> 3; matrix products, arithmetic and copies ran while one was open for 0% -> 0% of each run, Pallas kernels for 28% -> 28%
where the time goes in v7:
time: 33.5 us; the launch traced here: 33.2 us
  starting transfers between devices  15.1 us (45%)
  Pallas kernels  12.6 us (38%)
  waiting for transfers between devices  4.71 us (14%)
  between operations  0.73 us (2%)
    pallas_call x5, Pallas kernels, call(): pl.pallas_call(kernel, out_shape=outs, in_specs=specs, out_specs=[out_spe...  12.6 us
    all_to_all x1, starting transfers between devices, per_device(): lax.all_to_all(charges, ('frag', 'tile'), split_axis=0, concat_axis=0, ti...  5.88 us
    ppermute x6, starting transfers between devices, exchanged(): moved.append(lax.ppermute(chunks[shift], 'tile', pairs))  5.15 us
    ppermute x1, starting transfers between devices, neighbours(): found.append(lax.ppermute(x, ('frag', 'tile'), pairs))  3.65 us
    all_to_all x1, waiting for transfers between devices, per_device(): lax.all_to_all(charges, ('frag', 'tile'), split_axis=0, concat_axis=0, ti...  3.37 us
    ppermute x1, waiting for transfers between devices, from_next_tile(): return lax.ppermute(x, 'tile', [(tile, tile ^ 1) for tile in range(tiles)])  0.85 us
  transfers between devices with their start and end apart: 9, of which 3 were waited for; matrix products, arithmetic and copies ran while one was open for 0% of the time, Pallas kernels for 28%

profile of v7, /device:TPU:0, one launch (start us, length us, event | category | flops | bytes accessed | tf_op | source)
XLA Modules:
  0.0 33.2 jit_solution(1425979180410011492)
XLA Ops:
  0.6 0.0 copy-start.1
  0.6 1.7 %shard_map.113 = (f32[2,2,64,256]{3,2,1,0:T(8,128)S(1)}, f32[2,2,64,256]{3,2,1,0:T(8,128)S(1)}, f32[2,72,128]{2,1,0:T(8,128)S(1)}, f32[2,72,128]{2,1,0:T(8,128)S(1)}, f32[6,256]{1,0:T(8,128)S(1)}) custom-call(s32[8]{0:T(128)} %refs_0_.1, f32[8,256]{1,0:T(8,128)} %refs_1_.1, f32[8,256]{1,0:T(8,128)} %refs_2_.1, f32[8,256]{1,0:T(8,128)} %refs_3_.3, ...), custom_call_target="tpu_custom_call" | custom-call | tf_op jit(solution)/shard_map/pallas_call | solution.py:344
  2.4 0.5 %collective-permute-start = (f32[2,2,64,256]{3,2,1,0:T(8,128)S(1)}, f32[2,2,64,256]{3,2,1,0:T(8,128)S(1)}, u32[]{:S(2)}, u32[]{:S(2)}) collective-permute-start(f32[2,2,64,256]{3,2,1,0:T(8,128)S(1)} %get-tuple-element.23), channel_id=1, source_target_pairs={{0,1},{1,0},{2,3},{3,2},{4,5},{5,4},{6,7},{7,6},{8,9},{9,8},{10,11... | collective-permute-start | bytes 786440 | tf_op jit(solution)/shard_map/ppermute | solution.py:364
  2.9 2.6 %collective-permute-start.1 = (f32[2,72,128]{2,1,0:T(8,128)S(1)}, f32[2,72,128]{2,1,0:T(8,128)S(1)}, u32[]{:S(2)}, u32[]{:S(2)}) collective-permute-start(f32[2,72,128]{2,1,0:T(8,128)S(1)} %get-tuple-element.24), channel_id=1, source_target_pairs={{0,2},{1,3},{2,0},{3,1},{4,6},{5,7},{6,4},{7,5},{8,10},{9,11},{10,... | collective-permute-start | bytes 221192 | tf_op jit(solution)/shard_map/ppermute | solution.py:364
  5.5 0.1 collective-permute-start.2
  5.5 0.0 copy-done.1
  5.5 3.7 %collective-permute-start.3 = (f32[3,8,256]{2,1,0:T(8,128)S(1)}, f32[3,8,256]{2,1,0:T(8,128)S(1)}, u32[]{:S(2)}, u32[]{:S(2)}) collective-permute-start(f32[3,8,256]{2,1,0:T(8,128)S(1)} %bitcast.2), channel_id=1, source_target_pairs={{0,4},{4,0},{2,6},{6,2},{5,9},{9,5},{7,11},{11,7},{8,12},{12,8},{1... | collective-permute-start | bytes 73736 | tf_op jit(solution)/shard_map/ppermute | solution.py:377
  9.2 0.0 collective-permute-done.1.refs_2_
  9.2 0.5 %collective-permute-done.2.refs_3_ = f32[2,72,128]{2,1,0:T(8,128)S(1)} collective-permute-done((f32[2,72,128]{2,1,0:T(8,128)S(1)}, f32[2,72,128]{2,1,0:T(8,128)S(1)}, u32[]{:S(2)}, u32[]{:S(2)}) %collective-permute-start.2) | collective-permute-done | bytes 73760 | tf_op jit(solution)/shard_map/ppermute | solution.py:364
  9.7 0.0 collective-permute-done.refs_1_
  9.7 0.0 copy-start
  9.7 5.8 %shard_map.114 = (f32[2,64,256]{2,1,0:T(8,128)S(1)}, f32[2,64,256]{2,1,0:T(8,128)S(1)}, f32[2,64,256]{2,1,0:T(8,128)S(1)}, f32[2,64,256]{2,1,0:T(8,128)S(1)}, f32[32,2,384]{2,1,0:T(2,128)}) custom-call(f32[6,256]{1,0:T(8,128)S(1)} %get-tuple-element.21.facts_ref, f32[2,2,64,256]{3,2,1,0:T(8,128)S(1)} %get-tuple-element.22.refs_0_, ...), custom_call_target="tpu_custom_call" | custom-call | tf_op jit(solution)/shard_map/pallas_call | solution.py:344
  15.5 0.0 collective-permute-done.3.refs_1_
  15.5 0.0 copy-start.3
  15.5 5.9 %all-to-all-start = ((f32[32,2,384]{2,1,0:T(2,128)}), f32[32,2,384]{2,1,0:T(2,128)S(1)}, u32[]{:S(2)}, u32[]{:S(2)}) async-start(f32[32,2,384]{2,1,0:T(2,128)} %get-tuple-element.31), calls=%async_computation | async-start | bytes 196608 | tf_op jit(solution)/shard_map/all_to_all | solution.py:428
  21.4 0.0 copy-start.2
  21.4 0.3 collective-permute-start.5
  21.7 1.7 %collective-permute-start.6 = (f32[2,64,256]{2,1,0:T(8,128)S(1)}, f32[2,64,256]{2,1,0:T(8,128)S(1)}, u32[]{:S(2)}, u32[]{:S(2)}) collective-permute-start(f32[2,64,256]{2,1,0:T(8,128)S(1)} %get-tuple-element.38), channel_id=1, source_target_pairs={{0,2},{1,3},{2,0},{3,1},{4,6},{5,7},{6,4},{7,5},{8,10},{9,11},{10,... | collective-permute-start | bytes 393224 | tf_op jit(solution)/shard_map/ppermute | solution.py:364
  23.4 0.0 collective-permute-start.7
  23.4 0.5 %collective-permute-start.4 = (f32[3,8,256]{2,1,0:T(8,128)S(1)}, f32[3,8,256]{2,1,0:T(8,128)S(1)}, u32[]{:S(2)}, u32[]{:S(2)}) collective-permute-start(f32[3,8,256]{2,1,0:T(8,128)S(1)} %collective-permute-done.3.refs_1_), channel_id=1, source_target_pairs={{0,1},{1,0},{2,3},{3,2},{4,5},{5,4},{6,7},{7,6},{8,9},{9,8},{10,11... | collective-permute-start | bytes 73736 | tf_op jit(solution)/shard_map/ppermute | solution.py:383
  23.9 0.8 %collective-permute-done.4.refs_2_ = f32[3,8,256]{2,1,0:T(8,128)S(1)} collective-permute-done((f32[3,8,256]{2,1,0:T(8,128)S(1)}, f32[3,8,256]{2,1,0:T(8,128)S(1)}, u32[]{:S(2)}, u32[]{:S(2)}) %collective-permute-start.4) | collective-permute-done | bytes 24608 | tf_op jit(solution)/shard_map/ppermute | solution.py:383
  24.7 0.0 copy-done.3
  24.7 0.0 copy-done.2
  24.7 1.1 %shard_map.115 = (bf16[8,32,256]{2,1,0:T(8,128)(2,1)S(1)}, bf16[8,8,32,256]{3,2,1,0:T(8,128)(2,1)S(1)}, f32[8,8,64]{2,1,0:T(8,128)S(1)}, f32[8,8,64]{2,1,0:T(8,128)S(1)}) custom-call(s32[8,8]{1,0:T(8,128)S(1)} %copy-done.2, s32[8,8]{1,0:T(8,128)S(1)} %copy-done.3, f32[3,8,256]{2,1,0:T(8,128)S(1)} %bitcast.3, f32[3,8,256]{2,1,0:T(8,128)S(1)} %bitcast.4, ...), custom_call_target="tpu_custom_call" | custom-call | tf_op jit(solution)/shard_map/pallas_call | solution.py:344
  25.9 3.4 %all-to-all-done.charge_ref = f32[32,2,384]{2,1,0:T(2,128)S(1)} async-done(((f32[32,2,384]{2,1,0:T(2,128)}), f32[32,2,384]{2,1,0:T(2,128)S(1)}, u32[]{:S(2)}, u32[]{:S(2)}) %all-to-all-start) | async-done | bytes 98336 | tf_op jit(solution)/shard_map/all_to_all | solution.py:428
  29.2 0.0 copy-done
  29.2 2.3 %shard_map.116 = (f32[6,64,256]{2,1,0:T(8,128)S(1)}, f32[8,8,256]{2,1,0:T(8,128)S(1)}, f32[8,8,128]{2,1,0:T(8,128)S(1)}) custom-call(f32[32,2,384]{2,1,0:T(2,128)S(1)} %all-to-all-done.charge_ref, f32[8,8,64]{2,1,0:T(8,128)S(1)} %get-tuple-element.32.near_hot, f32[8,8,64]{2,1,0:T(8,128)S(1)} %get-tuple-element.33.far_hot, f32[3,8,256]{2,1,0:T(8,128)S(1)} %bitcast.5, ...), custom_call_target="tpu_custom_call" | custom-call | tf_op jit(solution)/shard_map/pallas_call | solution.py:344
  31.5 0.0 collective-permute-done.5.refs_8_
  31.5 0.0 collective-permute-done.6.refs_9_
  31.5 0.0 collective-permute-done.7.refs_10_
  31.5 1.7 %shard_map.117 = (f32[8,64,256]{2,1,0:T(8,128)}, f32[8,64,256]{2,1,0:T(8,128)}) custom-call(f32[3,8,256]{2,1,0:T(8,128)S(1)} %bitcast.6, bf16[8,32,256]{2,1,0:T(8,128)(2,1)S(1)} %get-tuple-element.29.refs_1_, bf16[8,8,32,256]{3,2,1,0:T(8,128)(2,1)S(1)} %get-tuple-element.30.refs_2_, f32[8,64,256]{2,1,0:T(8,128)S(1)} %copy-done, ...), custom_call_target="tpu_custom_call" | custom-call | tf_op jit(solution)/shard_map/pallas_call | solution.py:344
Async XLA Ops:
  0.6 4.9 %copy-start.1 = (f32[8,3,256]{2,0,1:T(8,128)S(1)}, f32[8,3,256]{2,0,1:T(8,128)}, u32[]{:S(2)}) copy-start(f32[8,3,256]{2,0,1:T(8,128)} %param.16) | copy-start | bytes 73732
  2.4 7.3 %collective-permute-start = (f32[2,2,64,256]{3,2,1,0:T(8,128)S(1)}, f32[2,2,64,256]{3,2,1,0:T(8,128)S(1)}, u32[]{:S(2)}, u32[]{:S(2)}) collective-permute-start(f32[2,2,64,256]{3,2,1,0:T(8,128)S(1)} %get-tuple-element.23), channel_id=1, source_target_pairs={{0,1},{1,0},{2,3},{3,2},{4,5},{5,4},{6,7},{7,6},{8,9},{9,8},{10,11... | collective-permute-start | bytes 786440 | tf_op jit(solution)/shard_map/ppermute | solution.py:364
  2.9 6.3 %collective-permute-start.1 = (f32[2,72,128]{2,1,0:T(8,128)S(1)}, f32[2,72,128]{2,1,0:T(8,128)S(1)}, u32[]{:S(2)}, u32[]{:S(2)}) collective-permute-start(f32[2,72,128]{2,1,0:T(8,128)S(1)} %get-tuple-element.24), channel_id=1, source_target_pairs={{0,2},{1,3},{2,0},{3,1},{4,6},{5,7},{6,4},{7,5},{8,10},{9,11},{10,... | collective-permute-start | bytes 221192 | tf_op jit(solution)/shard_map/ppermute | solution.py:364
  5.5 4.2 %collective-permute-start.2 = (f32[2,72,128]{2,1,0:T(8,128)S(1)}, f32[2,72,128]{2,1,0:T(8,128)S(1)}, u32[]{:S(2)}, u32[]{:S(2)}) collective-permute-start(f32[2,72,128]{2,1,0:T(8,128)S(1)} %get-tuple-element.25), channel_id=1, source_target_pairs={{0,3},{1,2},{2,1},{3,0},{4,7},{5,6},{6,5},{7,4},{8,11},{9,10},{10,... | collective-permute-start | bytes 221192 | tf_op jit(solution)/shard_map/ppermute | solution.py:364
  5.5 10.0 %collective-permute-start.3 = (f32[3,8,256]{2,1,0:T(8,128)S(1)}, f32[3,8,256]{2,1,0:T(8,128)S(1)}, u32[]{:S(2)}, u32[]{:S(2)}) collective-permute-start(f32[3,8,256]{2,1,0:T(8,128)S(1)} %bitcast.2), channel_id=1, source_target_pairs={{0,4},{4,0},{2,6},{6,2},{5,9},{9,5},{7,11},{11,7},{8,12},{12,8},{1... | collective-permute-start | bytes 73736 | tf_op jit(solution)/shard_map/ppermute | solution.py:377
  9.7 19.5 %copy-start = (f32[8,64,256]{2,1,0:T(8,128)S(1)}, f32[8,64,256]{2,1,0:T(8,128)}, u32[]{:S(2)}) copy-start(f32[8,64,256]{2,1,0:T(8,128)} %refs_3_.5) | copy-start | bytes 1572868
  15.5 9.2 %copy-start.3 = (s32[8,8]{1,0:T(8,128)S(1)}, s32[8,8]{1,0:T(8,128)}, u32[]{:S(2)}) copy-start(s32[8,8]{1,0:T(8,128)} %far_ref.1) | copy-start | bytes 772
  15.5 13.7 %all-to-all-start = ((f32[32,2,384]{2,1,0:T(2,128)}), f32[32,2,384]{2,1,0:T(2,128)S(1)}, u32[]{:S(2)}, u32[]{:S(2)}) async-start(f32[32,2,384]{2,1,0:T(2,128)} %get-tuple-element.31), calls=%async_computation | async-start | bytes 196608 | tf_op jit(solution)/shard_map/all_to_all | solution.py:428
  21.4 3.3 %copy-start.2 = (s32[8,8]{1,0:T(8,128)S(1)}, s32[8,8]{1,0:T(8,128)}, u32[]{:S(2)}) copy-start(s32[8,8]{1,0:T(8,128)} %near_ref.1) | copy-start | bytes 772
  21.4 10.1 %collective-permute-start.5 = (f32[2,64,256]{2,1,0:T(8,128)S(1)}, f32[2,64,256]{2,1,0:T(8,128)S(1)}, u32[]{:S(2)}, u32[]{:S(2)}) collective-permute-start(f32[2,64,256]{2,1,0:T(8,128)S(1)} %get-tuple-element.37), channel_id=1, source_target_pairs={{0,1},{1,0},{2,3},{3,2},{4,5},{5,4},{6,7},{7,6},{8,9},{9,8},{10,11... | collective-permute-start | bytes 393224 | tf_op jit(solution)/shard_map/ppermute | solution.py:364
  21.7 9.8 %collective-permute-start.6 = (f32[2,64,256]{2,1,0:T(8,128)S(1)}, f32[2,64,256]{2,1,0:T(8,128)S(1)}, u32[]{:S(2)}, u32[]{:S(2)}) collective-permute-start(f32[2,64,256]{2,1,0:T(8,128)S(1)} %get-tuple-element.38), channel_id=1, source_target_pairs={{0,2},{1,3},{2,0},{3,1},{4,6},{5,7},{6,4},{7,5},{8,10},{9,11},{10,... | collective-permute-start | bytes 393224 | tf_op jit(solution)/shard_map/ppermute | solution.py:364
  23.4 8.1 %collective-permute-start.7 = (f32[2,64,256]{2,1,0:T(8,128)S(1)}, f32[2,64,256]{2,1,0:T(8,128)S(1)}, u32[]{:S(2)}, u32[]{:S(2)}) collective-permute-start(f32[2,64,256]{2,1,0:T(8,128)S(1)} %get-tuple-element.39), channel_id=1, source_target_pairs={{0,3},{1,2},{2,1},{3,0},{4,7},{5,6},{6,5},{7,4},{8,11},{9,10},{10,... | collective-permute-start | bytes 393224 | tf_op jit(solution)/shard_map/ppermute | solution.py:364
  23.4 1.3 %collective-permute-start.4 = (f32[3,8,256]{2,1,0:T(8,128)S(1)}, f32[3,8,256]{2,1,0:T(8,128)S(1)}, u32[]{:S(2)}, u32[]{:S(2)}) collective-permute-start(f32[3,8,256]{2,1,0:T(8,128)S(1)} %collective-permute-done.3.refs_1_), channel_id=1, source_target_pairs={{0,1},{1,0},{2,3},{3,2},{4,5},{5,4},{6,7},{7,6},{8,9},{9,8},{10,11... | collective-permute-start | bytes 73736 | tf_op jit(solution)/shard_map/ppermute | solution.py:383

commit v8 on v7

--- a/solution.py
+++ b/solution.py
@@ -73,19 +73,24 @@
 
 
 def half_fock_kernel(tiles, *refs):
-    inputs, outs, buffers, sems = refs[:8], refs[8:-9], refs[-9:-1], refs[-1]
+    inputs, outs, buffers, sems = refs[:8], refs[8:-11], refs[-11:-1], refs[-1]
+    sizes_ref, charge_ref, embed_ref, pop_ref, place_ref, gamma_ref = buffers[:6]
+    over_near, core_near, over_there, core_there = buffers[6:]
+    half, place_at, places = seat(tiles)
+    count, rows, basis = over_near.shape
+    share, middle = count // places, basis // 2
+    here, there = pl.ds(half * count, count), pl.ds((1 - half) * count, count)
+    columns = pl.ds(pl.multiple_of(half * middle, middle), middle)
+    sources = [*inputs[:6], *[source.at[here] for source in inputs[6:]]]
+    sources += [source.at[there, :, columns] for source in inputs[6:]]
     copies = [
         pltpu.make_async_copy(source, buffer, sems.at[at])
-        for at, (source, buffer) in enumerate(zip(inputs, buffers))
+        for at, (source, buffer) in enumerate(zip(sources, buffers))
     ]
     for copy in copies:
         copy.start()
     for copy in copies:
         copy.wait()
-    sizes_ref, charge_ref, embed_ref, pop_ref, place_ref, gamma_ref, over_ref, core_ref = buffers
-    half, place_at, places = seat(tiles)
-    frag_dev, rows, basis = core_ref.shape
-    share, middle = frag_dev // tiles, basis // 2
     pick = own_rows(rows, basis, lax.axis_index("tile") * rows)
     pick_half = own_rows(rows, middle, place_at * rows)
     row = lax.broadcasted_iota(jnp.int32, (rows, middle), 0) + lax.axis_index("tile") * rows
@@ -100,8 +105,12 @@
             terms = gamma_ref[frag] * charge_ref[pl.ds(frag, 1), :]
             terms = terms + jnp.where(pick, embed_ref[pl.ds(frag, 1), :], 0.0)
             field = jnp.sum(terms, axis=1, keepdims=True)
-            core, core_far = swapped(half, core_ref[frag])
-            over, over_far = swapped(half, over_ref[frag])
+            at = lax.rem(place_at + shift, places) * share + spot
+            if shift < places:
+                core, core_far = swapped(half, core_near[at])
+                over, over_far = swapped(half, over_near[at])
+            else:
+                core, over = core_there[at], over_there[at]
             inside = (row < size) & (mine < size)
             core, over = jnp.where(inside, core, 0.0), jnp.where(inside, over, 0.0)
             out = outs[shift]
@@ -237,6 +246,13 @@
     lane = lax.broadcasted_iota(jnp.int32, (1, near_hot.shape[2]), 1)
     ones = jnp.ones((frag_dev, basis), jnp.float32)
     frag_at, reach = lax.axis_index("frag"), around // 2
+    tiles, peers = lax.axis_size("tile"), lax.axis_size("frag")
+    share = frag_dev // tiles
+
+    def row_of(frag):
+        inside = lax.rem(frag, frag_dev)
+        return (inside // share * peers + frag // frag_dev) * share + lax.rem(inside, share)
+
     first_frag = (frag_at - reach) * frag_dev
 
     def fill(target, first, place_ref, scale, extra, which):
@@ -264,10 +280,10 @@
     for frag in range(frag_dev):
         for k in range(near):
             other = near_ref[frag, k]
-            near_hot[frag, k : k + 1, :] = (lane == other).astype(jnp.float32)
+            near_hot[frag, k : k + 1, :] = (lane == row_of(other)).astype(jnp.float32)
             right_out[frag, k] = table_side[other - first_frag].astype(jnp.bfloat16)
         for m in range(far):
-            far_hot[frag, m : m + 1, :] = (lane == far_ref[frag, m]).astype(jnp.float32)
+            far_hot[frag, m : m + 1, :] = (lane == row_of(far_ref[frag, m])).astype(jnp.float32)
 
 
 def gather_charges(charge_ref, near_hot, far_hot, near_charge, far_block):
@@ -409,8 +425,9 @@
         [pltpu.with_memory_space_constraint(x, pltpu.HBM) for x in inputs],
         [HBM] * len(inputs),
         [pltpu.SMEM(frag_sizes.shape, jnp.int32)]
-        + [pltpu.VMEM(x.shape, jnp.float32) for x in inputs[1:]]
-        + [pltpu.SemaphoreType.DMA((len(inputs),))],
+        + [pltpu.VMEM(x.shape, jnp.float32) for x in inputs[1:6]]
+        + [pltpu.VMEM((frag_dev // 2, rows, width), jnp.float32) for width in (basis, basis, basis // 2, basis // 2)]
+        + [pltpu.SemaphoreType.DMA((len(inputs) + 2,))],
     )
     sent = exchanged(sent)
     swaps = neighbours(places, -(-SPAN // frag_dev))
@@ -425,7 +442,7 @@
     moved = exchanged(pieces)
     charges, swaps = lax.optimization_barrier((charges, swaps))
     sources = [places, *swaps, *[from_next_tile(x) for x in swaps]]
-    charges = lax.all_to_all(charges, ("frag", "tile"), split_axis=0, concat_axis=0, tiled=True)
+    charges = lax.all_to_all(charges, ("tile", "frag"), split_axis=0, concat_axis=0, tiled=True)
     near, far, frags = near_list.shape[1], far_list.shape[1], peers * frag_dev
     parts = call(
         functools.partial(geometry_kernel, len(sources)),

time: 33.5 us -> 33.1 us (0.988)
  waiting for transfers between devices: 4.71 us -> 3.35 us
  Pallas kernels: 12.6 us -> 13.6 us
    all_to_all x1, waiting for transfers between devices: 3.37 us -> 2 us  [per_device(): lax.all_to_all(charges, ('tile', 'frag'), split_axis=0, concat_axis=0, ti...]
    pallas_call x5, Pallas kernels: 12.6 us -> 13.6 us  [call(): pl.pallas_call(kernel, out_shape=outs, in_specs=specs, out_specs=[out_spe...]
  transfers between devices with their start and end apart: 9 -> 9, of which waited for: 3 -> 3; matrix products, arithmetic and copies ran while one was open for 0% -> 0% of each run, Pallas kernels for 28% -> 31%
where the time goes in v8:
time: 33.1 us; the launch traced here: 32.9 us
  starting transfers between devices  15.1 us (46%)
  Pallas kernels  13.6 us (41%)
  waiting for transfers between devices  3.35 us (10%)
  between operations  0.73 us (2%)
    pallas_call x5, Pallas kernels, call(): pl.pallas_call(kernel, out_shape=outs, in_specs=specs, out_specs=[out_spe...  13.6 us
    all_to_all x1, starting transfers between devices, per_device(): lax.all_to_all(charges, ('tile', 'frag'), split_axis=0, concat_axis=0, ti...  5.88 us
    ppermute x6, starting transfers between devices, exchanged(): moved.append(lax.ppermute(chunks[shift], 'tile', pairs))  5.15 us
    ppermute x1, starting transfers between devices, neighbours(): found.append(lax.ppermute(x, ('frag', 'tile'), pairs))  3.65 us
    all_to_all x1, waiting for transfers between devices, per_device(): lax.all_to_all(charges, ('tile', 'frag'), split_axis=0, concat_axis=0, ti...  2 us
    ppermute x1, waiting for transfers between devices, from_next_tile(): return lax.ppermute(x, 'tile', [(tile, tile ^ 1) for tile in range(tiles)])  0.85 us
  transfers between devices with their start and end apart: 9, of which 3 were waited for; matrix products, arithmetic and copies ran while one was open for 0% of the time, Pallas kernels for 31%

profile of v8, /device:TPU:0, one launch (start us, length us, event | category | flops | bytes accessed | tf_op | source)
XLA Modules:
  0.0 32.9 jit_solution(15503568563522569742)
XLA Ops:
  0.6 0.0 copy-start.1
  0.6 1.6 %shard_map.113 = (f32[2,2,64,256]{3,2,1,0:T(8,128)S(1)}, f32[2,2,64,256]{3,2,1,0:T(8,128)S(1)}, f32[2,72,128]{2,1,0:T(8,128)S(1)}, f32[2,72,128]{2,1,0:T(8,128)S(1)}, f32[6,256]{1,0:T(8,128)S(1)}) custom-call(s32[8]{0:T(128)} %refs_0_.1, f32[8,256]{1,0:T(8,128)} %refs_1_.1, f32[8,256]{1,0:T(8,128)} %refs_2_.1, f32[8,256]{1,0:T(8,128)} %refs_3_.3, ...), custom_call_target="tpu_custom_call" | custom-call | tf_op jit(solution)/shard_map/pallas_call | solution.py:360
  2.3 0.5 %collective-permute-start = (f32[2,2,64,256]{3,2,1,0:T(8,128)S(1)}, f32[2,2,64,256]{3,2,1,0:T(8,128)S(1)}, u32[]{:S(2)}, u32[]{:S(2)}) collective-permute-start(f32[2,2,64,256]{3,2,1,0:T(8,128)S(1)} %get-tuple-element.23), channel_id=1, source_target_pairs={{0,1},{1,0},{2,3},{3,2},{4,5},{5,4},{6,7},{7,6},{8,9},{9,8},{10,11... | collective-permute-start | bytes 786440 | tf_op jit(solution)/shard_map/ppermute | solution.py:380
  2.8 2.6 %collective-permute-start.1 = (f32[2,72,128]{2,1,0:T(8,128)S(1)}, f32[2,72,128]{2,1,0:T(8,128)S(1)}, u32[]{:S(2)}, u32[]{:S(2)}) collective-permute-start(f32[2,72,128]{2,1,0:T(8,128)S(1)} %get-tuple-element.24), channel_id=1, source_target_pairs={{0,2},{1,3},{2,0},{3,1},{4,6},{5,7},{6,4},{7,5},{8,10},{9,11},{10,... | collective-permute-start | bytes 221192 | tf_op jit(solution)/shard_map/ppermute | solution.py:380
  5.4 0.1 collective-permute-start.2
  5.4 0.0 copy-done.1
  5.4 3.7 %collective-permute-start.3 = (f32[3,8,256]{2,1,0:T(8,128)S(1)}, f32[3,8,256]{2,1,0:T(8,128)S(1)}, u32[]{:S(2)}, u32[]{:S(2)}) collective-permute-start(f32[3,8,256]{2,1,0:T(8,128)S(1)} %bitcast.2), channel_id=1, source_target_pairs={{0,4},{4,0},{2,6},{6,2},{5,9},{9,5},{7,11},{11,7},{8,12},{12,8},{1... | collective-permute-start | bytes 73736 | tf_op jit(solution)/shard_map/ppermute | solution.py:393
  9.1 0.0 collective-permute-done.1.refs_2_
  9.1 0.5 %collective-permute-done.2.refs_3_ = f32[2,72,128]{2,1,0:T(8,128)S(1)} collective-permute-done((f32[2,72,128]{2,1,0:T(8,128)S(1)}, f32[2,72,128]{2,1,0:T(8,128)S(1)}, u32[]{:S(2)}, u32[]{:S(2)}) %collective-permute-start.2) | collective-permute-done | bytes 73760 | tf_op jit(solution)/shard_map/ppermute | solution.py:380
  9.6 0.0 collective-permute-done.refs_1_
  9.6 0.0 copy-start
  9.6 5.8 %shard_map.114 = (f32[2,64,256]{2,1,0:T(8,128)S(1)}, f32[2,64,256]{2,1,0:T(8,128)S(1)}, f32[2,64,256]{2,1,0:T(8,128)S(1)}, f32[2,64,256]{2,1,0:T(8,128)S(1)}, f32[32,2,384]{2,1,0:T(2,128)}) custom-call(f32[6,256]{1,0:T(8,128)S(1)} %get-tuple-element.21.facts_ref, f32[2,2,64,256]{3,2,1,0:T(8,128)S(1)} %get-tuple-element.22.refs_0_, ...), custom_call_target="tpu_custom_call" | custom-call | tf_op jit(solution)/shard_map/pallas_call | solution.py:360
  15.4 0.0 collective-permute-done.3.refs_1_
  15.4 0.0 copy-start.3
  15.4 5.9 %all-to-all-start = ((f32[32,2,384]{2,1,0:T(2,128)}), f32[32,2,384]{2,1,0:T(2,128)S(1)}, u32[]{:S(2)}, u32[]{:S(2)}) async-start(f32[32,2,384]{2,1,0:T(2,128)} %get-tuple-element.31), calls=%async_computation | async-start | bytes 196608 | tf_op jit(solution)/shard_map/all_to_all | solution.py:445
  21.3 0.0 copy-start.2
  21.3 0.3 collective-permute-start.5
  21.6 1.7 %collective-permute-start.6 = (f32[2,64,256]{2,1,0:T(8,128)S(1)}, f32[2,64,256]{2,1,0:T(8,128)S(1)}, u32[]{:S(2)}, u32[]{:S(2)}) collective-permute-start(f32[2,64,256]{2,1,0:T(8,128)S(1)} %get-tuple-element.38), channel_id=1, source_target_pairs={{0,2},{1,3},{2,0},{3,1},{4,6},{5,7},{6,4},{7,5},{8,10},{9,11},{10,... | collective-permute-start | bytes 393224 | tf_op jit(solution)/shard_map/ppermute | solution.py:380
  23.3 0.0 collective-permute-start.7
  23.3 0.5 %collective-permute-start.4 = (f32[3,8,256]{2,1,0:T(8,128)S(1)}, f32[3,8,256]{2,1,0:T(8,128)S(1)}, u32[]{:S(2)}, u32[]{:S(2)}) collective-permute-start(f32[3,8,256]{2,1,0:T(8,128)S(1)} %collective-permute-done.3.refs_1_), channel_id=1, source_target_pairs={{0,1},{1,0},{2,3},{3,2},{4,5},{5,4},{6,7},{7,6},{8,9},{9,8},{10,11... | collective-permute-start | bytes 73736 | tf_op jit(solution)/shard_map/ppermute | solution.py:399
  23.8 0.8 %collective-permute-done.4.refs_2_ = f32[3,8,256]{2,1,0:T(8,128)S(1)} collective-permute-done((f32[3,8,256]{2,1,0:T(8,128)S(1)}, f32[3,8,256]{2,1,0:T(8,128)S(1)}, u32[]{:S(2)}, u32[]{:S(2)}) %collective-permute-start.4) | collective-permute-done | bytes 24608 | tf_op jit(solution)/shard_map/ppermute | solution.py:399
  24.6 0.0 copy-done.3
  24.6 0.0 copy-done.2
  24.6 2.2 %shard_map.115 = (bf16[8,32,256]{2,1,0:T(8,128)(2,1)S(1)}, bf16[8,8,32,256]{3,2,1,0:T(8,128)(2,1)S(1)}, f32[8,8,64]{2,1,0:T(8,128)S(1)}, f32[8,8,64]{2,1,0:T(8,128)S(1)}) custom-call(s32[8,8]{1,0:T(8,128)S(1)} %copy-done.2, s32[8,8]{1,0:T(8,128)S(1)} %copy-done.3, f32[3,8,256]{2,1,0:T(8,128)S(1)} %bitcast.3, f32[3,8,256]{2,1,0:T(8,128)S(1)} %bitcast.4, ...), custom_call_target="tpu_custom_call" | custom-call | tf_op jit(solution)/shard_map/pallas_call | solution.py:360
  26.9 2.0 %all-to-all-done.charge_ref = f32[32,2,384]{2,1,0:T(2,128)S(1)} async-done(((f32[32,2,384]{2,1,0:T(2,128)}), f32[32,2,384]{2,1,0:T(2,128)S(1)}, u32[]{:S(2)}, u32[]{:S(2)}) %all-to-all-start) | async-done | bytes 98336 | tf_op jit(solution)/shard_map/all_to_all | solution.py:445
  28.9 0.0 copy-done
  28.9 2.3 %shard_map.116 = (f32[6,64,256]{2,1,0:T(8,128)S(1)}, f32[8,8,256]{2,1,0:T(8,128)S(1)}, f32[8,8,128]{2,1,0:T(8,128)S(1)}) custom-call(f32[32,2,384]{2,1,0:T(2,128)S(1)} %all-to-all-done.charge_ref, f32[8,8,64]{2,1,0:T(8,128)S(1)} %get-tuple-element.32.near_hot, f32[8,8,64]{2,1,0:T(8,128)S(1)} %get-tuple-element.33.far_hot, f32[3,8,256]{2,1,0:T(8,128)S(1)} %bitcast.5, ...), custom_call_target="tpu_custom_call" | custom-call | tf_op jit(solution)/shard_map/pallas_call | solution.py:360
  31.2 0.0 collective-permute-done.5.refs_8_
  31.2 0.0 collective-permute-done.6.refs_9_
  31.2 0.0 collective-permute-done.7.refs_10_
  31.2 1.7 %shard_map.117 = (f32[8,64,256]{2,1,0:T(8,128)}, f32[8,64,256]{2,1,0:T(8,128)}) custom-call(f32[3,8,256]{2,1,0:T(8,128)S(1)} %bitcast.6, bf16[8,32,256]{2,1,0:T(8,128)(2,1)S(1)} %get-tuple-element.29.refs_1_, bf16[8,8,32,256]{3,2,1,0:T(8,128)(2,1)S(1)} %get-tuple-element.30.refs_2_, f32[8,64,256]{2,1,0:T(8,128)S(1)} %copy-done, ...), custom_call_target="tpu_custom_call" | custom-call | tf_op jit(solution)/shard_map/pallas_call | solution.py:360
Async XLA Ops:
  0.6 4.8 %copy-start.1 = (f32[8,3,256]{2,0,1:T(8,128)S(1)}, f32[8,3,256]{2,0,1:T(8,128)}, u32[]{:S(2)}) copy-start(f32[8,3,256]{2,0,1:T(8,128)} %param.16) | copy-start | bytes 73732
  2.3 7.3 %collective-permute-start = (f32[2,2,64,256]{3,2,1,0:T(8,128)S(1)}, f32[2,2,64,256]{3,2,1,0:T(8,128)S(1)}, u32[]{:S(2)}, u32[]{:S(2)}) collective-permute-start(f32[2,2,64,256]{3,2,1,0:T(8,128)S(1)} %get-tuple-element.23), channel_id=1, source_target_pairs={{0,1},{1,0},{2,3},{3,2},{4,5},{5,4},{6,7},{7,6},{8,9},{9,8},{10,11... | collective-permute-start | bytes 786440 | tf_op jit(solution)/shard_map/ppermute | solution.py:380
  2.8 6.3 %collective-permute-start.1 = (f32[2,72,128]{2,1,0:T(8,128)S(1)}, f32[2,72,128]{2,1,0:T(8,128)S(1)}, u32[]{:S(2)}, u32[]{:S(2)}) collective-permute-start(f32[2,72,128]{2,1,0:T(8,128)S(1)} %get-tuple-element.24), channel_id=1, source_target_pairs={{0,2},{1,3},{2,0},{3,1},{4,6},{5,7},{6,4},{7,5},{8,10},{9,11},{10,... | collective-permute-start | bytes 221192 | tf_op jit(solution)/shard_map/ppermute | solution.py:380
  5.4 4.2 %collective-permute-start.2 = (f32[2,72,128]{2,1,0:T(8,128)S(1)}, f32[2,72,128]{2,1,0:T(8,128)S(1)}, u32[]{:S(2)}, u32[]{:S(2)}) collective-permute-start(f32[2,72,128]{2,1,0:T(8,128)S(1)} %get-tuple-element.25), channel_id=1, source_target_pairs={{0,3},{1,2},{2,1},{3,0},{4,7},{5,6},{6,5},{7,4},{8,11},{9,10},{10,... | collective-permute-start | bytes 221192 | tf_op jit(solution)/shard_map/ppermute | solution.py:380
  5.4 10.0 %collective-permute-start.3 = (f32[3,8,256]{2,1,0:T(8,128)S(1)}, f32[3,8,256]{2,1,0:T(8,128)S(1)}, u32[]{:S(2)}, u32[]{:S(2)}) collective-permute-start(f32[3,8,256]{2,1,0:T(8,128)S(1)} %bitcast.2), channel_id=1, source_target_pairs={{0,4},{4,0},{2,6},{6,2},{5,9},{9,5},{7,11},{11,7},{8,12},{12,8},{1... | collective-permute-start | bytes 73736 | tf_op jit(solution)/shard_map/ppermute | solution.py:393
  9.6 19.3 %copy-start = (f32[8,64,256]{2,1,0:T(8,128)S(1)}, f32[8,64,256]{2,1,0:T(8,128)}, u32[]{:S(2)}) copy-start(f32[8,64,256]{2,1,0:T(8,128)} %refs_3_.5) | copy-start | bytes 1572868
  15.4 9.2 %copy-start.3 = (s32[8,8]{1,0:T(8,128)S(1)}, s32[8,8]{1,0:T(8,128)}, u32[]{:S(2)}) copy-start(s32[8,8]{1,0:T(8,128)} %far_ref.1) | copy-start | bytes 772
  15.4 13.4 %all-to-all-start = ((f32[32,2,384]{2,1,0:T(2,128)}), f32[32,2,384]{2,1,0:T(2,128)S(1)}, u32[]{:S(2)}, u32[]{:S(2)}) async-start(f32[32,2,384]{2,1,0:T(2,128)} %get-tuple-element.31), calls=%async_computation | async-start | bytes 196608 | tf_op jit(solution)/shard_map/all_to_all | solution.py:445
  21.3 3.3 %copy-start.2 = (s32[8,8]{1,0:T(8,128)S(1)}, s32[8,8]{1,0:T(8,128)}, u32[]{:S(2)}) copy-start(s32[8,8]{1,0:T(8,128)} %near_ref.1) | copy-start | bytes 772
  21.3 9.8 %collective-permute-start.5 = (f32[2,64,256]{2,1,0:T(8,128)S(1)}, f32[2,64,256]{2,1,0:T(8,128)S(1)}, u32[]{:S(2)}, u32[]{:S(2)}) collective-permute-start(f32[2,64,256]{2,1,0:T(8,128)S(1)} %get-tuple-element.37), channel_id=1, source_target_pairs={{0,1},{1,0},{2,3},{3,2},{4,5},{5,4},{6,7},{7,6},{8,9},{9,8},{10,11... | collective-permute-start | bytes 393224 | tf_op jit(solution)/shard_map/ppermute | solution.py:380
  21.6 9.5 %collective-permute-start.6 = (f32[2,64,256]{2,1,0:T(8,128)S(1)}, f32[2,64,256]{2,1,0:T(8,128)S(1)}, u32[]{:S(2)}, u32[]{:S(2)}) collective-permute-start(f32[2,64,256]{2,1,0:T(8,128)S(1)} %get-tuple-element.38), channel_id=1, source_target_pairs={{0,2},{1,3},{2,0},{3,1},{4,6},{5,7},{6,4},{7,5},{8,10},{9,11},{10,... | collective-permute-start | bytes 393224 | tf_op jit(solution)/shard_map/ppermute | solution.py:380
  23.3 7.9 %collective-permute-start.7 = (f32[2,64,256]{2,1,0:T(8,128)S(1)}, f32[2,64,256]{2,1,0:T(8,128)S(1)}, u32[]{:S(2)}, u32[]{:S(2)}) collective-permute-start(f32[2,64,256]{2,1,0:T(8,128)S(1)} %get-tuple-element.39), channel_id=1, source_target_pairs={{0,3},{1,2},{2,1},{3,0},{4,7},{5,6},{6,5},{7,4},{8,11},{9,10},{10,... | collective-permute-start | bytes 393224 | tf_op jit(solution)/shard_map/ppermute | solution.py:380
  23.3 1.3 %collective-permute-start.4 = (f32[3,8,256]{2,1,0:T(8,128)S(1)}, f32[3,8,256]{2,1,0:T(8,128)S(1)}, u32[]{:S(2)}, u32[]{:S(2)}) collective-permute-start(f32[3,8,256]{2,1,0:T(8,128)S(1)} %collective-permute-done.3.refs_1_), channel_id=1, source_target_pairs={{0,1},{1,0},{2,3},{3,2},{4,5},{5,4},{6,7},{7,6},{8,9},{9,8},{10,11... | collective-permute-start | bytes 73736 | tf_op jit(solution)/shard_map/ppermute | solution.py:399

commit v9 on v8

--- a/solution.py
+++ b/solution.py
@@ -293,8 +293,10 @@
         (near_hot, near_charge, table[:, :basis]),
         (far_hot, far_block, table[:, basis:]),
     ):
-        every = hot[...].reshape(-1, hot.shape[2])
-        picked = jnp.dot(every, part, precision=lax.Precision.HIGHEST, preferred_element_type=jnp.float32)
+        every = hot[...].reshape(-1, hot.shape[2]).astype(jnp.bfloat16)
+        pieces = [piece.astype(jnp.bfloat16) for piece in pieces_of(part)]
+        sums = [jnp.dot(every, piece, preferred_element_type=jnp.float32) for piece in pieces]
+        picked = sums[0] + sums[1] + sums[2]
         gathered[...] = picked.reshape(gathered.shape)
 
 
@@ -462,7 +464,7 @@
     )
     left, right, near_hot, far_hot = parts
     inputs = (places, left, right, intersection)
-    done = frag_dev * 3 // 4
+    done = frag_dev * 5 // 8
     rest = frag_dev - done
     esp_rows, near_charge, far_block = call(
         first_esp_kernel,

time: 33.1 us -> 33.2 us (level)
  no operation moved by 1% of the time
where the time goes in v9:
time: 33.2 us; the launch traced here: 32.9 us
  starting transfers between devices  15.1 us (45%)
  Pallas kernels  13.7 us (41%)
  waiting for transfers between devices  3.35 us (10%)
  between operations  0.73 us (2%)
    pallas_call x5, Pallas kernels, call(): pl.pallas_call(kernel, out_shape=outs, in_specs=specs, out_specs=[out_spe...  13.7 us
    all_to_all x1, starting transfers between devices, per_device(): lax.all_to_all(charges, ('tile', 'frag'), split_axis=0, concat_axis=0, ti...  5.88 us
    ppermute x6, starting transfers between devices, exchanged(): moved.append(lax.ppermute(chunks[shift], 'tile', pairs))  5.15 us
    ppermute x1, starting transfers between devices, neighbours(): found.append(lax.ppermute(x, ('frag', 'tile'), pairs))  3.65 us
    all_to_all x1, waiting for transfers between devices, per_device(): lax.all_to_all(charges, ('tile', 'frag'), split_axis=0, concat_axis=0, ti...  2 us
    ppermute x1, waiting for transfers between devices, from_next_tile(): return lax.ppermute(x, 'tile', [(tile, tile ^ 1) for tile in range(tiles)])  0.85 us
  transfers between devices with their start and end apart: 9, of which 3 were waited for; matrix products, arithmetic and copies ran while one was open for 0% of the time, Pallas kernels for 31%

profile of v9, /device:TPU:0, one launch (start us, length us, event | category | flops | bytes accessed | tf_op | source)
XLA Modules:
  0.0 32.9 jit_solution(8799632533772094783)
XLA Ops:
  0.6 0.0 copy-start.1
  0.6 1.6 %shard_map.113 = (f32[2,2,64,256]{3,2,1,0:T(8,128)S(1)}, f32[2,2,64,256]{3,2,1,0:T(8,128)S(1)}, f32[2,72,128]{2,1,0:T(8,128)S(1)}, f32[2,72,128]{2,1,0:T(8,128)S(1)}, f32[6,256]{1,0:T(8,128)S(1)}) custom-call(s32[8]{0:T(128)} %refs_0_.1, f32[8,256]{1,0:T(8,128)} %refs_1_.1, f32[8,256]{1,0:T(8,128)} %refs_2_.1, f32[8,256]{1,0:T(8,128)} %refs_3_.3, ...), custom_call_target="tpu_custom_call" | custom-call | tf_op jit(solution)/shard_map/pallas_call | solution.py:362
  2.3 0.5 %collective-permute-start = (f32[2,2,64,256]{3,2,1,0:T(8,128)S(1)}, f32[2,2,64,256]{3,2,1,0:T(8,128)S(1)}, u32[]{:S(2)}, u32[]{:S(2)}) collective-permute-start(f32[2,2,64,256]{3,2,1,0:T(8,128)S(1)} %get-tuple-element.23), channel_id=1, source_target_pairs={{0,1},{1,0},{2,3},{3,2},{4,5},{5,4},{6,7},{7,6},{8,9},{9,8},{10,11... | collective-permute-start | bytes 786440 | tf_op jit(solution)/shard_map/ppermute | solution.py:382
  2.8 2.6 %collective-permute-start.1 = (f32[2,72,128]{2,1,0:T(8,128)S(1)}, f32[2,72,128]{2,1,0:T(8,128)S(1)}, u32[]{:S(2)}, u32[]{:S(2)}) collective-permute-start(f32[2,72,128]{2,1,0:T(8,128)S(1)} %get-tuple-element.24), channel_id=1, source_target_pairs={{0,2},{1,3},{2,0},{3,1},{4,6},{5,7},{6,4},{7,5},{8,10},{9,11},{10,... | collective-permute-start | bytes 221192 | tf_op jit(solution)/shard_map/ppermute | solution.py:382
  5.4 0.1 collective-permute-start.2
  5.4 0.0 copy-done.1
  5.4 3.7 %collective-permute-start.3 = (f32[3,8,256]{2,1,0:T(8,128)S(1)}, f32[3,8,256]{2,1,0:T(8,128)S(1)}, u32[]{:S(2)}, u32[]{:S(2)}) collective-permute-start(f32[3,8,256]{2,1,0:T(8,128)S(1)} %bitcast.2), channel_id=1, source_target_pairs={{0,4},{4,0},{2,6},{6,2},{5,9},{9,5},{7,11},{11,7},{8,12},{12,8},{1... | collective-permute-start | bytes 73736 | tf_op jit(solution)/shard_map/ppermute | solution.py:395
  9.1 0.0 collective-permute-done.1.refs_2_
  9.1 0.5 %collective-permute-done.2.refs_3_ = f32[2,72,128]{2,1,0:T(8,128)S(1)} collective-permute-done((f32[2,72,128]{2,1,0:T(8,128)S(1)}, f32[2,72,128]{2,1,0:T(8,128)S(1)}, u32[]{:S(2)}, u32[]{:S(2)}) %collective-permute-start.2) | collective-permute-done | bytes 73760 | tf_op jit(solution)/shard_map/ppermute | solution.py:382
  9.6 0.0 collective-permute-done.refs_1_
  9.6 0.0 copy-start
  9.6 5.8 %shard_map.114 = (f32[2,64,256]{2,1,0:T(8,128)S(1)}, f32[2,64,256]{2,1,0:T(8,128)S(1)}, f32[2,64,256]{2,1,0:T(8,128)S(1)}, f32[2,64,256]{2,1,0:T(8,128)S(1)}, f32[32,2,384]{2,1,0:T(2,128)}) custom-call(f32[6,256]{1,0:T(8,128)S(1)} %get-tuple-element.21.facts_ref, f32[2,2,64,256]{3,2,1,0:T(8,128)S(1)} %get-tuple-element.22.refs_0_, ...), custom_call_target="tpu_custom_call" | custom-call | tf_op jit(solution)/shard_map/pallas_call | solution.py:362
  15.4 0.0 collective-permute-done.3.refs_1_
  15.4 0.0 copy-start.3
  15.4 5.9 %all-to-all-start = ((f32[32,2,384]{2,1,0:T(2,128)}), f32[32,2,384]{2,1,0:T(2,128)S(1)}, u32[]{:S(2)}, u32[]{:S(2)}) async-start(f32[32,2,384]{2,1,0:T(2,128)} %get-tuple-element.31), calls=%async_computation | async-start | bytes 196608 | tf_op jit(solution)/shard_map/all_to_all | solution.py:447
  21.3 0.0 copy-start.2
  21.3 0.3 collective-permute-start.5
  21.6 1.7 %collective-permute-start.6 = (f32[2,64,256]{2,1,0:T(8,128)S(1)}, f32[2,64,256]{2,1,0:T(8,128)S(1)}, u32[]{:S(2)}, u32[]{:S(2)}) collective-permute-start(f32[2,64,256]{2,1,0:T(8,128)S(1)} %get-tuple-element.38), channel_id=1, source_target_pairs={{0,2},{1,3},{2,0},{3,1},{4,6},{5,7},{6,4},{7,5},{8,10},{9,11},{10,... | collective-permute-start | bytes 393224 | tf_op jit(solution)/shard_map/ppermute | solution.py:382
  23.3 0.0 collective-permute-start.7
  23.3 0.5 %collective-permute-start.4 = (f32[3,8,256]{2,1,0:T(8,128)S(1)}, f32[3,8,256]{2,1,0:T(8,128)S(1)}, u32[]{:S(2)}, u32[]{:S(2)}) collective-permute-start(f32[3,8,256]{2,1,0:T(8,128)S(1)} %collective-permute-done.3.refs_1_), channel_id=1, source_target_pairs={{0,1},{1,0},{2,3},{3,2},{4,5},{5,4},{6,7},{7,6},{8,9},{9,8},{10,11... | collective-permute-start | bytes 73736 | tf_op jit(solution)/shard_map/ppermute | solution.py:401
  23.8 0.8 %collective-permute-done.4.refs_2_ = f32[3,8,256]{2,1,0:T(8,128)S(1)} collective-permute-done((f32[3,8,256]{2,1,0:T(8,128)S(1)}, f32[3,8,256]{2,1,0:T(8,128)S(1)}, u32[]{:S(2)}, u32[]{:S(2)}) %collective-permute-start.4) | collective-permute-done | bytes 24608 | tf_op jit(solution)/shard_map/ppermute | solution.py:401
  24.6 0.0 copy-done.3
  24.6 0.0 copy-done.2
  24.6 2.2 %shard_map.115 = (bf16[8,32,256]{2,1,0:T(8,128)(2,1)S(1)}, bf16[8,8,32,256]{3,2,1,0:T(8,128)(2,1)S(1)}, f32[8,8,64]{2,1,0:T(8,128)S(1)}, f32[8,8,64]{2,1,0:T(8,128)S(1)}) custom-call(s32[8,8]{1,0:T(8,128)S(1)} %copy-done.2, s32[8,8]{1,0:T(8,128)S(1)} %copy-done.3, f32[3,8,256]{2,1,0:T(8,128)S(1)} %bitcast.3, f32[3,8,256]{2,1,0:T(8,128)S(1)} %bitcast.4, ...), custom_call_target="tpu_custom_call" | custom-call | tf_op jit(solution)/shard_map/pallas_call | solution.py:362
  26.9 2.0 %all-to-all-done.charge_ref = f32[32,2,384]{2,1,0:T(2,128)S(1)} async-done(((f32[32,2,384]{2,1,0:T(2,128)}), f32[32,2,384]{2,1,0:T(2,128)S(1)}, u32[]{:S(2)}, u32[]{:S(2)}) %all-to-all-start) | async-done | bytes 98336 | tf_op jit(solution)/shard_map/all_to_all | solution.py:447
  28.9 0.0 copy-done
  28.9 2.0 %shard_map.116 = (f32[5,64,256]{2,1,0:T(8,128)S(1)}, f32[8,8,256]{2,1,0:T(8,128)S(1)}, f32[8,8,128]{2,1,0:T(8,128)S(1)}) custom-call(f32[32,2,384]{2,1,0:T(2,128)S(1)} %all-to-all-done.charge_ref, f32[8,8,64]{2,1,0:T(8,128)S(1)} %get-tuple-element.32.near_hot, f32[8,8,64]{2,1,0:T(8,128)S(1)} %get-tuple-element.33.far_hot, f32[3,8,256]{2,1,0:T(8,128)S(1)} %bitcast.5, ...), custom_call_target="tpu_custom_call" | custom-call | tf_op jit(solution)/shard_map/pallas_call | solution.py:362
  30.9 0.0 collective-permute-done.5.refs_8_
  30.9 0.0 collective-permute-done.6.refs_9_
  30.9 0.0 collective-permute-done.7.refs_10_
  30.9 2.0 %shard_map.117 = (f32[8,64,256]{2,1,0:T(8,128)}, f32[8,64,256]{2,1,0:T(8,128)}) custom-call(f32[3,8,256]{2,1,0:T(8,128)S(1)} %bitcast.6, bf16[8,32,256]{2,1,0:T(8,128)(2,1)S(1)} %get-tuple-element.29.refs_1_, bf16[8,8,32,256]{3,2,1,0:T(8,128)(2,1)S(1)} %get-tuple-element.30.refs_2_, f32[8,64,256]{2,1,0:T(8,128)S(1)} %copy-done, ...), custom_call_target="tpu_custom_call" | custom-call | tf_op jit(solution)/shard_map/pallas_call | solution.py:362
Async XLA Ops:
  0.6 4.8 %copy-start.1 = (f32[8,3,256]{2,0,1:T(8,128)S(1)}, f32[8,3,256]{2,0,1:T(8,128)}, u32[]{:S(2)}) copy-start(f32[8,3,256]{2,0,1:T(8,128)} %param.16) | copy-start | bytes 73732
  2.3 7.3 %collective-permute-start = (f32[2,2,64,256]{3,2,1,0:T(8,128)S(1)}, f32[2,2,64,256]{3,2,1,0:T(8,128)S(1)}, u32[]{:S(2)}, u32[]{:S(2)}) collective-permute-start(f32[2,2,64,256]{3,2,1,0:T(8,128)S(1)} %get-tuple-element.23), channel_id=1, source_target_pairs={{0,1},{1,0},{2,3},{3,2},{4,5},{5,4},{6,7},{7,6},{8,9},{9,8},{10,11... | collective-permute-start | bytes 786440 | tf_op jit(solution)/shard_map/ppermute | solution.py:382
  2.8 6.3 %collective-permute-start.1 = (f32[2,72,128]{2,1,0:T(8,128)S(1)}, f32[2,72,128]{2,1,0:T(8,128)S(1)}, u32[]{:S(2)}, u32[]{:S(2)}) collective-permute-start(f32[2,72,128]{2,1,0:T(8,128)S(1)} %get-tuple-element.24), channel_id=1, source_target_pairs={{0,2},{1,3},{2,0},{3,1},{4,6},{5,7},{6,4},{7,5},{8,10},{9,11},{10,... | collective-permute-start | bytes 221192 | tf_op jit(solution)/shard_map/ppermute | solution.py:382
  5.4 4.2 %collective-permute-start.2 = (f32[2,72,128]{2,1,0:T(8,128)S(1)}, f32[2,72,128]{2,1,0:T(8,128)S(1)}, u32[]{:S(2)}, u32[]{:S(2)}) collective-permute-start(f32[2,72,128]{2,1,0:T(8,128)S(1)} %get-tuple-element.25), channel_id=1, source_target_pairs={{0,3},{1,2},{2,1},{3,0},{4,7},{5,6},{6,5},{7,4},{8,11},{9,10},{10,... | collective-permute-start | bytes 221192 | tf_op jit(solution)/shard_map/ppermute | solution.py:382
  5.4 10.0 %collective-permute-start.3 = (f32[3,8,256]{2,1,0:T(8,128)S(1)}, f32[3,8,256]{2,1,0:T(8,128)S(1)}, u32[]{:S(2)}, u32[]{:S(2)}) collective-permute-start(f32[3,8,256]{2,1,0:T(8,128)S(1)} %bitcast.2), channel_id=1, source_target_pairs={{0,4},{4,0},{2,6},{6,2},{5,9},{9,5},{7,11},{11,7},{8,12},{12,8},{1... | collective-permute-start | bytes 73736 | tf_op jit(solution)/shard_map/ppermute | solution.py:395
  9.6 19.3 %copy-start = (f32[8,64,256]{2,1,0:T(8,128)S(1)}, f32[8,64,256]{2,1,0:T(8,128)}, u32[]{:S(2)}) copy-start(f32[8,64,256]{2,1,0:T(8,128)} %refs_3_.5) | copy-start | bytes 1572868
  15.4 9.2 %copy-start.3 = (s32[8,8]{1,0:T(8,128)S(1)}, s32[8,8]{1,0:T(8,128)}, u32[]{:S(2)}) copy-start(s32[8,8]{1,0:T(8,128)} %far_ref.1) | copy-start | bytes 772
  15.4 13.4 %all-to-all-start = ((f32[32,2,384]{2,1,0:T(2,128)}), f32[32,2,384]{2,1,0:T(2,128)S(1)}, u32[]{:S(2)}, u32[]{:S(2)}) async-start(f32[32,2,384]{2,1,0:T(2,128)} %get-tuple-element.31), calls=%async_computation | async-start | bytes 196608 | tf_op jit(solution)/shard_map/all_to_all | solution.py:447
  21.3 3.3 %copy-start.2 = (s32[8,8]{1,0:T(8,128)S(1)}, s32[8,8]{1,0:T(8,128)}, u32[]{:S(2)}) copy-start(s32[8,8]{1,0:T(8,128)} %near_ref.1) | copy-start | bytes 772
  21.3 9.5 %collective-permute-start.5 = (f32[2,64,256]{2,1,0:T(8,128)S(1)}, f32[2,64,256]{2,1,0:T(8,128)S(1)}, u32[]{:S(2)}, u32[]{:S(2)}) collective-permute-start(f32[2,64,256]{2,1,0:T(8,128)S(1)} %get-tuple-element.37), channel_id=1, source_target_pairs={{0,1},{1,0},{2,3},{3,2},{4,5},{5,4},{6,7},{7,6},{8,9},{9,8},{10,11... | collective-permute-start | bytes 393224 | tf_op jit(solution)/shard_map/ppermute | solution.py:382
  21.6 9.2 %collective-permute-start.6 = (f32[2,64,256]{2,1,0:T(8,128)S(1)}, f32[2,64,256]{2,1,0:T(8,128)S(1)}, u32[]{:S(2)}, u32[]{:S(2)}) collective-permute-start(f32[2,64,256]{2,1,0:T(8,128)S(1)} %get-tuple-element.38), channel_id=1, source_target_pairs={{0,2},{1,3},{2,0},{3,1},{4,6},{5,7},{6,4},{7,5},{8,10},{9,11},{10,... | collective-permute-start | bytes 393224 | tf_op jit(solution)/shard_map/ppermute | solution.py:382
  23.3 7.6 %collective-permute-start.7 = (f32[2,64,256]{2,1,0:T(8,128)S(1)}, f32[2,64,256]{2,1,0:T(8,128)S(1)}, u32[]{:S(2)}, u32[]{:S(2)}) collective-permute-start(f32[2,64,256]{2,1,0:T(8,128)S(1)} %get-tuple-element.39), channel_id=1, source_target_pairs={{0,3},{1,2},{2,1},{3,0},{4,7},{5,6},{6,5},{7,4},{8,11},{9,10},{10,... | collective-permute-start | bytes 393224 | tf_op jit(solution)/shard_map/ppermute | solution.py:382
  23.3 1.3 %collective-permute-start.4 = (f32[3,8,256]{2,1,0:T(8,128)S(1)}, f32[3,8,256]{2,1,0:T(8,128)S(1)}, u32[]{:S(2)}, u32[]{:S(2)}) collective-permute-start(f32[3,8,256]{2,1,0:T(8,128)S(1)} %collective-permute-done.3.refs_1_), channel_id=1, source_target_pairs={{0,1},{1,0},{2,3},{3,2},{4,5},{5,4},{6,7},{7,6},{8,9},{9,8},{10,11... | collective-permute-start | bytes 73736 | tf_op jit(solution)/shard_map/ppermute | solution.py:401

commit v10 on v8

--- a/solution.py
+++ b/solution.py
@@ -134,7 +134,7 @@
                 facts[spot : spot + 1, middle:] = idle[1]
                 facts[share + spot : share + spot + 1, :] = pop_ref[pl.ds(frag, 1), :]
                 spots = [place_ref[axis, pl.ds(frag, 1), :] for axis in range(3)]
-                means = block_row(spots, 0) * (PC / basis)
+                means = block_row(spots, 4 * spot) * (PC / basis)
                 facts[2 * share + spot : 2 * share + spot + 1, :LANES] = means
 
 
@@ -203,6 +203,7 @@
         for square, (spot, span) in zip(squares, spans):
             x_ref[spot, span] = 1.5 * estimates[spot][span] - product(square, parts[spot])
 
+    sent, total = [], jnp.zeros((1, LANES), jnp.float32)
     for spot in range(share):
         density = jnp.where(row == column, 0.5, 0.0) - 0.5 * x_ref[spot]
         x_ref[spot] = density
@@ -212,9 +213,11 @@
         sums = [jnp.sum(block, axis=0, keepdims=True) for block in (corner, last)]
         charge = jnp.concatenate(swapped(half, jnp.concatenate(sums, axis=1)), axis=1)
         charge = charge - facts_ref[share + spot : share + spot + 1, :]
-        blocks = block_row([charge], 3) + facts_ref[2 * share + spot : 2 * share + spot + 1, :LANES]
-        whole = jnp.concatenate([charge, blocks], axis=1)
-        charge_ref[:, spot : spot + 1, :] = jnp.broadcast_to(whole[None], (charge_ref.shape[0],) + whole.shape)
+        blocks = block_row([charge], 4 * spot + 3) + facts_ref[2 * share + spot : 2 * share + spot + 1, :LANES]
+        sent.append(charge)
+        total = total + blocks
+    whole = jnp.concatenate([*sent, total], axis=1)
+    charge_ref[...] = jnp.broadcast_to(whole[None], (charge_ref.shape[0],) + whole.shape)
     for shift in range(tiles):
         first = partner(shift, tiles) % places * rows + (0 if shift < places else middle)
         span = pl.ds(pl.multiple_of(first, rows), rows)
@@ -251,7 +254,7 @@
 
     def row_of(frag):
         inside = lax.rem(frag, frag_dev)
-        return (inside // share * peers + frag // frag_dev) * share + lax.rem(inside, share)
+        return (lax.rem(inside, share) * tiles + inside // share) * peers + frag // frag_dev
 
     first_frag = (frag_at - reach) * frag_dev
 
@@ -288,10 +291,16 @@
 
 def gather_charges(charge_ref, near_hot, far_hot, near_charge, far_block):
     basis = near_charge.shape[2]
-    table = charge_ref[...].reshape(-1, basis + LANES)
+    rows = charge_ref[...].reshape(charge_ref.shape[0], charge_ref.shape[2])
+    share = rows.shape[1] // basis
+    tail, wide = rows[:, share * basis :], 4 * PC
+    charges = [rows[:, spot * basis : (spot + 1) * basis] for spot in range(share)]
+    blocks = [tail]
+    for spot in range(1, share):
+        blocks.append(jnp.concatenate([tail[:, spot * wide :], tail[:, : spot * wide]], axis=1))
     for hot, gathered, part in (
-        (near_hot, near_charge, table[:, :basis]),
-        (far_hot, far_block, table[:, basis:]),
+        (near_hot, near_charge, jnp.concatenate(charges, axis=0)),
+        (far_hot, far_block, jnp.concatenate(blocks, axis=0)),
     ):
         every = hot[...].reshape(-1, hot.shape[2])
         picked = jnp.dot(every, part, precision=lax.Precision.HIGHEST, preferred_element_type=jnp.float32)
@@ -433,7 +442,7 @@
     swaps = neighbours(places, -(-SPAN // frag_dev))
     *pieces, charges = call(
         functools.partial(density_kernel, tiles),
-        [chunk] * tiles + [floats(devices, share, basis + LANES)],
+        [chunk] * tiles + [floats(devices, 1, share * basis + LANES)],
         (facts, *sent),
         [VMEM] * (1 + tiles),
         [pltpu.VMEM((share, basis, basis), jnp.float32)] * 2,

time: 33.1 us -> 33.1 us (level)
  transfers between devices with their start and end apart: 9 -> 9, of which waited for: 3 -> 3; matrix products, arithmetic and copies ran while one was open for 0% -> 0% of each run, Pallas kernels for 31% -> 32%
where the time goes in v10:
time: 33.1 us; the launch traced here: 32.8 us
  starting transfers between devices  15.1 us (46%)
  Pallas kernels  13.7 us (41%)
  waiting for transfers between devices  3.22 us (10%)
  between operations  0.73 us (2%)
    pallas_call x5, Pallas kernels, call(): pl.pallas_call(kernel, out_shape=outs, in_specs=specs, out_specs=[out_spe...  13.7 us
    all_to_all x1, starting transfers between devices, per_device(): lax.all_to_all(charges, ('tile', 'frag'), split_axis=0, concat_axis=0, ti...  5.88 us
    ppermute x6, starting transfers between devices, exchanged(): moved.append(lax.ppermute(chunks[shift], 'tile', pairs))  5.15 us
    ppermute x1, starting transfers between devices, neighbours(): found.append(lax.ppermute(x, ('frag', 'tile'), pairs))  3.65 us
    all_to_all x1, waiting for transfers between devices, per_device(): lax.all_to_all(charges, ('tile', 'frag'), split_axis=0, concat_axis=0, ti...  1.87 us
    ppermute x1, waiting for transfers between devices, from_next_tile(): return lax.ppermute(x, 'tile', [(tile, tile ^ 1) for tile in range(tiles)])  0.85 us
  transfers between devices with their start and end apart: 9, of which 3 were waited for; matrix products, arithmetic and copies ran while one was open for 0% of the time, Pallas kernels for 32%

profile of v10, /device:TPU:0, one launch (start us, length us, event | category | flops | bytes accessed | tf_op | source)
XLA Modules:
  0.0 32.8 jit_solution(8496240628460950295)
XLA Ops:
  0.6 0.0 copy-start.1
  0.6 1.6 %shard_map.113 = (f32[2,2,64,256]{3,2,1,0:T(8,128)S(1)}, f32[2,2,64,256]{3,2,1,0:T(8,128)S(1)}, f32[2,72,128]{2,1,0:T(8,128)S(1)}, f32[2,72,128]{2,1,0:T(8,128)S(1)}, f32[6,256]{1,0:T(8,128)S(1)}) custom-call(s32[8]{0:T(128)} %refs_0_.1, f32[8,256]{1,0:T(8,128)} %refs_1_.1, f32[8,256]{1,0:T(8,128)} %refs_2_.1, f32[8,256]{1,0:T(8,128)} %refs_3_.3, ...), custom_call_target="tpu_custom_call" | custom-call | tf_op jit(solution)/shard_map/pallas_call | solution.py:369
  2.3 0.5 %collective-permute-start = (f32[2,2,64,256]{3,2,1,0:T(8,128)S(1)}, f32[2,2,64,256]{3,2,1,0:T(8,128)S(1)}, u32[]{:S(2)}, u32[]{:S(2)}) collective-permute-start(f32[2,2,64,256]{3,2,1,0:T(8,128)S(1)} %get-tuple-element.23), channel_id=1, source_target_pairs={{0,1},{1,0},{2,3},{3,2},{4,5},{5,4},{6,7},{7,6},{8,9},{9,8},{10,11... | collective-permute-start | bytes 786440 | tf_op jit(solution)/shard_map/ppermute | solution.py:389
  2.8 2.6 %collective-permute-start.1 = (f32[2,72,128]{2,1,0:T(8,128)S(1)}, f32[2,72,128]{2,1,0:T(8,128)S(1)}, u32[]{:S(2)}, u32[]{:S(2)}) collective-permute-start(f32[2,72,128]{2,1,0:T(8,128)S(1)} %get-tuple-element.24), channel_id=1, source_target_pairs={{0,2},{1,3},{2,0},{3,1},{4,6},{5,7},{6,4},{7,5},{8,10},{9,11},{10,... | collective-permute-start | bytes 221192 | tf_op jit(solution)/shard_map/ppermute | solution.py:389
  5.4 0.1 collective-permute-start.2
  5.4 0.0 copy-done.1
  5.4 3.7 %collective-permute-start.3 = (f32[3,8,256]{2,1,0:T(8,128)S(1)}, f32[3,8,256]{2,1,0:T(8,128)S(1)}, u32[]{:S(2)}, u32[]{:S(2)}) collective-permute-start(f32[3,8,256]{2,1,0:T(8,128)S(1)} %bitcast.2), channel_id=1, source_target_pairs={{0,4},{4,0},{2,6},{6,2},{5,9},{9,5},{7,11},{11,7},{8,12},{12,8},{1... | collective-permute-start | bytes 73736 | tf_op jit(solution)/shard_map/ppermute | solution.py:402
  9.1 0.0 collective-permute-done.1.refs_2_
  9.1 0.5 %collective-permute-done.2.refs_3_ = f32[2,72,128]{2,1,0:T(8,128)S(1)} collective-permute-done((f32[2,72,128]{2,1,0:T(8,128)S(1)}, f32[2,72,128]{2,1,0:T(8,128)S(1)}, u32[]{:S(2)}, u32[]{:S(2)}) %collective-permute-start.2) | collective-permute-done | bytes 73760 | tf_op jit(solution)/shard_map/ppermute | solution.py:389
  9.6 0.0 collective-permute-done.refs_1_
  9.6 0.0 copy-start
  9.6 5.8 %shard_map.114 = (f32[2,64,256]{2,1,0:T(8,128)S(1)}, f32[2,64,256]{2,1,0:T(8,128)S(1)}, f32[2,64,256]{2,1,0:T(8,128)S(1)}, f32[2,64,256]{2,1,0:T(8,128)S(1)}, f32[32,1,640]{2,1,0:T(1,128)}) custom-call(f32[6,256]{1,0:T(8,128)S(1)} %get-tuple-element.21.facts_ref, f32[2,2,64,256]{3,2,1,0:T(8,128)S(1)} %get-tuple-element.22.refs_0_, ...), custom_call_target="tpu_custom_call" | custom-call | tf_op jit(solution)/shard_map/pallas_call | solution.py:369
  15.4 0.0 collective-permute-done.3.refs_1_
  15.4 0.0 copy-start.3
  15.4 5.9 %all-to-all-start = ((f32[32,1,640]{2,1,0:T(1,128)}), f32[32,1,640]{2,1,0:T(1,128)S(1)}, u32[]{:S(2)}, u32[]{:S(2)}) async-start(f32[32,1,640]{2,1,0:T(1,128)} %get-tuple-element.31), calls=%async_computation | async-start | bytes 163840 | tf_op jit(solution)/shard_map/all_to_all | solution.py:454
  21.3 0.0 copy-start.2
  21.3 0.3 collective-permute-start.5
  21.6 1.7 %collective-permute-start.6 = (f32[2,64,256]{2,1,0:T(8,128)S(1)}, f32[2,64,256]{2,1,0:T(8,128)S(1)}, u32[]{:S(2)}, u32[]{:S(2)}) collective-permute-start(f32[2,64,256]{2,1,0:T(8,128)S(1)} %get-tuple-element.38), channel_id=1, source_target_pairs={{0,2},{1,3},{2,0},{3,1},{4,6},{5,7},{6,4},{7,5},{8,10},{9,11},{10,... | collective-permute-start | bytes 393224 | tf_op jit(solution)/shard_map/ppermute | solution.py:389
  23.3 0.0 collective-permute-start.7
  23.3 0.5 %collective-permute-start.4 = (f32[3,8,256]{2,1,0:T(8,128)S(1)}, f32[3,8,256]{2,1,0:T(8,128)S(1)}, u32[]{:S(2)}, u32[]{:S(2)}) collective-permute-start(f32[3,8,256]{2,1,0:T(8,128)S(1)} %collective-permute-done.3.refs_1_), channel_id=1, source_target_pairs={{0,1},{1,0},{2,3},{3,2},{4,5},{5,4},{6,7},{7,6},{8,9},{9,8},{10,11... | collective-permute-start | bytes 73736 | tf_op jit(solution)/shard_map/ppermute | solution.py:408
  23.8 0.8 %collective-permute-done.4.refs_2_ = f32[3,8,256]{2,1,0:T(8,128)S(1)} collective-permute-done((f32[3,8,256]{2,1,0:T(8,128)S(1)}, f32[3,8,256]{2,1,0:T(8,128)S(1)}, u32[]{:S(2)}, u32[]{:S(2)}) %collective-permute-start.4) | collective-permute-done | bytes 24608 | tf_op jit(solution)/shard_map/ppermute | solution.py:408
  24.6 0.0 copy-done.3
  24.6 0.0 copy-done.2
  24.6 2.2 %shard_map.115 = (bf16[8,32,256]{2,1,0:T(8,128)(2,1)S(1)}, bf16[8,8,32,256]{3,2,1,0:T(8,128)(2,1)S(1)}, f32[8,8,64]{2,1,0:T(8,128)S(1)}, f32[8,8,64]{2,1,0:T(8,128)S(1)}) custom-call(s32[8,8]{1,0:T(8,128)S(1)} %copy-done.2, s32[8,8]{1,0:T(8,128)S(1)} %copy-done.3, f32[3,8,256]{2,1,0:T(8,128)S(1)} %bitcast.3, f32[3,8,256]{2,1,0:T(8,128)S(1)} %bitcast.4, ...), custom_call_target="tpu_custom_call" | custom-call | tf_op jit(solution)/shard_map/pallas_call | solution.py:369
  26.9 1.9 %all-to-all-done.charge_ref = f32[32,1,640]{2,1,0:T(1,128)S(1)} async-done(((f32[32,1,640]{2,1,0:T(1,128)}), f32[32,1,640]{2,1,0:T(1,128)S(1)}, u32[]{:S(2)}, u32[]{:S(2)}) %all-to-all-start) | async-done | bytes 81952 | tf_op jit(solution)/shard_map/all_to_all | solution.py:454
  28.8 0.0 copy-done
  28.8 2.3 %shard_map.116 = (f32[6,64,256]{2,1,0:T(8,128)S(1)}, f32[8,8,256]{2,1,0:T(8,128)S(1)}, f32[8,8,128]{2,1,0:T(8,128)S(1)}) custom-call(f32[32,1,640]{2,1,0:T(1,128)S(1)} %all-to-all-done.charge_ref, f32[8,8,64]{2,1,0:T(8,128)S(1)} %get-tuple-element.32.near_hot, f32[8,8,64]{2,1,0:T(8,128)S(1)} %get-tuple-element.33.far_hot, f32[3,8,256]{2,1,0:T(8,128)S(1)} %bitcast.5, ...), custom_call_target="tpu_custom_call" | custom-call | tf_op jit(solution)/shard_map/pallas_call | solution.py:369
  31.1 0.0 collective-permute-done.5.refs_8_
  31.1 0.0 collective-permute-done.6.refs_9_
  31.1 0.0 collective-permute-done.7.refs_10_
  31.1 1.7 %shard_map.117 = (f32[8,64,256]{2,1,0:T(8,128)}, f32[8,64,256]{2,1,0:T(8,128)}) custom-call(f32[3,8,256]{2,1,0:T(8,128)S(1)} %bitcast.6, bf16[8,32,256]{2,1,0:T(8,128)(2,1)S(1)} %get-tuple-element.29.refs_1_, bf16[8,8,32,256]{3,2,1,0:T(8,128)(2,1)S(1)} %get-tuple-element.30.refs_2_, f32[8,64,256]{2,1,0:T(8,128)S(1)} %copy-done, ...), custom_call_target="tpu_custom_call" | custom-call | tf_op jit(solution)/shard_map/pallas_call | solution.py:369
Async XLA Ops:
  0.6 4.8 %copy-start.1 = (f32[8,3,256]{2,0,1:T(8,128)S(1)}, f32[8,3,256]{2,0,1:T(8,128)}, u32[]{:S(2)}) copy-start(f32[8,3,256]{2,0,1:T(8,128)} %param.16) | copy-start | bytes 73732
  2.3 7.3 %collective-permute-start = (f32[2,2,64,256]{3,2,1,0:T(8,128)S(1)}, f32[2,2,64,256]{3,2,1,0:T(8,128)S(1)}, u32[]{:S(2)}, u32[]{:S(2)}) collective-permute-start(f32[2,2,64,256]{3,2,1,0:T(8,128)S(1)} %get-tuple-element.23), channel_id=1, source_target_pairs={{0,1},{1,0},{2,3},{3,2},{4,5},{5,4},{6,7},{7,6},{8,9},{9,8},{10,11... | collective-permute-start | bytes 786440 | tf_op jit(solution)/shard_map/ppermute | solution.py:389
  2.8 6.3 %collective-permute-start.1 = (f32[2,72,128]{2,1,0:T(8,128)S(1)}, f32[2,72,128]{2,1,0:T(8,128)S(1)}, u32[]{:S(2)}, u32[]{:S(2)}) collective-permute-start(f32[2,72,128]{2,1,0:T(8,128)S(1)} %get-tuple-element.24), channel_id=1, source_target_pairs={{0,2},{1,3},{2,0},{3,1},{4,6},{5,7},{6,4},{7,5},{8,10},{9,11},{10,... | collective-permute-start | bytes 221192 | tf_op jit(solution)/shard_map/ppermute | solution.py:389
  5.4 4.2 %collective-permute-start.2 = (f32[2,72,128]{2,1,0:T(8,128)S(1)}, f32[2,72,128]{2,1,0:T(8,128)S(1)}, u32[]{:S(2)}, u32[]{:S(2)}) collective-permute-start(f32[2,72,128]{2,1,0:T(8,128)S(1)} %get-tuple-element.25), channel_id=1, source_target_pairs={{0,3},{1,2},{2,1},{3,0},{4,7},{5,6},{6,5},{7,4},{8,11},{9,10},{10,... | collective-permute-start | bytes 221192 | tf_op jit(solution)/shard_map/ppermute | solution.py:389
  5.4 10.0 %collective-permute-start.3 = (f32[3,8,256]{2,1,0:T(8,128)S(1)}, f32[3,8,256]{2,1,0:T(8,128)S(1)}, u32[]{:S(2)}, u32[]{:S(2)}) collective-permute-start(f32[3,8,256]{2,1,0:T(8,128)S(1)} %bitcast.2), channel_id=1, source_target_pairs={{0,4},{4,0},{2,6},{6,2},{5,9},{9,5},{7,11},{11,7},{8,12},{12,8},{1... | collective-permute-start | bytes 73736 | tf_op jit(solution)/shard_map/ppermute | solution.py:402
  9.6 19.2 %copy-start = (f32[8,64,256]{2,1,0:T(8,128)S(1)}, f32[8,64,256]{2,1,0:T(8,128)}, u32[]{:S(2)}) copy-start(f32[8,64,256]{2,1,0:T(8,128)} %refs_3_.5) | copy-start | bytes 1572868
  15.4 9.2 %copy-start.3 = (s32[8,8]{1,0:T(8,128)S(1)}, s32[8,8]{1,0:T(8,128)}, u32[]{:S(2)}) copy-start(s32[8,8]{1,0:T(8,128)} %far_ref.1) | copy-start | bytes 772
  15.4 13.3 %all-to-all-start = ((f32[32,1,640]{2,1,0:T(1,128)}), f32[32,1,640]{2,1,0:T(1,128)S(1)}, u32[]{:S(2)}, u32[]{:S(2)}) async-start(f32[32,1,640]{2,1,0:T(1,128)} %get-tuple-element.31), calls=%async_computation | async-start | bytes 163840 | tf_op jit(solution)/shard_map/all_to_all | solution.py:454
  21.3 3.3 %copy-start.2 = (s32[8,8]{1,0:T(8,128)S(1)}, s32[8,8]{1,0:T(8,128)}, u32[]{:S(2)}) copy-start(s32[8,8]{1,0:T(8,128)} %near_ref.1) | copy-start | bytes 772
  21.3 9.8 %collective-permute-start.5 = (f32[2,64,256]{2,1,0:T(8,128)S(1)}, f32[2,64,256]{2,1,0:T(8,128)S(1)}, u32[]{:S(2)}, u32[]{:S(2)}) collective-permute-start(f32[2,64,256]{2,1,0:T(8,128)S(1)} %get-tuple-element.37), channel_id=1, source_target_pairs={{0,1},{1,0},{2,3},{3,2},{4,5},{5,4},{6,7},{7,6},{8,9},{9,8},{10,11... | collective-permute-start | bytes 393224 | tf_op jit(solution)/shard_map/ppermute | solution.py:389
  21.6 9.5 %collective-permute-start.6 = (f32[2,64,256]{2,1,0:T(8,128)S(1)}, f32[2,64,256]{2,1,0:T(8,128)S(1)}, u32[]{:S(2)}, u32[]{:S(2)}) collective-permute-start(f32[2,64,256]{2,1,0:T(8,128)S(1)} %get-tuple-element.38), channel_id=1, source_target_pairs={{0,2},{1,3},{2,0},{3,1},{4,6},{5,7},{6,4},{7,5},{8,10},{9,11},{10,... | collective-permute-start | bytes 393224 | tf_op jit(solution)/shard_map/ppermute | solution.py:389
  23.3 7.8 %collective-permute-start.7 = (f32[2,64,256]{2,1,0:T(8,128)S(1)}, f32[2,64,256]{2,1,0:T(8,128)S(1)}, u32[]{:S(2)}, u32[]{:S(2)}) collective-permute-start(f32[2,64,256]{2,1,0:T(8,128)S(1)} %get-tuple-element.39), channel_id=1, source_target_pairs={{0,3},{1,2},{2,1},{3,0},{4,7},{5,6},{6,5},{7,4},{8,11},{9,10},{10,... | collective-permute-start | bytes 393224 | tf_op jit(solution)/shard_map/ppermute | solution.py:389
  23.3 1.3 %collective-permute-start.4 = (f32[3,8,256]{2,1,0:T(8,128)S(1)}, f32[3,8,256]{2,1,0:T(8,128)S(1)}, u32[]{:S(2)}, u32[]{:S(2)}) collective-permute-start(f32[3,8,256]{2,1,0:T(8,128)S(1)} %collective-permute-done.3.refs_1_), channel_id=1, source_target_pairs={{0,1},{1,0},{2,3},{3,2},{4,5},{5,4},{6,7},{7,6},{8,9},{9,8},{10,11... | collective-permute-start | bytes 73736 | tf_op jit(solution)/shard_map/ppermute | solution.py:408

commit v11 on v10

--- a/solution.py
+++ b/solution.py
@@ -302,8 +302,10 @@
         (near_hot, near_charge, jnp.concatenate(charges, axis=0)),
         (far_hot, far_block, jnp.concatenate(blocks, axis=0)),
     ):
-        every = hot[...].reshape(-1, hot.shape[2])
-        picked = jnp.dot(every, part, precision=lax.Precision.HIGHEST, preferred_element_type=jnp.float32)
+        every = hot[...].reshape(-1, hot.shape[2]).astype(jnp.bfloat16)
+        pieces = [piece.astype(jnp.bfloat16) for piece in pieces_of(part)]
+        sums = [jnp.dot(every, piece, preferred_element_type=jnp.float32) for piece in pieces]
+        picked = sums[0] + sums[1] + sums[2]
         gathered[...] = picked.reshape(gathered.shape)
 
 

time: 33.1 us -> 33 us (level)
  no operation moved by 1% of the time
where the time goes in v11:
time: 33 us; the launch traced here: 32.8 us
  starting transfers between devices  15.1 us (46%)
  Pallas kernels  13.7 us (42%)
  waiting for transfers between devices  3.22 us (10%)
  between operations  0.73 us (2%)
    pallas_call x5, Pallas kernels, call(): pl.pallas_call(kernel, out_shape=outs, in_specs=specs, out_specs=[out_spe...  13.7 us
    all_to_all x1, starting transfers between devices, per_device(): lax.all_to_all(charges, ('tile', 'frag'), split_axis=0, concat_axis=0, ti...  5.88 us
    ppermute x6, starting transfers between devices, exchanged(): moved.append(lax.ppermute(chunks[shift], 'tile', pairs))  5.15 us
    ppermute x1, starting transfers between devices, neighbours(): found.append(lax.ppermute(x, ('frag', 'tile'), pairs))  3.65 us
    all_to_all x1, waiting for transfers between devices, per_device(): lax.all_to_all(charges, ('tile', 'frag'), split_axis=0, concat_axis=0, ti...  1.87 us
    ppermute x1, waiting for transfers between devices, from_next_tile(): return lax.ppermute(x, 'tile', [(tile, tile ^ 1) for tile in range(tiles)])  0.85 us
  transfers between devices with their start and end apart: 9, of which 3 were waited for; matrix products, arithmetic and copies ran while one was open for 0% of the time, Pallas kernels for 32%

profile of v11, /device:TPU:0, one launch (start us, length us, event | category | flops | bytes accessed | tf_op | source)
XLA Modules:
  0.0 32.8 jit_solution(2788720750177729129)
XLA Ops:
  0.6 0.0 copy-start.1
  0.6 1.6 %shard_map.113 = (f32[2,2,64,256]{3,2,1,0:T(8,128)S(1)}, f32[2,2,64,256]{3,2,1,0:T(8,128)S(1)}, f32[2,72,128]{2,1,0:T(8,128)S(1)}, f32[2,72,128]{2,1,0:T(8,128)S(1)}, f32[6,256]{1,0:T(8,128)S(1)}) custom-call(s32[8]{0:T(128)} %refs_0_.1, f32[8,256]{1,0:T(8,128)} %refs_1_.1, f32[8,256]{1,0:T(8,128)} %refs_2_.1, f32[8,256]{1,0:T(8,128)} %refs_3_.3, ...), custom_call_target="tpu_custom_call" | custom-call | tf_op jit(solution)/shard_map/pallas_call | solution.py:371
  2.3 0.5 %collective-permute-start = (f32[2,2,64,256]{3,2,1,0:T(8,128)S(1)}, f32[2,2,64,256]{3,2,1,0:T(8,128)S(1)}, u32[]{:S(2)}, u32[]{:S(2)}) collective-permute-start(f32[2,2,64,256]{3,2,1,0:T(8,128)S(1)} %get-tuple-element.23), channel_id=1, source_target_pairs={{0,1},{1,0},{2,3},{3,2},{4,5},{5,4},{6,7},{7,6},{8,9},{9,8},{10,11... | collective-permute-start | bytes 786440 | tf_op jit(solution)/shard_map/ppermute | solution.py:391
  2.8 2.6 %collective-permute-start.1 = (f32[2,72,128]{2,1,0:T(8,128)S(1)}, f32[2,72,128]{2,1,0:T(8,128)S(1)}, u32[]{:S(2)}, u32[]{:S(2)}) collective-permute-start(f32[2,72,128]{2,1,0:T(8,128)S(1)} %get-tuple-element.24), channel_id=1, source_target_pairs={{0,2},{1,3},{2,0},{3,1},{4,6},{5,7},{6,4},{7,5},{8,10},{9,11},{10,... | collective-permute-start | bytes 221192 | tf_op jit(solution)/shard_map/ppermute | solution.py:391
  5.4 0.1 collective-permute-start.2
  5.4 0.0 copy-done.1
  5.4 3.7 %collective-permute-start.3 = (f32[3,8,256]{2,1,0:T(8,128)S(1)}, f32[3,8,256]{2,1,0:T(8,128)S(1)}, u32[]{:S(2)}, u32[]{:S(2)}) collective-permute-start(f32[3,8,256]{2,1,0:T(8,128)S(1)} %bitcast.2), channel_id=1, source_target_pairs={{0,4},{4,0},{2,6},{6,2},{5,9},{9,5},{7,11},{11,7},{8,12},{12,8},{1... | collective-permute-start | bytes 73736 | tf_op jit(solution)/shard_map/ppermute | solution.py:404
  9.1 0.0 collective-permute-done.1.refs_2_
  9.1 0.5 %collective-permute-done.2.refs_3_ = f32[2,72,128]{2,1,0:T(8,128)S(1)} collective-permute-done((f32[2,72,128]{2,1,0:T(8,128)S(1)}, f32[2,72,128]{2,1,0:T(8,128)S(1)}, u32[]{:S(2)}, u32[]{:S(2)}) %collective-permute-start.2) | collective-permute-done | bytes 73760 | tf_op jit(solution)/shard_map/ppermute | solution.py:391
  9.6 0.0 collective-permute-done.refs_1_
  9.6 0.0 copy-start
  9.6 5.8 %shard_map.114 = (f32[2,64,256]{2,1,0:T(8,128)S(1)}, f32[2,64,256]{2,1,0:T(8,128)S(1)}, f32[2,64,256]{2,1,0:T(8,128)S(1)}, f32[2,64,256]{2,1,0:T(8,128)S(1)}, f32[32,1,640]{2,1,0:T(1,128)}) custom-call(f32[6,256]{1,0:T(8,128)S(1)} %get-tuple-element.21.facts_ref, f32[2,2,64,256]{3,2,1,0:T(8,128)S(1)} %get-tuple-element.22.refs_0_, ...), custom_call_target="tpu_custom_call" | custom-call | tf_op jit(solution)/shard_map/pallas_call | solution.py:371
  15.4 0.0 collective-permute-done.3.refs_1_
  15.4 0.0 copy-start.3
  15.4 5.9 %all-to-all-start = ((f32[32,1,640]{2,1,0:T(1,128)}), f32[32,1,640]{2,1,0:T(1,128)S(1)}, u32[]{:S(2)}, u32[]{:S(2)}) async-start(f32[32,1,640]{2,1,0:T(1,128)} %get-tuple-element.31), calls=%async_computation | async-start | bytes 163840 | tf_op jit(solution)/shard_map/all_to_all | solution.py:456
  21.3 0.0 copy-start.2
  21.3 0.3 collective-permute-start.5
  21.6 1.7 %collective-permute-start.6 = (f32[2,64,256]{2,1,0:T(8,128)S(1)}, f32[2,64,256]{2,1,0:T(8,128)S(1)}, u32[]{:S(2)}, u32[]{:S(2)}) collective-permute-start(f32[2,64,256]{2,1,0:T(8,128)S(1)} %get-tuple-element.38), channel_id=1, source_target_pairs={{0,2},{1,3},{2,0},{3,1},{4,6},{5,7},{6,4},{7,5},{8,10},{9,11},{10,... | collective-permute-start | bytes 393224 | tf_op jit(solution)/shard_map/ppermute | solution.py:391
  23.3 0.0 collective-permute-start.7
  23.3 0.5 %collective-permute-start.4 = (f32[3,8,256]{2,1,0:T(8,128)S(1)}, f32[3,8,256]{2,1,0:T(8,128)S(1)}, u32[]{:S(2)}, u32[]{:S(2)}) collective-permute-start(f32[3,8,256]{2,1,0:T(8,128)S(1)} %collective-permute-done.3.refs_1_), channel_id=1, source_target_pairs={{0,1},{1,0},{2,3},{3,2},{4,5},{5,4},{6,7},{7,6},{8,9},{9,8},{10,11... | collective-permute-start | bytes 73736 | tf_op jit(solution)/shard_map/ppermute | solution.py:410
  23.8 0.8 %collective-permute-done.4.refs_2_ = f32[3,8,256]{2,1,0:T(8,128)S(1)} collective-permute-done((f32[3,8,256]{2,1,0:T(8,128)S(1)}, f32[3,8,256]{2,1,0:T(8,128)S(1)}, u32[]{:S(2)}, u32[]{:S(2)}) %collective-permute-start.4) | collective-permute-done | bytes 24608 | tf_op jit(solution)/shard_map/ppermute | solution.py:410
  24.6 0.0 copy-done.3
  24.6 0.0 copy-done.2
  24.6 2.2 %shard_map.115 = (bf16[8,32,256]{2,1,0:T(8,128)(2,1)S(1)}, bf16[8,8,32,256]{3,2,1,0:T(8,128)(2,1)S(1)}, f32[8,8,64]{2,1,0:T(8,128)S(1)}, f32[8,8,64]{2,1,0:T(8,128)S(1)}) custom-call(s32[8,8]{1,0:T(8,128)S(1)} %copy-done.2, s32[8,8]{1,0:T(8,128)S(1)} %copy-done.3, f32[3,8,256]{2,1,0:T(8,128)S(1)} %bitcast.3, f32[3,8,256]{2,1,0:T(8,128)S(1)} %bitcast.4, ...), custom_call_target="tpu_custom_call" | custom-call | tf_op jit(solution)/shard_map/pallas_call | solution.py:371
  26.9 1.9 %all-to-all-done.charge_ref = f32[32,1,640]{2,1,0:T(1,128)S(1)} async-done(((f32[32,1,640]{2,1,0:T(1,128)}), f32[32,1,640]{2,1,0:T(1,128)S(1)}, u32[]{:S(2)}, u32[]{:S(2)}) %all-to-all-start) | async-done | bytes 81952 | tf_op jit(solution)/shard_map/all_to_all | solution.py:456
  28.8 0.0 copy-done
  28.8 2.3 %shard_map.116 = (f32[6,64,256]{2,1,0:T(8,128)S(1)}, f32[8,8,256]{2,1,0:T(8,128)S(1)}, f32[8,8,128]{2,1,0:T(8,128)S(1)}) custom-call(f32[32,1,640]{2,1,0:T(1,128)S(1)} %all-to-all-done.charge_ref, f32[8,8,64]{2,1,0:T(8,128)S(1)} %get-tuple-element.32.near_hot, f32[8,8,64]{2,1,0:T(8,128)S(1)} %get-tuple-element.33.far_hot, f32[3,8,256]{2,1,0:T(8,128)S(1)} %bitcast.5, ...), custom_call_target="tpu_custom_call" | custom-call | tf_op jit(solution)/shard_map/pallas_call | solution.py:371
  31.1 0.0 collective-permute-done.5.refs_8_
  31.1 0.0 collective-permute-done.6.refs_9_
  31.1 0.0 collective-permute-done.7.refs_10_
  31.1 1.7 %shard_map.117 = (f32[8,64,256]{2,1,0:T(8,128)}, f32[8,64,256]{2,1,0:T(8,128)}) custom-call(f32[3,8,256]{2,1,0:T(8,128)S(1)} %bitcast.6, bf16[8,32,256]{2,1,0:T(8,128)(2,1)S(1)} %get-tuple-element.29.refs_1_, bf16[8,8,32,256]{3,2,1,0:T(8,128)(2,1)S(1)} %get-tuple-element.30.refs_2_, f32[8,64,256]{2,1,0:T(8,128)S(1)} %copy-done, ...), custom_call_target="tpu_custom_call" | custom-call | tf_op jit(solution)/shard_map/pallas_call | solution.py:371
Async XLA Ops:
  0.6 4.8 %copy-start.1 = (f32[8,3,256]{2,0,1:T(8,128)S(1)}, f32[8,3,256]{2,0,1:T(8,128)}, u32[]{:S(2)}) copy-start(f32[8,3,256]{2,0,1:T(8,128)} %param.16) | copy-start | bytes 73732
  2.3 7.3 %collective-permute-start = (f32[2,2,64,256]{3,2,1,0:T(8,128)S(1)}, f32[2,2,64,256]{3,2,1,0:T(8,128)S(1)}, u32[]{:S(2)}, u32[]{:S(2)}) collective-permute-start(f32[2,2,64,256]{3,2,1,0:T(8,128)S(1)} %get-tuple-element.23), channel_id=1, source_target_pairs={{0,1},{1,0},{2,3},{3,2},{4,5},{5,4},{6,7},{7,6},{8,9},{9,8},{10,11... | collective-permute-start | bytes 786440 | tf_op jit(solution)/shard_map/ppermute | solution.py:391
  2.8 6.3 %collective-permute-start.1 = (f32[2,72,128]{2,1,0:T(8,128)S(1)}, f32[2,72,128]{2,1,0:T(8,128)S(1)}, u32[]{:S(2)}, u32[]{:S(2)}) collective-permute-start(f32[2,72,128]{2,1,0:T(8,128)S(1)} %get-tuple-element.24), channel_id=1, source_target_pairs={{0,2},{1,3},{2,0},{3,1},{4,6},{5,7},{6,4},{7,5},{8,10},{9,11},{10,... | collective-permute-start | bytes 221192 | tf_op jit(solution)/shard_map/ppermute | solution.py:391
  5.4 4.2 %collective-permute-start.2 = (f32[2,72,128]{2,1,0:T(8,128)S(1)}, f32[2,72,128]{2,1,0:T(8,128)S(1)}, u32[]{:S(2)}, u32[]{:S(2)}) collective-permute-start(f32[2,72,128]{2,1,0:T(8,128)S(1)} %get-tuple-element.25), channel_id=1, source_target_pairs={{0,3},{1,2},{2,1},{3,0},{4,7},{5,6},{6,5},{7,4},{8,11},{9,10},{10,... | collective-permute-start | bytes 221192 | tf_op jit(solution)/shard_map/ppermute | solution.py:391
  5.4 10.0 %collective-permute-start.3 = (f32[3,8,256]{2,1,0:T(8,128)S(1)}, f32[3,8,256]{2,1,0:T(8,128)S(1)}, u32[]{:S(2)}, u32[]{:S(2)}) collective-permute-start(f32[3,8,256]{2,1,0:T(8,128)S(1)} %bitcast.2), channel_id=1, source_target_pairs={{0,4},{4,0},{2,6},{6,2},{5,9},{9,5},{7,11},{11,7},{8,12},{12,8},{1... | collective-permute-start | bytes 73736 | tf_op jit(solution)/shard_map/ppermute | solution.py:404
  9.6 19.2 %copy-start = (f32[8,64,256]{2,1,0:T(8,128)S(1)}, f32[8,64,256]{2,1,0:T(8,128)}, u32[]{:S(2)}) copy-start(f32[8,64,256]{2,1,0:T(8,128)} %refs_3_.5) | copy-start | bytes 1572868
  15.4 9.2 %copy-start.3 = (s32[8,8]{1,0:T(8,128)S(1)}, s32[8,8]{1,0:T(8,128)}, u32[]{:S(2)}) copy-start(s32[8,8]{1,0:T(8,128)} %far_ref.1) | copy-start | bytes 772
  15.4 13.3 %all-to-all-start = ((f32[32,1,640]{2,1,0:T(1,128)}), f32[32,1,640]{2,1,0:T(1,128)S(1)}, u32[]{:S(2)}, u32[]{:S(2)}) async-start(f32[32,1,640]{2,1,0:T(1,128)} %get-tuple-element.31), calls=%async_computation | async-start | bytes 163840 | tf_op jit(solution)/shard_map/all_to_all | solution.py:456
  21.3 3.3 %copy-start.2 = (s32[8,8]{1,0:T(8,128)S(1)}, s32[8,8]{1,0:T(8,128)}, u32[]{:S(2)}) copy-start(s32[8,8]{1,0:T(8,128)} %near_ref.1) | copy-start | bytes 772
  21.3 9.8 %collective-permute-start.5 = (f32[2,64,256]{2,1,0:T(8,128)S(1)}, f32[2,64,256]{2,1,0:T(8,128)S(1)}, u32[]{:S(2)}, u32[]{:S(2)}) collective-permute-start(f32[2,64,256]{2,1,0:T(8,128)S(1)} %get-tuple-element.37), channel_id=1, source_target_pairs={{0,1},{1,0},{2,3},{3,2},{4,5},{5,4},{6,7},{7,6},{8,9},{9,8},{10,11... | collective-permute-start | bytes 393224 | tf_op jit(solution)/shard_map/ppermute | solution.py:391
  21.6 9.5 %collective-permute-start.6 = (f32[2,64,256]{2,1,0:T(8,128)S(1)}, f32[2,64,256]{2,1,0:T(8,128)S(1)}, u32[]{:S(2)}, u32[]{:S(2)}) collective-permute-start(f32[2,64,256]{2,1,0:T(8,128)S(1)} %get-tuple-element.38), channel_id=1, source_target_pairs={{0,2},{1,3},{2,0},{3,1},{4,6},{5,7},{6,4},{7,5},{8,10},{9,11},{10,... | collective-permute-start | bytes 393224 | tf_op jit(solution)/shard_map/ppermute | solution.py:391
  23.3 7.8 %collective-permute-start.7 = (f32[2,64,256]{2,1,0:T(8,128)S(1)}, f32[2,64,256]{2,1,0:T(8,128)S(1)}, u32[]{:S(2)}, u32[]{:S(2)}) collective-permute-start(f32[2,64,256]{2,1,0:T(8,128)S(1)} %get-tuple-element.39), channel_id=1, source_target_pairs={{0,3},{1,2},{2,1},{3,0},{4,7},{5,6},{6,5},{7,4},{8,11},{9,10},{10,... | collective-permute-start | bytes 393224 | tf_op jit(solution)/shard_map/ppermute | solution.py:391
  23.3 1.3 %collective-permute-start.4 = (f32[3,8,256]{2,1,0:T(8,128)S(1)}, f32[3,8,256]{2,1,0:T(8,128)S(1)}, u32[]{:S(2)}, u32[]{:S(2)}) collective-permute-start(f32[3,8,256]{2,1,0:T(8,128)S(1)} %collective-permute-done.3.refs_1_), channel_id=1, source_target_pairs={{0,1},{1,0},{2,3},{3,2},{4,5},{5,4},{6,7},{7,6},{8,9},{9,8},{10,11... | collective-permute-start | bytes 73736 | tf_op jit(solution)/shard_map/ppermute | solution.py:410
